TPU v7x, 32 devices: a whole 2x2x4 slice. The times are simulated.
32 devices in a mesh: groups: 2 (over y), seq: 8 (over z, x), chan: 2 (over core).
Axes of the slice: x: 2, y: 2, z: 4, core: 2. Of those that a mesh axis runs over, the one named last changes fastest.
Arguments:
- inputs: bfloat16 [4096, 8192], P(('groups', 'seq'), 'chan'), parts along dimension 0, may hold values from -6 to 6
- bounds: int32 [16], P(('groups', 'seq')), parts along dimension 0, may hold values from 0 to 256, as said below
- feat_first: float32 [3, 3, 8192], P(None, None, 'chan'), may hold values from -4 to 4
- li_decay: float32 [16, 16], P('chan'), may hold values from 0 to 1
- li_residue: float32 [16, 16], P('chan'), may hold values from -4 to 4
- feat_second: float32 [3, 3, 8192], P(None, None, 'chan'), may hold values from -4 to 4
- mr_filter: bfloat16 [16, 128], P('chan'), may hold values from -0.5 to 0.5
Outputs:
- mixed: bfloat16 [4096, 8192], P(('groups', 'seq'), 'chan'), parts along dimension 0
There are 2 independent parts, one for each index of `groups`. A program takes and returns all parts, laid end to end along the dimension named above; an argument that names none is the same for every part. Nothing has to cross between parts.
Inputs may be any that keep to these rules, and one draw needn't show every extreme that they name: bounds[s] is the position within block s where a document begins; 256 means no document begins in that block.
All inputs are finite; a program needn't handle non-finite values.
Results may differ from a plain program's by a relative error of at most 0.0081.
Values may be sent and summed in bfloat16 or wider, within the bound.
No kernel may reach another device: no remote copies, remote signals or barrier semaphores. Data moves between devices by JAX's collectives and lax.ppermute only.
A program may use at most 192 MiB of HBM per device.

v0:
```python
import math

import jax
import jax.numpy as jnp
from jax import lax
from jax.sharding import PartitionSpec as P

PRECISE = lax.Precision.HIGHEST


def from_behind(array, axis, by):
    size = lax.axis_size(axis)
    pairs = [(i, i + by) for i in range(size) if 0 <= i + by < size]
    return lax.ppermute(array, axis, pairs)


def carried_in(part, axis, combine, identity):
    place = lax.axis_index(axis)
    gathered = jax.tree.map(lambda a: lax.all_gather(a, axis), part)
    state = jax.tree.map(lambda a, e: jnp.zeros_like(a) + jnp.asarray(e, a.dtype), part, identity)

    def one(step, state):
        return combine(
            state, jax.tree.map(lambda a: lax.dynamic_index_in_dim(a, step, 0, False), gathered)
        )

    return lax.fori_loop(0, place, one, state)


def doc_counts(positions, prior_start, own_start, length_dev):
    first_term = ((prior_start < length_dev) & (positions >= prior_start - length_dev)).astype(
        jnp.int32
    )
    second_term = ((own_start < length_dev) & (positions >= own_start)).astype(jnp.int32)
    return first_term + second_term


def features(extended, ext_counts, weights, rows_out):
    target = ext_counts[2 : 2 + rows_out]
    outputs = []
    for branch in range(3):
        summed = jnp.zeros((rows_out, extended.shape[1]), jnp.float32)
        for offset in range(3):
            shifted = extended[2 - offset : 2 - offset + rows_out].astype(jnp.float32)
            agrees = (ext_counts[2 - offset : 2 - offset + rows_out] == target).astype(jnp.float32)
            summed = summed + weights[branch, offset] * shifted * agrees[:, None]
        outputs.append(summed)
    return (outputs[0], outputs[1], outputs[2])


def compose(earlier, latter):
    return (earlier[0] * latter[0], earlier[1] * latter[0][:, :, None] + latter[1])


def per_device(inputs, bounds, feat_first, li_decay, li_residue, feat_second, mr_filter):
    length_dev, channels = inputs.shape
    groups, mode_count = li_decay.shape
    group_size = channels // groups
    filter_len = mr_filter.shape[1]
    tail_len = filter_len - 1
    own_start = bounds[0]
    edge_rows, edge_bound = (
        from_behind(
            inputs[length_dev - 2 :].astype(jnp.float32).astype(jnp.bfloat16), "seq", 1
        ).astype(jnp.float32),
        from_behind(bounds.astype(jnp.float32).astype(jnp.bfloat16), "seq", 1).astype(jnp.float32),
    )
    prior_start = edge_bound[0].astype(jnp.int32)
    positions = jnp.arange(-2, length_dev, dtype=jnp.int32)
    ext_counts = doc_counts(positions, prior_start, own_start, length_dev)
    own_counts = ext_counts[2:]
    extended = jnp.concatenate([edge_rows.astype(jnp.bfloat16), inputs], 0)
    query_gate, key_part, value_part = features(extended, ext_counts, feat_first, length_dev)
    mixed_in = (key_part * value_part).astype(jnp.bfloat16)
    mixed_wide = (
        lax.optimization_barrier(mixed_in)
        .astype(jnp.float32)
        .reshape(length_dev, groups, group_size)
    )
    mode_weight = li_residue * jnp.sqrt(-jnp.expm1(-2.0 * li_decay)) / math.sqrt(mode_count)
    lag_pos = jnp.arange(length_dev).astype(jnp.float32)
    kernel = jnp.sum(mode_weight[:, :, None] * jnp.exp(-li_decay[:, :, None] * lag_pos), axis=1)
    differ = (
        jnp.arange(length_dev, dtype=jnp.int32)[:, None]
        - jnp.arange(length_dev, dtype=jnp.int32)[None, :]
    )
    agrees = (own_counts[:, None] == own_counts[None, :]) & (differ >= 0)
    toeplitz = jnp.where(agrees[None], kernel[:, jnp.clip(differ, 0, length_dev - 1)], 0.0)
    near_part = jnp.einsum("gtp,pgc->tgc", toeplitz, mixed_wide, precision=PRECISE)
    reaches_end = (own_counts == own_counts[-1]).astype(jnp.float32)
    end_decay = jnp.exp(-li_decay[:, :, None] * (length_dev - 1.0 - lag_pos)) * reaches_end
    end_state = jnp.einsum("gmp,pgc->gmc", end_decay, mixed_wide, precision=PRECISE)
    no_start = (own_start >= length_dev).astype(jnp.float32)
    through = jnp.exp(-li_decay * length_dev) * no_start
    factor_in, state_in = carried_in(
        (through, end_state), "seq", compose, (jnp.ones_like(through), jnp.zeros_like(end_state))
    )
    before = (own_counts == ext_counts[1]).astype(jnp.float32)
    rise_weight = (
        jnp.exp(-li_decay[:, :, None] * (lag_pos + 1.0)) * mode_weight[:, :, None] * before
    )
    far_part = jnp.einsum("gmt,gmc->tgc", rise_weight, state_in, precision=PRECISE)
    first_out = (query_gate * (near_part + far_part).reshape(length_dev, channels)).astype(
        jnp.bfloat16
    )
    prior_rows = from_behind(first_out[length_dev - filter_len - 1 :], "seq", 1)
    second_pos = jnp.arange(-(filter_len + 1), length_dev, dtype=jnp.int32)
    second_counts = doc_counts(second_pos, prior_start, own_start, length_dev)
    extended_two = jnp.concatenate([prior_rows, first_out], 0)
    query_two, key_two, value_two = features(
        extended_two, second_counts, feat_second, length_dev + tail_len
    )
    product = (key_two * value_two).astype(jnp.bfloat16)
    query_two = query_two[tail_len:]
    span_all = length_dev + tail_len
    band_pos = jnp.arange(-tail_len, length_dev, dtype=jnp.int32)
    band_counts = doc_counts(band_pos, prior_start, own_start, length_dev)
    lag_taps = (
        jnp.arange(length_dev, dtype=jnp.int32)[:, None]
        + tail_len
        - jnp.arange(span_all, dtype=jnp.int32)[None, :]
    )
    inside = (
        (lag_taps >= 0) & (lag_taps < filter_len) & (own_counts[:, None] == band_counts[None, :])
    )
    band_matrix = jnp.where(
        inside[None],
        mr_filter[:, jnp.clip(lag_taps, 0, filter_len - 1)],
        jnp.zeros((), mr_filter.dtype),
    )
    conv_out = jnp.einsum(
        "gtp,pgc->tgc",
        band_matrix,
        product.reshape(span_all, groups, group_size),
        preferred_element_type=jnp.float32,
    )
    return (query_two * conv_out.reshape(length_dev, channels)).astype(jnp.bfloat16)


def solution(mesh):
    in_specs = (
        P(("groups", "seq"), "chan"),
        P(("groups", "seq")),
        P(None, None, "chan"),
        P("chan", None),
        P("chan", None),
        P(None, None, "chan"),
        P("chan", None),
    )
    out_specs = P(("groups", "seq"), "chan")
    return jax.shard_map(
        per_device, mesh=mesh, in_specs=in_specs, out_specs=out_specs, check_vma=False
    )
```

profile of v0, /device:TPU:24, one launch (start us, length us, event | category | flops | bytes accessed | tf_op | source)
XLA Modules:
  0.0 611.5 jit_solution(7430293093852981670)
XLA Ops:
  7.2 4.7 collective-permute-start.1
  12.7 1.9 collective-permute-start
  19.9 5.6 fusion.7
  25.5 1.7 fusion.29
  27.3 217.0 %gather_fusion = f32[65536,8]{1,0:T(8,128)} fusion(f32[8,256]{0,1:T(8,128)S(1)} %copy.24, s32[65536]{0:T(1024)S(1)} %broadcast_clamp_fusion), kind=kCustom, calls=%fused_computation | custom fusion | bytes 4456448 | tf_op jit(solution)/shard_map/gather | solution.py:88
  244.3 19.4 %copy.25 = f32[256,256,8]{1,0,2:T(8,128)} copy(f32[256,256,8]{2,1,0:T(8,128)} %bitcast.73) | data formatting | bytes 4194304 | tf_op jit(solution)/shard_map/gather | solution.py:88
  264.4 28.9 %all-gather = f32[64,16]{1,0:T(8,128)S(1)} all-gather(f32[8,16]{1,0:T(8,128)S(1)} %get-tuple-element.82), channel_id=2, replica_groups=mesh['groups'=2,'seq'=8,'chan'=2] {'seq'}, dimensions={0}, use_global_device_ids=true | all-gather | bytes 4608 | tf_op jit(solution)/shard_map/all_gather | solution.py:19
  294.3 6.8 %while.12 = (s32[]{:T(128)}, f32[8,16,512]{2,1,0:T(8,128)S(1)}, s32[]{:T(128)}, f32[8,8,16]{2,1,0:T(8,128)S(1)}, f32[8,8,16,512]{3,2,1,0:T(8,128)}, /*index=5*/s32[]{:T(128)}, s32[]{:T(128)}, s32[]{:T(128)}) while((s32[]{:T(128)}, f32[8,16,512]{2,1,0:T(8,128)S(1)}, s32[]{:T(128)}, f32[8,8,16]{2,1,0:T(8,128)S(1)}, f32[8,8,16,512]{3,2,1,0:T(8,128)}, ...), condition=%wide.region_2.3_spmd, body=%wide.region_1.2_spmd.sunk | while | flops 131077 | bytes 788103 | solution.py:27
  301.2 3.6 fusion.48
  304.8 4.7 convolution_add_fusion
  309.5 5.7 copy.28
  315.2 6.8 %fusion.3 = bf16[256,4096]{1,0:T(8,128)(2,1)S(1)} fusion(f32[256,4096]{1,0:T(8,128)} %copy.28, bf16[256,4096]{1,0:T(8,128)(2,1)} %param.9, bf16[2,4096]{1,0:T(2,128)(2,1)S(1)} %collective-permute-done, f32[256]{0:T(256)S(1)} %get-tuple-element.86, f32[4096]{0:T(1024)S(1)} %bitcast.84, f32[256]{0:T(256)S(1)} %get-tuple-element.87, f32[4096]{0:T(1024)S(1)} %bitcast.85, ...), kind=kLoop, calls=%fused_computation.17 | loop fusion | flops 18874368 | bytes 8456192 | tf_op jit(solution)/shard_map/convert_element_type | solution.py:103
  322.0 1.4 slice.168
  323.3 4.9 collective-permute-start.2
  328.5 213.8 %gather_fusion.1 = bf16[98048,8]{1,0:T(8,128)(2,1)} fusion(bf16[8,128]{0,1:T(8,128)(2,1)S(1)} %copy.29, s32[98304]{0:T(1024)} %pad_clamp_fusion), kind=kCustom, calls=%fused_computation.1 | custom fusion | bytes 3529728 | tf_op jit(solution)/shard_map/gather | solution.py:128
  542.3 18.1 %copy.30 = bf16[98048,8]{0,1:T(8,128)(2,1)} copy(bf16[98048,8]{1,0:T(8,128)(2,1)} %gather_fusion.1) | data formatting | bytes 3137536 | tf_op jit(solution)/shard_map/gather | solution.py:128
  560.4 4.9 reshape.254
  565.3 5.7 reshape.255
  571.5 9.6 %multiply_convert_fusion = bf16[383,4096]{1,0:T(8,128)(2,1)} fusion(f32[4096]{0:T(1024)S(1)} %bitcast.96, f32[4096]{0:T(1024)S(1)} %bitcast.97, f32[4096]{0:T(1024)S(1)} %bitcast.92, f32[4096]{0:T(1024)S(1)} %bitcast.93, f32[4096]{0:T(1024)S(1)} %bitcast.94, f32[4096]{0:T(1024)S(1)} %bitcast.95, f32[383]{0:T(512)S(1)} %get-tuple-element.91, ...), kind=kLoop, calls=%fused_computation.4 | loop fusion | flops 43925504 | bytes 6392824 | tf_op jit(solution)/shard_map/convert_element_type | solution.py:113
  581.1 4.7 copy.33
  585.8 5.6 fusion.35
  591.4 5.7 copy.32
  597.1 2.6 fusion.23
  599.7 5.0 fusion.19
  (53 shorter events, 14.1 us)
Async XLA Ops:
  6.5 287.8 %all-gather.4.cloned.1.call-start = ((), (), s32[]{:S(2)}) async-start(), calls=%async_computation | async-start | bytes 2359296 | tf_op jit(solution)/shard_map/all_gather | solution.py:19
  7.2 10.0 %collective-permute-start.1 = (bf16[1]{0:T(256)(128)(2,1)}, bf16[1]{0:T(256)(128)(2,1)}, u32[]{:S(2)}, u32[]{:S(2)}) collective-permute-start(bf16[1]{0:T(256)(128)(2,1)} %convert_element_type.144), channel_id=1, source_target_pairs={{0,2},{2,4},{4,6},{6,8},{8,10},{10,12},{12,14},{1,3},{3,5},{5,7},{... | collective-permute-start | bytes 14 | tf_op jit(solution)/shard_map/ppermute | solution.py:14
  12.7 7.1 %collective-permute-start = (bf16[2,4096]{1,0:T(2,128)(2,1)S(1)}, bf16[2,4096]{1,0:T(2,128)(2,1)S(1)}, u32[]{:S(2)}, u32[]{:S(2)}) collective-permute-start(bf16[2,4096]{1,0:T(2,128)(2,1)S(1)} %slice.131), channel_id=1, source_target_pairs={{0,2},{2,4},{4,6},{6,8},{8,10},{10,12},{12,14},{1,3},{3,5},{5,7},{... | collective-permute-start | bytes 49160 | tf_op jit(solution)/shard_map/ppermute | solution.py:14
  301.2 3.6 copy-start
  315.2 13.1 %copy-start.1 = (f32[3,3,4096]{2,1,0:T(4,128)S(1)}, f32[3,3,4096]{2,1,0:T(4,128)}, u32[]{:S(2)}) copy-start(f32[3,3,4096]{2,1,0:T(4,128)} %param.14) | copy-start | bytes 442372
  315.2 13.2 %copy-start.2 = (bf16[8,128]{1,0:T(8,128)(2,1)S(1)}, bf16[8,128]{1,0:T(8,128)(2,1)}, u32[]{:S(2)}) copy-start(bf16[8,128]{1,0:T(8,128)(2,1)} %param.15) | copy-start | bytes 6148
  323.3 248.2 %collective-permute-start.2 = (bf16[129,4096]{1,0:T(8,128)(2,1)}, bf16[129,4096]{1,0:T(8,128)(2,1)S(1)}, u32[]{:S(2)}, u32[]{:S(2)}) collective-permute-start(bf16[129,4096]{1,0:T(8,128)(2,1)} %slice.168), channel_id=1, source_target_pairs={{0,2},{2,4},{4,6},{6,8},{8,10},{10,12},{12,14},{1,3},{3,5},{5,7},{... | collective-permute-start | bytes 3170312 | tf_op jit(solution)/shard_map/ppermute | solution.py:14
Sparse Core Ops, SparseCore 0:
  27.3 49.2 all-gather.3
where the time goes:
time: 620 us; the launch traced here: 612 us
  local copies, waits for them, and re-layouts  500 us (81%)
  other arithmetic  39.6 us (6%)
  blocking collectives  28.9 us (5%)
  matrix products  15.6 us (3%)
  between operations  15 us (2%)
  starting transfers between devices  11.5 us (2%)
    gather x2, local copies, waits for them, and re-layouts, per_device(): kernel[:, jnp.clip(differ, 0, length_dev - 1)]  236 us
    gather x2, local copies, waits for them, and re-layouts, per_device(): mr_filter[:, jnp.clip(lag_taps, 0, filter_len - 1)]  232 us
    all_gather x1, blocking collectives, carried_in(): gathered = jax.tree.map(lambda a: lax.all_gather(a, axis), part)  28.9 us
  transfers between devices with their start and end apart: 4, of which 0 were waited for; matrix products, arithmetic and copies ran while one was open for 80% of the time, Pallas kernels for 0%

commit v1 on v0

v1 whole, which is shorter than its diff:
```python
import functools
import math

import jax
import jax.numpy as jnp
from jax import lax
from jax.experimental import pallas as pl
from jax.experimental.pallas import tpu as pltpu
from jax.sharding import PartitionSpec as P

F32 = jnp.float32
BF = jnp.bfloat16
WIN = 144
LANE = 128
SMEM = pltpu.SMEM


def dot(a, b):
    return lax.dot_general(a, b, (((1,), (0,)), ((), ())), preferred_element_type=F32)


def iota(shape, dim):
    return lax.broadcasted_iota(jnp.int32, shape, dim)


def column(row):
    n = row.shape[1]
    return jnp.sum(
        jnp.where(iota((n, n), 0) == iota((n, n), 1), row, 0.0), axis=1, keepdims=True
    )


def one(cond):
    return jnp.where(cond, 1.0, 0.0).astype(BF)


def shift_matrix(rows, by, start):
    t, p = iota((rows, rows), 0), iota((rows, rows), 1)
    return one((p == t - by) & ((p >= start) == (t >= start)))


def combine(w, branch, taps):
    total = w[branch, 0:1, :] * taps[0]
    for o in (1, 2):
        total = total + w[branch, o : o + 1, :] * taps[o]
    return total


def first_taps(x, edge, s1, s2, own, prior, length):
    lanes = x.shape[1]
    x1, x2 = dot(s1, x), dot(s2, x)
    row = iota((16, lanes), 0)
    e0, e1 = edge[0:1].astype(F32), edge[1:2].astype(F32)
    m10 = jnp.where(own == 0, 0.0, 1.0)
    m20 = jnp.where((own == 0) | (prior == length - 1), 0.0, 1.0)
    m21 = jnp.where((own == 0) | (own == 1), 0.0, 1.0)
    add1 = jnp.where(row == 0, e1 * m10, 0.0)
    add2 = jnp.where(row == 0, e0 * m20, 0.0) + jnp.where(row == 1, e1 * m21, 0.0)
    x1 = jnp.concatenate([x1[:16] + add1, x1[16:]], 0)
    x2 = jnp.concatenate([x2[:16] + add2, x2[16:]], 0)
    return x.astype(F32), x1, x2


def split(v):
    hi = v.astype(BF)
    return hi, (v - hi.astype(F32)).astype(BF)


def states_kernel(cut, modes, scal, x_ref, edge_ref, w_ref, dec_ref, out_ref, sh_ref):
    g = pl.program_id(0)
    length, lanes = x_ref.shape
    own, prior = scal[0], scal[1]

    @pl.when(g == 0)
    def _():
        sh_ref[0] = shift_matrix(length, 1, own)
        sh_ref[1] = shift_matrix(length, 2, own)
        flag = jnp.full((2 * modes, LANE), own, jnp.int32).astype(F32)
        out_ref[:, pl.ds(out_ref.shape[1] - LANE, LANE)] = flag.astype(BF)

    taps = first_taps(x_ref[...], edge_ref[...], sh_ref[0], sh_ref[1], own, prior, length)
    u = (combine(w_ref, 1, taps) * combine(w_ref, 2, taps)).astype(BF)
    dec = column(dec_ref[pl.ds(g, 1), :])
    p = iota((modes, length), 1)
    lag = (length - 1 - p).astype(F32)
    full = jnp.where((p >= own) | (own >= length), jnp.exp(-dec * lag), 0.0)
    lag = jnp.maximum(cut - 1 - p, 0).astype(F32)
    part = jnp.where(
        (p < cut) & ((p >= own) | (own >= cut)), jnp.exp(-dec * lag), 0.0
    )
    hi, lo = split(jnp.concatenate([full, part], 0))
    both = dot(jnp.concatenate([hi, lo], 0), u)
    state = both[: 2 * modes] + both[2 * modes :]
    out_ref[:, pl.ds(pl.multiple_of(g * lanes, lanes), lanes)] = state.astype(BF)


def pair_kernel(cut, modes, length, scal, mine_ref, other_ref, dec_ref, out_ref):
    groups = dec_ref.shape[0]
    width = mine_ref.shape[1] - LANE
    lanes = width // groups
    even = scal[2] == 0
    end = slice(width, width + LANE)

    def pick(rows, cols):
        a = mine_ref[rows, cols].astype(F32)
        b = other_ref[rows, cols].astype(F32)
        return jnp.where(even, a, b), jnp.where(even, b, a)

    top, low = slice(0, modes), slice(modes, 2 * modes)
    f_bound, s_bound = pick(top, end)
    free_f = jnp.where(f_bound >= length, 1.0, 0.0)
    free_s = jnp.where(s_bound >= length, 1.0, 0.0)
    free_c = jnp.where(s_bound >= cut, 1.0, 0.0)
    out_ref[top, end] = (free_f * free_s).astype(BF)
    out_ref[low, end] = (free_f * free_c).astype(BF)
    for g in range(groups):
        cols = slice(g * lanes, (g + 1) * lanes)
        dec = column(dec_ref[g : g + 1, :])
        f_full, s_full = pick(top, cols)
        _, s_part = pick(low, cols)
        out_ref[top, cols] = (
            s_full + jnp.exp(-dec * length) * free_s[:, :1] * f_full
        ).astype(BF)
        out_ref[low, cols] = (
            s_part + jnp.exp(-dec * cut) * free_c[:, :1] * f_full
        ).astype(BF)


def carry_kernel(cut, modes, length, scal, other_ref, near_ref, dec_ref, *refs):
    far, (own_ref, win_ref) = refs[:-2], refs[-2:]
    groups = dec_ref.shape[0]
    width = other_ref.shape[1] - LANE
    lanes = width // groups
    even = scal[2] == 0
    prior = scal[1]
    end = slice(width, width + 1)
    top, low = slice(0, modes), slice(modes, 2 * modes)
    near_free = near_ref[top, width : width + LANE].astype(F32)[:, :1]
    near_part = near_ref[low, width : width + LANE].astype(F32)[:, :1]
    far_free = [f[:, width : width + LANE].astype(F32)[:, :1] for f in far]
    pass_own = jnp.where(prior >= length, 1.0, 0.0)
    pass_cut = jnp.where(prior >= cut, 1.0, 0.0)
    for g in range(groups):
        cols = slice(g * lanes, (g + 1) * lanes)
        dec = column(dec_ref[g : g + 1, :])
        pair = jnp.exp(-dec * (2 * length))
        behind = jnp.zeros((modes, lanes), F32)
        for f, free in zip(far[::-1], far_free[::-1]):
            behind = f[:, cols].astype(F32) + pair * free * behind
        whole = near_ref[top, cols].astype(F32) + pair * near_free * behind
        odd_own = other_ref[top, cols].astype(F32) + jnp.exp(-dec * length) * pass_own * whole
        odd_win = other_ref[low, cols].astype(F32) + jnp.exp(-dec * cut) * pass_cut * whole
        even_win = near_ref[low, cols].astype(F32) + (
            jnp.exp(-dec * (cut + length)) * near_part * behind
        )
        own = jnp.where(even, whole, odd_own)
        win = jnp.where(even, even_win, odd_win)
        for ref, v in ((own_ref, own), (win_ref, win)):
            hi, lo = split(v)
            ref[:, cols] = jnp.concatenate([hi, lo, hi], 0)


def tables_kernel(cut, modes, length, scal, dec_ref, res_ref, mr_ref, *outs):
    t_own, t_win, r_own, r_win, b_own, b_win, b_head = outs
    g = pl.program_id(0)
    own, prior = scal[0], scal[1]
    wide = 2 * length
    base = length - WIN
    dec_row = dec_ref[pl.ds(g, 1), :]
    weight_row = res_ref[pl.ds(g, 1), :] * jnp.sqrt(
        jnp.maximum(1.0 - jnp.exp(-2.0 * dec_row), 0.0)
    ) / math.sqrt(modes)
    small = 2.0 * dec_row
    series = small * (1.0 - small * (0.5 - small * (1.0 / 6 - small * (1.0 / 24))))
    weight_row = jnp.where(
        small < 0.05,
        res_ref[pl.ds(g, 1), :] * jnp.sqrt(series) / math.sqrt(modes),
        weight_row,
    )
    dec, weight = column(dec_row), column(weight_row)
    back = iota((modes, wide), 1)
    back = jnp.where(back == 0, 0, wide - back).astype(F32)
    taps = jnp.sum(weight * jnp.exp(-dec * back), axis=0, keepdims=True)
    full = pltpu.roll(jnp.broadcast_to(taps, (length, wide)), 0, 1, stride=1, stride_axis=0)
    t, p = iota((length, length), 0), iota((length, length), 1)
    seen = (p <= t) & ((p >= own) == (t >= own))
    t_own[...] = jnp.where(seen, full[:, :length], 0.0).astype(BF)
    tw, pw = iota((WIN, WIN), 0) + base, iota((WIN, WIN), 1) + base
    seen = (pw <= tw) & (pw >= cut) & ((pw >= prior) == (tw >= prior))
    t_win[...] = jnp.where(seen, full[:WIN, :WIN], 0.0).astype(BF)

    tl = iota((modes, length), 1)
    rise = jnp.where(tl < own, weight * jnp.exp(-dec * (tl + 1).astype(F32)), 0.0)
    wl = tl + base
    lag = jnp.maximum(wl - cut + 1, 0)
    fits = (wl >= cut) & ((prior < cut) | (prior > wl))
    rise_w = jnp.where(fits, weight * jnp.exp(-dec * lag.astype(F32)), 0.0)
    for ref, v, rows in ((r_own, rise, length), (r_win, rise_w, WIN)):
        hi = v.astype(BF).astype(F32)
        stack = jnp.concatenate([hi, hi, v - hi, jnp.zeros((LANE - 3 * modes, length), F32)], 0)
        ref[...] = jnp.transpose(stack)[:rows, : 3 * modes].astype(BF)

    count = mr_ref.shape[1]
    o, n = iota((count, wide), 0), iota((count, wide), 1)
    back = dot(mr_ref[...], one(((n == 0) & (o == 0)) | ((n > 0) & (wide - n == o))))
    band = pltpu.roll(
        jnp.broadcast_to(back, (2 * WIN, wide)), 0, 1, stride=1, stride_axis=0
    )
    seen = (p <= t) & ((p >= own) == (t >= own))
    here = jnp.where(seen, band[:length, :length], 0.0)
    b_own[...] = jnp.where(p >= 2, here, 0.0).astype(BF)
    b_head[...] = jnp.where(p >= 2, 0.0, here)[:WIN, :16].astype(BF)
    tb, pb = iota((WIN, WIN), 0), iota((WIN, WIN), 1) + base
    seen = (tb < own) & ((prior >= length) | (pb >= prior))
    b_win[...] = jnp.where(seen, band[WIN : 2 * WIN, :WIN], 0.0).astype(BF)


def own_kernel(
    scal, x_ref, edge_ref, w1_ref, w2_ref, t_ref, r_ref, b_ref, st_ref,
    out_ref, z_ref, q_ref, y_ref, sh_ref,
):
    g = pl.program_id(0)
    length, lanes = x_ref.shape
    own, prior = scal[0], scal[1]

    @pl.when(g == 0)
    def _():
        sh_ref[0] = shift_matrix(length, 1, own)
        sh_ref[1] = shift_matrix(length, 2, own)

    taps = first_taps(x_ref[...], edge_ref[...], sh_ref[0], sh_ref[1], own, prior, length)
    u = (combine(w1_ref, 1, taps) * combine(w1_ref, 2, taps)).astype(BF)
    z = dot(t_ref[...], u) + dot(r_ref[...], st_ref[...])
    y = (combine(w1_ref, 0, taps) * z).astype(BF)
    y_ref[...] = y[:16]
    taps = (y.astype(F32), dot(sh_ref[0], y), dot(sh_ref[1], y))
    w = (combine(w2_ref, 1, taps) * combine(w2_ref, 2, taps)).astype(BF)
    z = dot(b_ref[...], w)
    q = combine(w2_ref, 0, taps)
    z_ref[...] = z[:WIN]
    q_ref[...] = q[:WIN]
    out_ref[...] = (q * z).astype(BF)


def head_kernel(
    scal, tail_ref, w1_ref, w2_ref, t_ref, r_ref, b_ref, bh_ref, st_ref, z_ref, q_ref, y_ref,
    old_ref, out_ref, length,
):
    del old_ref
    rows, lanes = tail_ref.shape
    own, prior = scal[0], scal[1]
    base = length - WIN
    i, k = iota((WIN, rows), 0), iota((WIN, rows), 1)
    tb, pb = i + base, k + (length - rows)
    taps = []
    for o in range(3):
        m = one((pb == tb - o) & ((pb >= prior) == (tb >= prior)))
        taps.append(dot(m, tail_ref[...]))
    u = (combine(w1_ref, 1, taps) * combine(w1_ref, 2, taps)).astype(BF)
    z = dot(t_ref[...], u) + dot(r_ref[...], st_ref[...])
    y = (combine(w1_ref, 0, taps) * z).astype(BF)
    i, k = iota((WIN, WIN), 0), iota((WIN, WIN), 1)
    same = (k + base >= prior) == (i + base >= prior)
    taps = [y.astype(F32)] + [dot(one((k == i - o) & same), y) for o in (1, 2)]
    w = (combine(w2_ref, 1, taps) * combine(w2_ref, 2, taps)).astype(BF)
    head = y_ref[...]
    i, k = iota((16, WIN), 0), iota((16, WIN), 1) - WIN
    ih, kh = iota((16, 16), 0), iota((16, 16), 1)
    reach = (i < own) & ((prior >= length) | (k + length >= prior))
    far = [dot(one((k == i - o) & reach), y) for o in (1, 2)]
    near = [dot(shift_matrix(16, o, own), head) for o in (1, 2)]
    taps = (head.astype(F32), near[0] + far[0], near[1] + far[1])
    wh = combine(w2_ref, 1, taps) * combine(w2_ref, 2, taps)
    z = z_ref[...] + dot(b_ref[...], w) + dot(bh_ref[...], wh.astype(BF))
    q = q_ref[...]
    q = jnp.concatenate([combine(w2_ref, 0, taps), q[16:]], 0)
    out_ref[...] = (q * z).astype(BF)


def per_device(inputs, bounds, feat_first, li_decay, li_residue, feat_second, mr_filter):
    length, channels = inputs.shape
    groups, modes = li_decay.shape
    lanes = channels // groups
    filter_len = mr_filter.shape[1]
    rows = filter_len + 3 + (-(filter_len + 3)) % 16
    cut = length - rows + 2
    size = lax.axis_size("seq")
    place = lax.axis_index("seq")

    def behind(array, by):
        return lax.ppermute(array, "seq", [(i, i + by) for i in range(size - by)])

    own_row = jnp.broadcast_to(bounds.astype(BF)[:, None], (1, channels))
    edge = behind(jnp.concatenate([inputs[length - 2 :], own_row], 0), 1)
    tail = behind(inputs[length - rows :], 1)
    prior = jnp.where(place == 0, length, edge[2, 0].astype(F32).astype(jnp.int32))
    scal = jnp.stack([bounds[0], prior, (place % 2).astype(jnp.int32)])

    sm = pl.BlockSpec(memory_space=SMEM)
    whole = pl.BlockSpec(memory_space=pltpu.VMEM)
    params = pltpu.CompilerParams(vmem_limit_bytes=48 * 1024 * 1024)

    def block(*shape):
        return pl.BlockSpec(shape, lambda g: (0,) * (len(shape) - 1) + (g,))

    def table(*shape):
        return pl.BlockSpec((None,) + shape, lambda g: (g, 0, 0))

    def fixed(*shape):
        return pl.BlockSpec(shape, lambda g: (0,) * len(shape))

    shifts = pltpu.VMEM((2, length, length), BF)
    mine = pl.pallas_call(
        functools.partial(states_kernel, cut, modes),
        grid=(groups,),
        in_specs=[sm, block(length, lanes), block(3, lanes), block(3, 3, lanes), fixed(groups, modes)],
        out_specs=fixed(2 * modes, channels + LANE),
        out_shape=jax.ShapeDtypeStruct((2 * modes, channels + LANE), BF),
        scratch_shapes=[shifts],
        compiler_params=params,
        cost_estimate=pl.CostEstimate(flops=2 * 10**9, bytes_accessed=2**21, transcendentals=0),
        name="states",
    )(scal, inputs, edge, feat_first, li_decay)
    other = lax.ppermute(mine, "seq", [(i, i ^ 1) for i in range(size)])
    pair = pl.pallas_call(
        functools.partial(pair_kernel, cut, modes, length),
        in_specs=[sm] + [whole] * 3,
        out_specs=whole,
        out_shape=jax.ShapeDtypeStruct(mine.shape, BF),
        compiler_params=params,
        name="pair",
    )(scal, mine, other, li_decay)
    near = behind(pair, 2)
    far = [behind(pair[:modes], by) for by in range(4, size, 2)]
    state_shape = jax.ShapeDtypeStruct((3 * modes, channels), BF)
    own_state, win_state = pl.pallas_call(
        functools.partial(carry_kernel, cut, modes, length),
        in_specs=[sm] + [whole] * (3 + len(far)),
        out_specs=[whole] * 2,
        out_shape=[state_shape] * 2,
        compiler_params=params,
        name="carry",
    )(scal, other, near, li_decay, *far)

    shapes = [
        (length, length), (WIN, WIN), (length, 3 * modes), (WIN, 3 * modes),
        (length, length), (WIN, WIN), (WIN, 16),
    ]
    t_own, t_win, r_own, r_win, b_own, b_win, b_head = pl.pallas_call(
        functools.partial(tables_kernel, cut, modes, length),
        grid=(groups,),
        in_specs=[sm, fixed(groups, modes), fixed(groups, modes), table(1, filter_len)],
        out_specs=[table(*s) for s in shapes],
        out_shape=[jax.ShapeDtypeStruct((groups,) + s, BF) for s in shapes],
        compiler_params=params,
        cost_estimate=pl.CostEstimate(flops=8 * 10**9, bytes_accessed=2**22, transcendentals=0),
        name="tables",
    )(scal, li_decay, li_residue, mr_filter.reshape(groups, 1, filter_len))

    out_shape = jax.ShapeDtypeStruct((length, channels), BF)
    head_shape = jax.ShapeDtypeStruct((WIN, channels), F32)
    out, z_head, q_head, y_head = pl.pallas_call(
        own_kernel,
        grid=(groups,),
        in_specs=[
            sm, block(length, lanes), block(3, lanes), block(3, 3, lanes), block(3, 3, lanes),
            table(length, length), table(length, 3 * modes), table(length, length),
            block(3 * modes, lanes),
        ],
        out_specs=[block(length, lanes), block(WIN, lanes), block(WIN, lanes), block(16, lanes)],
        out_shape=[out_shape, head_shape, head_shape, jax.ShapeDtypeStruct((16, channels), BF)],
        scratch_shapes=[shifts],
        compiler_params=params,
        cost_estimate=pl.CostEstimate(flops=8 * 10**9, bytes_accessed=2**23, transcendentals=0),
        name="own",
    )(scal, inputs, edge, feat_first, feat_second, t_own, r_own, b_own, own_state)
    return pl.pallas_call(
        functools.partial(head_kernel, length=length),
        grid=(groups,),
        in_specs=[
            sm, block(rows, lanes), block(3, 3, lanes), block(3, 3, lanes),
            table(WIN, WIN), table(WIN, 3 * modes), table(WIN, WIN), table(WIN, 16),
            block(3 * modes, lanes), block(WIN, lanes), block(WIN, lanes), block(16, lanes),
            pl.BlockSpec(memory_space=pl.ANY),
        ],
        out_specs=block(WIN, lanes),
        out_shape=out_shape,
        input_output_aliases={12: 0},
        compiler_params=params,
        cost_estimate=pl.CostEstimate(flops=8 * 10**9, bytes_accessed=2**22, transcendentals=0),
        name="head",
    )(
        scal, tail, feat_first, feat_second, t_win, r_win, b_win, b_head, win_state,
        z_head, q_head, y_head, out,
    )


def solution(mesh):
    in_specs = (
        P(("groups", "seq"), "chan"),
        P(("groups", "seq")),
        P(None, None, "chan"),
        P("chan", None),
        P("chan", None),
        P(None, None, "chan"),
        P("chan", None),
    )
    out_specs = P(("groups", "seq"), "chan")
    return jax.shard_map(
        per_device, mesh=mesh, in_specs=in_specs, out_specs=out_specs, check_vma=False
    )
```

time: 620 us -> 90.1 us (0.15)
  the two profiles are of different devices: /device:TPU:24 before, /device:TPU:0 now
where the time goes in v1:
time: 90.1 us; the launch traced here: 89.6 us
  starting transfers between devices  43.4 us (48%)
  Pallas kernels  33.4 us (37%)
  waiting for transfers between devices  6.4 us (7%)
  local copies, waits for them, and re-layouts  4.75 us (5%)
  between operations  1.53 us (2%)
    ppermute x5, starting transfers between devices, behind(): return lax.ppermute(array, 'seq', [(i, i + by) for i in range(size - by)])  41 us
    pallas_call x1, Pallas kernels, per_device(): pl.pallas_call(own_kernel, grid=(groups,), in_specs=[sm, block(length, la...  12.7 us
    pallas_call x1, Pallas kernels, per_device(): pl.pallas_call(functools.partial(head_kernel, length=length), grid=(group...  10.1 us
    pallas_call x1, Pallas kernels, per_device(): pl.pallas_call(functools.partial(states_kernel, cut, modes), grid=(groups...  4.97 us
    ppermute x1, waiting for transfers between devices, per_device(): other = lax.ppermute(mine, 'seq', [(i, i ^ 1) for i in range(size)])  4.83 us
    pallas_call x1, Pallas kernels, per_device(): pl.pallas_call(functools.partial(tables_kernel, cut, modes, length), grid...  3.93 us
    unnamed x16, local copies, waits for them, and re-layouts  3.24 us
    ppermute x1, starting transfers between devices, per_device(): other = lax.ppermute(mine, 'seq', [(i, i ^ 1) for i in range(size)])  2.38 us
  transfers between devices with their start and end apart: 6, of which 2 were waited for; matrix products, arithmetic and copies ran while one was open for 0% of the time, Pallas kernels for 20%

profile of v1, /device:TPU:0, one launch (start us, length us, event | category | flops | bytes accessed | tf_op | source)
XLA Modules:
  0.0 89.6 jit_solution(4734695013291909190)
XLA Ops:
  0.7 0.9 slice.13
  1.5 4.8 %collective-permute-start = (bf16[3,4096]{1,0:T(4,128)(2,1)S(1)}, bf16[3,4096]{1,0:T(4,128)(2,1)S(1)}, u32[]{:S(2)}, u32[]{:S(2)}) collective-permute-start(bf16[3,4096]{1,0:T(4,128)(2,1)S(1)} %concatenate.3), channel_id=1, source_target_pairs={{0,2},{2,4},{4,6},{6,8},{8,10},{10,12},{12,14},{1,3},{3,5},{5,7},{... | collective-permute-start | bytes 73736 | tf_op jit(solution)/shard_map/ppermute | solution.py:291
  6.4 1.6 %collective-permute-done.edge_ref = bf16[3,4096]{1,0:T(4,128)(2,1)S(1)} collective-permute-done((bf16[3,4096]{1,0:T(4,128)(2,1)S(1)}, bf16[3,4096]{1,0:T(4,128)(2,1)S(1)}, u32[]{:S(2)}, u32[]{:S(2)}) %collective-permute-start) | collective-permute-done | bytes 24608 | tf_op jit(solution)/shard_map/ppermute | solution.py:291
  8.0 0.5 slice.17
  9.2 0.1 pad_add_fusion.scal
  9.3 1.6 %copy-done = bf16[256,4096]{1,0:T(8,128)(2,1)S(1)} copy-done((bf16[256,4096]{1,0:T(8,128)(2,1)S(1)}, bf16[256,4096]{1,0:T(8,128)(2,1)}, u32[]{:S(2)}) %copy-start) | copy-done | bytes 2097176
  10.8 0.7 copy-done.2
  11.5 0.9 %copy-done.3 = f32[3,3,4096]{2,1,0:T(4,128)S(1)} copy-done((f32[3,3,4096]{2,1,0:T(4,128)S(1)}, f32[3,3,4096]{2,1,0:T(4,128)}, u32[]{:S(2)}) %copy-start.3) | copy-done | bytes 147480
  12.5 5.0 %states.1.mine_ref = bf16[32,4224]{1,0:T(8,128)(2,1)S(1)} custom-call(s32[3]{0:T(128)S(1)} %pad_add_fusion.scal, bf16[256,4096]{1,0:T(8,128)(2,1)S(1)} %copy-done, bf16[3,4096]{1,0:T(4,128)(2,1)S(1)} %collective-permute-done.edge_ref, f32[3,3,4096]{2,1,0:T(4,128)S(1)} %copy-done.3, f32[8,16]{1,0:T(8,128)S(1)} %copy-done.2), custom_call_target="tpu_custom_call" | custom-call | flops 2000000000 | bytes 2097152 | tf_op jit(solution)/shard_map/states/pallas_call | solution.py:313
  17.4 0.0 copy-start.7
  17.5 2.4 %collective-permute-start.2 = (bf16[32,4224]{1,0:T(8,128)(2,1)S(1)}, bf16[32,4224]{1,0:T(8,128)(2,1)S(1)}, u32[]{:S(2)}, u32[]{:S(2)}) collective-permute-start(bf16[32,4224]{1,0:T(8,128)(2,1)S(1)} %states.1.mine_ref), channel_id=1, source_target_pairs={{0,2},{2,0},{4,6},{6,4},{8,10},{10,8},{12,14},{14,12},{1,3},{3,1},... | collective-permute-start | bytes 811016 | tf_op jit(solution)/shard_map/ppermute | solution.py:324
  19.8 0.1 slice.15
  19.9 2.0 %collective-permute-start.1 = (bf16[144,4096]{1,0:T(8,128)(2,1)S(1)}, bf16[144,4096]{1,0:T(8,128)(2,1)S(1)}, u32[]{:S(2)}, u32[]{:S(2)}) collective-permute-start(bf16[144,4096]{1,0:T(8,128)(2,1)S(1)} %slice.15), channel_id=1, source_target_pairs={{0,2},{2,4},{4,6},{6,8},{8,10},{10,12},{12,14},{1,3},{3,5},{5,7},{... | collective-permute-start | bytes 3538952 | tf_op jit(solution)/shard_map/ppermute | solution.py:291
  21.9 4.8 %collective-permute-done.2.other_ref = bf16[32,4224]{1,0:T(8,128)(2,1)S(1)} collective-permute-done((bf16[32,4224]{1,0:T(8,128)(2,1)S(1)}, bf16[32,4224]{1,0:T(8,128)(2,1)S(1)}, u32[]{:S(2)}, u32[]{:S(2)}) %collective-permute-start.2) | collective-permute-done | bytes 270368 | tf_op jit(solution)/shard_map/ppermute | solution.py:324
  26.8 0.8 pair.1
  27.5 28.3 %collective-permute-start.3 = (bf16[32,4224]{1,0:T(8,128)(2,1)S(1)}, bf16[32,4224]{1,0:T(8,128)(2,1)S(1)}, u32[]{:S(2)}, u32[]{:S(2)}) collective-permute-start(bf16[32,4224]{1,0:T(8,128)(2,1)S(1)} %pair.1), channel_id=1, source_target_pairs={{0,4},{2,6},{4,8},{6,10},{8,12},{10,14},{1,5},{3,7},{5,9},{7,11},{... | collective-permute-start | bytes 811016 | tf_op jit(solution)/shard_map/ppermute | solution.py:291
  55.9 0.0 copy-start.4
  55.9 0.0 copy-start.5
  55.9 4.6 %collective-permute-start.4 = (bf16[16,4224]{1,0:T(8,128)(2,1)S(1)}, bf16[16,4224]{1,0:T(8,128)(2,1)S(1)}, u32[]{:S(2)}, u32[]{:S(2)}) collective-permute-start(bf16[16,4224]{1,0:T(8,128)(2,1)S(1)} %slice.18), channel_id=1, source_target_pairs={{0,8},{2,10},{4,12},{6,14},{1,9},{3,11},{5,13},{7,15},{16,24},{18,... | collective-permute-start | bytes 405512 | tf_op jit(solution)/shard_map/ppermute | solution.py:291
  60.5 1.3 %collective-permute-start.5 = (bf16[16,4224]{1,0:T(8,128)(2,1)S(1)}, bf16[16,4224]{1,0:T(8,128)(2,1)S(1)}, u32[]{:S(2)}, u32[]{:S(2)}) collective-permute-start(bf16[16,4224]{1,0:T(8,128)(2,1)S(1)} %slice.18), channel_id=1, source_target_pairs={{0,12},{2,14},{1,13},{3,15},{16,28},{18,30},{17,29},{19,31}} | collective-permute-start | bytes 405512 | tf_op jit(solution)/shard_map/ppermute | solution.py:291
  61.8 3.9 %tables.1 = (bf16[8,256,256]{2,1,0:T(8,128)(2,1)S(1)}, bf16[8,144,144]{2,1,0:T(8,128)(2,1)S(1)}, bf16[8,256,48]{2,1,0:T(8,128)(2,1)S(1)}, bf16[8,144,48]{2,1,0:T...) custom-call(s32[3]{0:T(128)S(1)} %pad_add_fusion.scal, ...), custom_call_target="tpu_custom_call" | custom-call | flops 8000000000 | bytes 4194304 | tf_op jit(solution)/shard_map/tables/pallas_call | solution.py:349
  65.8 0.9 %carry.1 = (bf16[48,4096]{1,0:T(8,128)(2,1)S(1)}, bf16[48,4096]{1,0:T(8,128)(2,1)S(1)}) custom-call(s32[3]{0:T(128)S(1)} %pad_add_fusion.scal, bf16[32,4224]{1,0:T(8,128)(2,1)S(1)} %collective-permute-done.2.other_ref, bf16[32,4224]{1,0:T(8,128)(2,1)S(1)} %collective-permute-done.3.near_ref, f32[8,16]{1,0:T(8,128)S(1)} %copy-done.2, ...), custom_call_target="tpu_custom_call" | custom-call | tf_op jit(solution)/shard_map/carry/pallas_call | solution.py:336
  66.8 12.7 %own.1 = (bf16[256,4096]{1,0:T(8,128)(2,1)}, f32[144,4096]{1,0:T(8,128)}, f32[144,4096]{1,0:T(8,128)}, bf16[16,4096]{1,0:T(8,128)(2,1)S(1)}) custom-call(s32[3]{0:T(128)S(1)} %pad_add_fusion.scal, bf16[256,4096]{1,0:T(8,128)(2,1)S(1)} %copy-done.1, bf16[3,4096]{1,0:T(4,128)(2,1)S(1)} %collective-permute-done.edge_ref, f32[3,3,4096]{2,1,0:T(4,128)S(1)} %copy-done.4, ...), custom_call_target="tpu_custom_call" | custom-call | flops 8000000000 | bytes 8388608 | tf_op jit(solution)/shard_map/own/pallas_call | solution.py:362
  79.5 10.1 %head.1 = bf16[256,4096]{1,0:T(8,128)(2,1)} custom-call(s32[3]{0:T(128)S(1)} %pad_add_fusion.scal, bf16[144,4096]{1,0:T(8,128)(2,1)S(1)} %collective-permute-done.1.tail_ref, f32[3,3,4096]{2,1,0:T(4,128)S(1)} %copy-done.4, f32[3,3,4096]{2,1,0:T(4,128)S(1)} %copy-done.5, ...), custom_call_target="tpu_custom_call", output_to_operand_aliasing={{}: (12, {})} | custom-call | flops 8000000000 | bytes 4194304 | tf_op jit(solution)/shard_map/head/pallas_call | solution.py:377
  (17 shorter events, 0.1 us)
Async XLA Ops:
  1.5 6.4 %collective-permute-start = (bf16[3,4096]{1,0:T(4,128)(2,1)S(1)}, bf16[3,4096]{1,0:T(4,128)(2,1)S(1)}, u32[]{:S(2)}, u32[]{:S(2)}) collective-permute-start(bf16[3,4096]{1,0:T(4,128)(2,1)S(1)} %concatenate.3), channel_id=1, source_target_pairs={{0,2},{2,4},{4,6},{6,8},{8,10},{10,12},{12,14},{1,3},{3,5},{5,7},{... | collective-permute-start | bytes 73736 | tf_op jit(solution)/shard_map/ppermute | solution.py:291
  9.2 1.6 %copy-start = (bf16[256,4096]{1,0:T(8,128)(2,1)S(1)}, bf16[256,4096]{1,0:T(8,128)(2,1)}, u32[]{:S(2)}) copy-start(bf16[256,4096]{1,0:T(8,128)(2,1)} %x_ref.3) | copy-start | bytes 6291460
  10.8 0.7 copy-start.2
  11.5 0.9 %copy-start.3 = (f32[3,3,4096]{2,1,0:T(4,128)S(1)}, f32[3,3,4096]{2,1,0:T(4,128)}, u32[]{:S(2)}) copy-start(f32[3,3,4096]{2,1,0:T(4,128)} %w1_ref.3) | copy-start | bytes 442372
  17.4 4.5 %copy-start.7 = (bf16[8,128]{1,0:T(8,128)(2,1)S(1)}, bf16[8,128]{1,0:T(8,128)(2,1)}, u32[]{:S(2)}) copy-start(bf16[8,128]{1,0:T(8,128)(2,1)} %param.13) | copy-start | bytes 6148
  17.4 44.4 %copy-start.6 = (f32[8,16]{1,0:T(8,128)S(1)}, f32[8,16]{1,0:T(8,128)}, u32[]{:S(2)}) copy-start(f32[8,16]{1,0:T(8,128)} %res_ref.1) | copy-start | bytes 1540
  17.5 9.3 %collective-permute-start.2 = (bf16[32,4224]{1,0:T(8,128)(2,1)S(1)}, bf16[32,4224]{1,0:T(8,128)(2,1)S(1)}, u32[]{:S(2)}, u32[]{:S(2)}) collective-permute-start(bf16[32,4224]{1,0:T(8,128)(2,1)S(1)} %states.1.mine_ref), channel_id=1, source_target_pairs={{0,2},{2,0},{4,6},{6,4},{8,10},{10,8},{12,14},{14,12},{1,3},{3,1},... | collective-permute-start | bytes 811016 | tf_op jit(solution)/shard_map/ppermute | solution.py:324
  19.9 59.5 %collective-permute-start.1 = (bf16[144,4096]{1,0:T(8,128)(2,1)S(1)}, bf16[144,4096]{1,0:T(8,128)(2,1)S(1)}, u32[]{:S(2)}, u32[]{:S(2)}) collective-permute-start(bf16[144,4096]{1,0:T(8,128)(2,1)S(1)} %slice.15), channel_id=1, source_target_pairs={{0,2},{2,4},{4,6},{6,8},{8,10},{10,12},{12,14},{1,3},{3,5},{5,7},{... | collective-permute-start | bytes 3538952 | tf_op jit(solution)/shard_map/ppermute | solution.py:291
  27.5 38.2 %collective-permute-start.3 = (bf16[32,4224]{1,0:T(8,128)(2,1)S(1)}, bf16[32,4224]{1,0:T(8,128)(2,1)S(1)}, u32[]{:S(2)}, u32[]{:S(2)}) collective-permute-start(bf16[32,4224]{1,0:T(8,128)(2,1)S(1)} %pair.1), channel_id=1, source_target_pairs={{0,4},{2,6},{4,8},{6,10},{8,12},{10,14},{1,5},{3,7},{5,9},{7,11},{... | collective-permute-start | bytes 811016 | tf_op jit(solution)/shard_map/ppermute | solution.py:291
  55.9 10.9 %copy-start.1 = (bf16[256,4096]{1,0:T(8,128)(2,1)S(1)}, bf16[256,4096]{1,0:T(8,128)(2,1)}, u32[]{:S(2)}) copy-start(bf16[256,4096]{1,0:T(8,128)(2,1)} %x_ref.3) | copy-start | bytes 6291460
  55.9 10.9 %copy-start.4 = (f32[3,3,4096]{2,1,0:T(4,128)S(1)}, f32[3,3,4096]{2,1,0:T(4,128)}, u32[]{:S(2)}) copy-start(f32[3,3,4096]{2,1,0:T(4,128)} %w1_ref.3) | copy-start | bytes 442372
  55.9 10.9 %copy-start.5 = (f32[3,3,4096]{2,1,0:T(4,128)S(1)}, f32[3,3,4096]{2,1,0:T(4,128)}, u32[]{:S(2)}) copy-start(f32[3,3,4096]{2,1,0:T(4,128)} %w2_ref.3) | copy-start | bytes 442372
  55.9 9.9 %collective-permute-start.4 = (bf16[16,4224]{1,0:T(8,128)(2,1)S(1)}, bf16[16,4224]{1,0:T(8,128)(2,1)S(1)}, u32[]{:S(2)}, u32[]{:S(2)}) collective-permute-start(bf16[16,4224]{1,0:T(8,128)(2,1)S(1)} %slice.18), channel_id=1, source_target_pairs={{0,8},{2,10},{4,12},{6,14},{1,9},{3,11},{5,13},{7,15},{16,24},{18,... | collective-permute-start | bytes 405512 | tf_op jit(solution)/shard_map/ppermute | solution.py:291
  60.5 5.3 %collective-permute-start.5 = (bf16[16,4224]{1,0:T(8,128)(2,1)S(1)}, bf16[16,4224]{1,0:T(8,128)(2,1)S(1)}, u32[]{:S(2)}, u32[]{:S(2)}) collective-permute-start(bf16[16,4224]{1,0:T(8,128)(2,1)S(1)} %slice.18), channel_id=1, source_target_pairs={{0,12},{2,14},{1,13},{3,15},{16,28},{18,30},{17,29},{19,31}} | collective-permute-start | bytes 405512 | tf_op jit(solution)/shard_map/ppermute | solution.py:291

commit v2 on v1

v2 whole, which is shorter than its diff:
```python
import functools
import math

import jax
import jax.numpy as jnp
from jax import lax
from jax.experimental import pallas as pl
from jax.experimental.pallas import tpu as pltpu
from jax.sharding import PartitionSpec as P

F32 = jnp.float32
BF = jnp.bfloat16
WIN = 144
LANE = 128
SMEM = pltpu.SMEM


def dot(a, b):
    return lax.dot_general(a, b, (((1,), (0,)), ((), ())), preferred_element_type=F32)


def iota(shape, dim):
    return lax.broadcasted_iota(jnp.int32, shape, dim)


def column(row):
    n = row.shape[1]
    return jnp.sum(
        jnp.where(iota((n, n), 0) == iota((n, n), 1), row, 0.0), axis=1, keepdims=True
    )


def one(cond):
    return jnp.where(cond, 1.0, 0.0).astype(BF)


def combine(w, branch, taps, cols):
    total = w[branch, 0:1, cols] * taps[0]
    for o in (1, 2):
        total = total + w[branch, o : o + 1, cols] * taps[o]
    return total


def spans(count, lanes):
    return [(i, slice(i * lanes, (i + 1) * lanes)) for i in range(count)]


def write_masks(ref, offset, own, prior, length):
    rows = ref.shape[1]
    t = iota((rows, LANE), 0) - offset
    before = jnp.where(prior < length, prior, -length) - length
    one_back = (t != own) & (t != before)
    two_back = one_back & (t - 1 != own) & (t - 1 != before)
    ref[0] = jnp.where(one_back, 1.0, 0.0)
    ref[1] = jnp.where(two_back, 1.0, 0.0)


def widen(mask, lanes):
    return jnp.concatenate([mask] * (lanes // LANE), 1)


def first_taps(x, edge, mask_ref):
    length, lanes = x.shape
    x0 = x.astype(F32)
    row = iota((8, lanes), 0)
    e0, e1 = edge[0:1].astype(F32), edge[1:2].astype(F32)
    x1, x2 = pltpu.roll(x0, 1, 0), pltpu.roll(x0, 2, 0)
    top1 = jnp.where(row == 0, e1, x1[:8])
    top2 = jnp.where(row == 0, e0, jnp.where(row == 1, e1, x2[:8]))
    x1 = jnp.concatenate([top1, x1[8:]], 0) * widen(mask_ref[0], lanes)
    x2 = jnp.concatenate([top2, x2[8:]], 0) * widen(mask_ref[1], lanes)
    return x0, x1, x2


def split(v):
    hi = v.astype(BF)
    return hi, (v - hi.astype(F32)).astype(BF)


def states_kernel(
    cut, modes, lanes, scal, x_ref, edge_ref, w_ref, dec_ref, out_ref, part_ref, mask_ref
):
    step = pl.program_id(0)
    length, step_lanes = x_ref.shape
    count = step_lanes // lanes
    own, prior = scal[0], scal[1]

    @pl.when(step == 0)
    def _():
        write_masks(mask_ref, 0, own, prior, length)
        flag = jnp.full((modes, LANE), own, jnp.int32).astype(F32)
        out_ref[:, pl.ds(out_ref.shape[1] - LANE, LANE)] = flag.astype(BF)

    p = iota((modes, length), 1)
    lag = (length - 1 - p).astype(F32)
    lag_cut = jnp.maximum(cut - 1 - p, 0).astype(F32)
    reach = (p >= own) | (own >= length)
    reach_cut = (p < cut) & ((p >= own) | (own >= cut))
    for i, cols in spans(count, lanes):
        taps = first_taps(x_ref[:, cols], edge_ref[:, cols], mask_ref)
        u = (combine(w_ref, 1, taps, cols) * combine(w_ref, 2, taps, cols)).astype(BF)
        dec = column(dec_ref[pl.ds(step * count + i, 1), :])
        full = jnp.where(reach, jnp.exp(-dec * lag), 0.0)
        part = jnp.where(reach_cut, jnp.exp(-dec * lag_cut), 0.0)
        hi, lo = split(jnp.concatenate([full, part], 0))
        both = dot(jnp.concatenate([hi, lo], 0), u)
        state = both[: 2 * modes] + both[2 * modes :]
        at = pl.ds(pl.multiple_of((step * count + i) * lanes, lanes), lanes)
        out_ref[:, at] = state[:modes].astype(BF)
        part_ref[:, at] = state[modes:].astype(BF)


def pair_kernel(modes, length, scal, mine_ref, other_ref, dec_ref, out_ref):
    groups = dec_ref.shape[0]
    width = mine_ref.shape[1] - LANE
    lanes = width // groups
    even = scal[2] == 0
    end = slice(width, width + LANE)

    def pick(cols):
        a, b = mine_ref[:, cols].astype(F32), other_ref[:, cols].astype(F32)
        return jnp.where(even, a, b), jnp.where(even, b, a)

    top, low = slice(0, modes), slice(modes, 2 * modes)
    f_bound, s_bound = pick(end)
    free_f = jnp.where(f_bound >= length, 1.0, 0.0)
    free_s = jnp.where(s_bound >= length, 1.0, 0.0)
    out_ref[top, end] = (free_f * free_s).astype(BF)
    out_ref[low, end] = free_f.astype(BF)
    for g in range(groups):
        cols = slice(g * lanes, (g + 1) * lanes)
        dec = column(dec_ref[g : g + 1, :])
        first, second = pick(cols)
        out_ref[top, cols] = (second + jnp.exp(-dec * length) * free_s[:, :1] * first).astype(BF)
        out_ref[low, cols] = first.astype(BF)


def carry_kernel(modes, length, near_ref, dec_ref, *refs):
    far, (send_ref, own_ref, late_ref) = refs[:-3], refs[-3:]
    groups = dec_ref.shape[0]
    width = own_ref.shape[1]
    lanes = width // groups
    top, low = slice(0, modes), slice(modes, 2 * modes)
    near_free = near_ref[top, width : width + LANE].astype(F32)[:, :1]
    late_free = near_ref[low, width : width + LANE].astype(F32)[:, :1]
    far_free = [f[:, width : width + LANE].astype(F32)[:, :1] for f in far]
    for g in range(groups):
        cols = slice(g * lanes, (g + 1) * lanes)
        dec = column(dec_ref[g : g + 1, :])
        once = jnp.exp(-dec * length)
        pair = jnp.exp(-dec * (2 * length))
        behind = jnp.zeros((modes, lanes), F32)
        for f, free in zip(far[::-1], far_free[::-1]):
            behind = f[:, cols].astype(F32) + pair * free * behind
        whole = near_ref[top, cols].astype(F32) + pair * near_free * behind
        send_ref[:, cols] = whole.astype(BF)
        own_ref[:, cols] = whole
        late_ref[:, cols] = near_ref[low, cols].astype(F32) + once * late_free * behind


def place_kernel(
    cut, modes, length, scal, other_ref, part_ref, sent_ref, even_own, even_late, dec_ref,
    own_ref, win_ref,
):
    groups = dec_ref.shape[0]
    lanes = own_ref.shape[1] // groups
    even = scal[2] == 0
    prior = scal[1]
    pass_own = jnp.where(prior >= length, 1.0, 0.0)
    pass_cut = jnp.where(prior >= cut, 1.0, 0.0)
    for g in range(groups):
        cols = slice(g * lanes, (g + 1) * lanes)
        dec = column(dec_ref[g : g + 1, :])
        sent = sent_ref[:, cols].astype(F32)
        odd_own = other_ref[:, cols].astype(F32) + jnp.exp(-dec * length) * pass_own * sent
        before = jnp.where(even, even_late[:, cols], sent)
        own = jnp.where(even, even_own[:, cols], odd_own)
        win = part_ref[:, cols].astype(F32) + jnp.exp(-dec * cut) * pass_cut * before
        for ref, v in ((own_ref, own), (win_ref, win)):
            hi, lo = split(v)
            ref[:, cols] = jnp.concatenate([hi, lo, hi], 0)


def tables_kernel(cut, modes, length, scal, dec_ref, res_ref, mr_ref, *outs):
    t_own, t_own_lo, t_win, t_win_lo, r_own, r_win, b_win, b_own = outs
    g = pl.program_id(0)
    own, prior = scal[0], scal[1]
    wide = 2 * length
    base = length - WIN
    dec_row = dec_ref[pl.ds(g, 1), :]
    weight_row = res_ref[pl.ds(g, 1), :] * jnp.sqrt(
        jnp.maximum(1.0 - jnp.exp(-2.0 * dec_row), 0.0)
    ) / math.sqrt(modes)
    small = 2.0 * dec_row
    series = small * (1.0 - small * (0.5 - small * (1.0 / 6 - small * (1.0 / 24))))
    weight_row = jnp.where(
        small < 0.05,
        res_ref[pl.ds(g, 1), :] * jnp.sqrt(series) / math.sqrt(modes),
        weight_row,
    )
    dec, weight = column(dec_row), column(weight_row)
    back = iota((modes, wide), 1)
    back = jnp.where(back == 0, 0, wide - back).astype(F32)
    taps = jnp.sum(weight * jnp.exp(-dec * back), axis=0, keepdims=True)
    full = pltpu.roll(jnp.broadcast_to(taps, (length, wide)), 0, 1, stride=1, stride_axis=0)
    t, p = iota((length, length), 0), iota((length, length), 1)
    seen = (p <= t) & ((p >= own) == (t >= own))
    t_own[...], t_own_lo[...] = split(jnp.where(seen, full[:, :length], 0.0))
    tw, pw = iota((WIN, WIN), 0) + base, iota((WIN, WIN), 1) + base
    seen = (pw <= tw) & (pw >= cut) & ((pw >= prior) == (tw >= prior))
    t_win[...], t_win_lo[...] = split(jnp.where(seen, full[:WIN, :WIN], 0.0))

    tl = iota((modes, length), 1)
    rise = jnp.where(tl < own, weight * jnp.exp(-dec * (tl + 1).astype(F32)), 0.0)
    wl = tl + base
    lag = jnp.maximum(wl - cut + 1, 0)
    fits = (wl >= cut) & ((prior < cut) | (prior > wl))
    rise_w = jnp.where(fits, weight * jnp.exp(-dec * lag.astype(F32)), 0.0)
    for ref, v, rows in ((r_own, rise, length), (r_win, rise_w, WIN)):
        hi = v.astype(BF).astype(F32)
        stack = jnp.concatenate([hi, hi, v - hi, jnp.zeros((LANE - 3 * modes, length), F32)], 0)
        ref[...] = jnp.transpose(stack)[:rows, : 3 * modes].astype(BF)

    count = mr_ref.shape[1]
    o, n = iota((count, wide), 0), iota((count, wide), 1)
    back = dot(mr_ref[...], one(((n == 0) & (o == 0)) | ((n > 0) & (wide - n == o))))
    band = pltpu.roll(
        jnp.broadcast_to(back, (WIN + length, wide)), 0, 1, stride=1, stride_axis=0
    )
    seen = (p <= t) & ((p >= own) == (t >= own))
    b_own[...] = jnp.where(seen, band[:length, :length], 0.0).astype(BF)
    tb, pb = iota((length, WIN), 0), iota((length, WIN), 1) + base
    seen = (tb < own) & ((prior >= length) | (pb >= prior))
    b_win[...] = jnp.where(seen, band[WIN : WIN + length, :WIN], 0.0).astype(BF)


def near_kernel(lanes, scal, x_ref, edge_ref, w_ref, t_ref, lo_ref, q_ref, z_ref, mask_ref):
    @pl.when(pl.program_id(0) == 0)
    def _():
        write_masks(mask_ref, 0, scal[0], scal[1], x_ref.shape[0])

    for i, cols in spans(x_ref.shape[1] // lanes, lanes):
        taps = first_taps(x_ref[:, cols], edge_ref[:, cols], mask_ref)
        u = (combine(w_ref, 1, taps, cols) * combine(w_ref, 2, taps, cols)).astype(BF)
        z_ref[:, cols] = dot(t_ref[i], u) + dot(lo_ref[i], u)
        q_ref[:, cols] = combine(w_ref, 0, taps, cols)


def near_tail_kernel(length, lanes, scal, tail_ref, w_ref, t_ref, lo_ref, q_ref, z_ref, sh_ref):
    rows = tail_ref.shape[0]
    prior = scal[1]

    @pl.when(pl.program_id(0) == 0)
    def _():
        tb = iota((WIN, rows), 0) + (length - WIN)
        pb = iota((WIN, rows), 1) + (length - rows)
        for o in range(3):
            sh_ref[o] = one((pb == tb - o) & ((pb >= prior) == (tb >= prior)))

    for i, cols in spans(tail_ref.shape[1] // lanes, lanes):
        x = tail_ref[:, cols]
        taps = [dot(sh_ref[o], x) for o in range(3)]
        u = (combine(w_ref, 1, taps, cols) * combine(w_ref, 2, taps, cols)).astype(BF)
        z_ref[:, cols] = dot(t_ref[i], u) + dot(lo_ref[i], u)
        q_ref[:, cols] = combine(w_ref, 0, taps, cols)


def final_kernel(
    lanes, scal, q_ref, z_ref, qt_ref, zt_ref, r_ref, rt_ref, st_ref, stt_ref, w_ref, bt_ref,
    b_ref, out_ref, mask_ref,
):
    length = q_ref.shape[0]

    @pl.when(pl.program_id(0) == 0)
    def _():
        write_masks(mask_ref, WIN, scal[0], scal[1], length)

    for i, cols in spans(q_ref.shape[1] // lanes, lanes):
        yt = qt_ref[:, cols] * (zt_ref[:, cols] + dot(rt_ref[i], stt_ref[:, cols]))
        y = q_ref[:, cols] * (z_ref[:, cols] + dot(r_ref[i], st_ref[:, cols]))
        y = jnp.concatenate([yt, y], 0).astype(BF).astype(F32)
        m1, m2 = widen(mask_ref[0], lanes), widen(mask_ref[1], lanes)
        taps = (y, pltpu.roll(y, 1, 0) * m1, pltpu.roll(y, 2, 0) * m2)
        w = (combine(w_ref, 1, taps, cols) * combine(w_ref, 2, taps, cols)).astype(BF)
        z = dot(bt_ref[i], w[:WIN]) + dot(b_ref[i], w[WIN:])
        q = combine(w_ref, 0, [a[WIN:] for a in taps], cols)
        out_ref[:, cols] = (q * z).astype(BF)


def per_device(inputs, bounds, feat_first, li_decay, li_residue, feat_second, mr_filter):
    length, channels = inputs.shape
    groups, modes = li_decay.shape
    lanes = channels // groups
    filter_len = mr_filter.shape[1]
    rows = filter_len + 3
    cut = length - rows + 2
    size = lax.axis_size("seq")
    place = lax.axis_index("seq")

    def behind(array, by):
        return lax.ppermute(array, "seq", [(i, i + by) for i in range(size - by)])

    own_row = jnp.broadcast_to(bounds.astype(BF)[:, None], (1, channels))
    edge = behind(jnp.concatenate([inputs[length - 2 :], own_row], 0), 1)
    prior = jnp.where(place == 0, length, edge[2, 0].astype(F32).astype(jnp.int32))
    scal = jnp.stack([bounds[0], prior, (place % 2).astype(jnp.int32)])

    sm = pl.BlockSpec(memory_space=SMEM)
    whole = pl.BlockSpec(memory_space=pltpu.VMEM)
    params = pltpu.CompilerParams(vmem_limit_bytes=24 * 1024 * 1024)
    count = 2 if groups % 2 == 0 else 1
    steps, wide = groups // count, lanes * count

    def block(*shape):
        return pl.BlockSpec(shape, lambda g: (0,) * (len(shape) - 1) + (g,))

    def table(*shape):
        return pl.BlockSpec((count,) + shape, lambda g: (g, 0, 0))

    def single(*shape):
        return pl.BlockSpec((None,) + shape, lambda g: (g, 0, 0))

    def fixed(*shape):
        return pl.BlockSpec(shape, lambda g: (0,) * len(shape))

    mine, part = pl.pallas_call(
        functools.partial(states_kernel, cut, modes, lanes),
        grid=(steps,),
        in_specs=[sm, block(length, wide), block(3, wide), block(3, 3, wide), fixed(groups, modes)],
        out_specs=[fixed(modes, channels + LANE), fixed(modes, channels)],
        out_shape=[
            jax.ShapeDtypeStruct((modes, channels + LANE), BF),
            jax.ShapeDtypeStruct((modes, channels), BF),
        ],
        scratch_shapes=[pltpu.VMEM((2, length, LANE), F32)],
        compiler_params=params,
        cost_estimate=pl.CostEstimate(flops=2 * 10**9, bytes_accessed=2**21, transcendentals=0),
        name="states",
    )(scal, inputs, edge, feat_first, li_decay)
    other = lax.ppermute(mine, "seq", [(i, i ^ 1) for i in range(size)])
    inputs_late, other = lax.optimization_barrier((inputs, other))
    tail_rows, other = lax.optimization_barrier((inputs_late[length - rows :], other))
    tail = behind(tail_rows, 1)
    pair = pl.pallas_call(
        functools.partial(pair_kernel, modes, length),
        in_specs=[sm] + [whole] * 3,
        out_specs=whole,
        out_shape=jax.ShapeDtypeStruct((2 * modes, channels + LANE), BF),
        compiler_params=params,
        name="pair",
    )(scal, mine, other, li_decay)
    near = lax.ppermute(pair, "seq", [(i, i + 2) for i in range(0, size - 2, 2)])
    far = [
        lax.ppermute(pair[:modes], "seq", [(i, i + by) for i in range(0, size - by, 2)])
        for by in range(4, size, 2)
    ]
    state_shape = jax.ShapeDtypeStruct((modes, channels), F32)
    send, even_own, even_late = pl.pallas_call(
        functools.partial(carry_kernel, modes, length),
        in_specs=[whole] * (2 + len(far)),
        out_specs=[whole] * 3,
        out_shape=[jax.ShapeDtypeStruct((modes, channels), BF), state_shape, state_shape],
        compiler_params=params,
        name="carry",
    )(near, li_decay, *far)
    part, send = lax.optimization_barrier((part, send))
    part = behind(part, 1)
    sent = lax.ppermute(send, "seq", [(i, i + 1) for i in range(0, size, 2)])
    own_state, win_state = pl.pallas_call(
        functools.partial(place_kernel, cut, modes, length),
        in_specs=[sm] + [whole] * 6,
        out_specs=[whole] * 2,
        out_shape=[jax.ShapeDtypeStruct((3 * modes, channels), BF)] * 2,
        compiler_params=params,
        name="place",
    )(scal, other, part, sent, even_own, even_late, li_decay)

    shapes = [
        (length, length), (length, length), (WIN, WIN), (WIN, WIN),
        (length, 3 * modes), (WIN, 3 * modes), (length, WIN), (length, length),
    ]
    t_own, t_own_lo, t_win, t_win_lo, r_own, r_win, b_win, b_own = pl.pallas_call(
        functools.partial(tables_kernel, cut, modes, length),
        grid=(groups,),
        in_specs=[sm, fixed(groups, modes), fixed(groups, modes), single(1, filter_len)],
        out_specs=[single(*s) for s in shapes],
        out_shape=[jax.ShapeDtypeStruct((groups,) + s, BF) for s in shapes],
        compiler_params=params,
        cost_estimate=pl.CostEstimate(flops=8 * 10**9, bytes_accessed=2**22, transcendentals=0),
        name="tables",
    )(scal, li_decay, li_residue, mr_filter.reshape(groups, 1, filter_len))

    q_own, z_own = pl.pallas_call(
        functools.partial(near_kernel, lanes),
        grid=(steps,),
        in_specs=[
            sm, block(length, wide), block(3, wide), block(3, 3, wide),
            table(length, length), table(length, length),
        ],
        out_specs=[block(length, wide)] * 2,
        out_shape=[jax.ShapeDtypeStruct((length, channels), F32)] * 2,
        scratch_shapes=[pltpu.VMEM((2, length, LANE), F32)],
        compiler_params=params,
        cost_estimate=pl.CostEstimate(flops=8 * 10**9, bytes_accessed=2**23, transcendentals=0),
        name="near",
    )(scal, inputs, edge, feat_first, t_own, t_own_lo)
    q_win, z_win = pl.pallas_call(
        functools.partial(near_tail_kernel, length, lanes),
        grid=(steps,),
        in_specs=[
            sm, block(rows, wide), block(3, 3, wide), table(WIN, WIN), table(WIN, WIN),
        ],
        out_specs=[block(WIN, wide)] * 2,
        out_shape=[jax.ShapeDtypeStruct((WIN, channels), F32)] * 2,
        scratch_shapes=[pltpu.VMEM((3, WIN, rows), BF)],
        compiler_params=params,
        cost_estimate=pl.CostEstimate(flops=4 * 10**9, bytes_accessed=2**22, transcendentals=0),
        name="near_tail",
    )(scal, tail, feat_first, t_win, t_win_lo)
    return pl.pallas_call(
        functools.partial(final_kernel, lanes),
        grid=(steps,),
        in_specs=[
            sm, block(length, wide), block(length, wide), block(WIN, wide), block(WIN, wide),
            table(length, 3 * modes), table(WIN, 3 * modes),
            block(3 * modes, wide), block(3 * modes, wide), block(3, 3, wide),
            table(length, WIN), table(length, length),
        ],
        out_specs=block(length, wide),
        out_shape=jax.ShapeDtypeStruct((length, channels), BF),
        scratch_shapes=[pltpu.VMEM((2, WIN + length, LANE), F32)],
        compiler_params=params,
        cost_estimate=pl.CostEstimate(flops=8 * 10**9, bytes_accessed=2**24, transcendentals=0),
        name="final",
    )(
        scal, q_own, z_own, q_win, z_win, r_own, r_win, own_state, win_state, feat_second,
        b_win, b_own,
    )


def solution(mesh):
    in_specs = (
        P(("groups", "seq"), "chan"),
        P(("groups", "seq")),
        P(None, None, "chan"),
        P("chan", None),
        P("chan", None),
        P(None, None, "chan"),
        P("chan", None),
    )
    out_specs = P(("groups", "seq"), "chan")
    return jax.shard_map(
        per_device, mesh=mesh, in_specs=in_specs, out_specs=out_specs, check_vma=False
    )
```

time: 90.1 us -> 77.9 us (0.86)
  starting transfers between devices: 43.4 us -> 26.7 us
  waiting for transfers between devices: 6.4 us -> 13.3 us
  Pallas kernels: 33.4 us -> 30.9 us
    ppermute x5 -> x3, starting transfers between devices: 41 us -> 8.88 us  [behind(): return lax.ppermute(array, 'seq', [(i, i + by) for i in range(size - by)])]
    ppermute x0 -> x4, starting transfers between devices: none -> 15.5 us  [the longest x2 5.92 us: per_device(): lax.ppermute(pair[:modes], 'seq', [(i, i + by) for i in range(0, size - b...]
    ppermute x5 -> x3, waiting for transfers between devices: 1.58 us -> 8.94 us  [behind(): return lax.ppermute(array, 'seq', [(i, i + by) for i in range(size - by)])]
    pallas_call x5 -> x7, Pallas kernels: 29.5 us -> 26.6 us  [the longest x1 9.73 us: per_device(): pl.pallas_call(functools.partial(final_kernel, lanes), grid=(steps,), in_...]
    ppermute x1, waiting for transfers between devices: 4.83 us -> 2.98 us  [per_device(): other = lax.ppermute(mine, 'seq', [(i, i ^ 1) for i in range(size)])]
    ppermute x0 -> x4, waiting for transfers between devices: none -> 1.41 us  [the longest x1 1.4 us: per_device(): sent = lax.ppermute(send, 'seq', [(i, i + 1) for i in range(0, size, 2)])]
    unnamed x16 -> x18, local copies, waits for them, and re-layouts: 3.24 us -> 3.24 us
  transfers between devices with their start and end apart: 6 -> 8, of which waited for: 2 -> 4; matrix products, arithmetic and copies ran while one was open for 0% -> 0% of each run, Pallas kernels for 20% -> 15%
where the time goes in v2:
time: 77.9 us; the launch traced here: 77.5 us
  Pallas kernels  30.9 us (40%)
  starting transfers between devices  26.7 us (34%)
  waiting for transfers between devices  13.3 us (17%)
  local copies, waits for them, and re-layouts  4.95 us (6%)
  between operations  1.56 us (2%)
    pallas_call x1, Pallas kernels, per_device(): pl.pallas_call(functools.partial(final_kernel, lanes), grid=(steps,), in_...  9.73 us
    ppermute x3, waiting for transfers between devices, behind(): return lax.ppermute(array, 'seq', [(i, i + by) for i in range(size - by)])  8.94 us
    ppermute x3, starting transfers between devices, behind(): return lax.ppermute(array, 'seq', [(i, i + by) for i in range(size - by)])  8.88 us
    pallas_call x1, Pallas kernels, per_device(): pl.pallas_call(functools.partial(near_kernel, lanes), grid=(steps,), in_s...  6.04 us
    ppermute x2, starting transfers between devices, per_device(): lax.ppermute(pair[:modes], 'seq', [(i, i + by) for i in range(0, size - b...  5.92 us
    pallas_call x1, Pallas kernels, per_device(): pl.pallas_call(functools.partial(near_tail_kernel, length, lanes), grid=(...  4.95 us
    ppermute x1, starting transfers between devices, per_device(): lax.ppermute(pair, 'seq', [(i, i + 2) for i in range(0, size - 2, 2)])  4.93 us
    ppermute x1, starting transfers between devices, per_device(): sent = lax.ppermute(send, 'seq', [(i, i + 1) for i in range(0, size, 2)])  4.61 us
  transfers between devices with their start and end apart: 8, of which 4 were waited for; matrix products, arithmetic and copies ran while one was open for 0% of the time, Pallas kernels for 15%

profile of v2, /device:TPU:0, one launch (start us, length us, event | category | flops | bytes accessed | tf_op | source)
XLA Modules:
  0.0 77.5 jit_solution(10653670709633335365)
XLA Ops:
  0.0 0.9 %slice.13 = bf16[2,4096]{1,0:T(2,128)(2,1)S(1)} slice(bf16[256,4096]{1,0:T(8,128)(2,1)} %x_ref.3), slice={[254:256], [0:4096]} | slice | bytes 32768 | tf_op jit(solution)/shard_map/slice | solution.py:304
  1.5 4.8 %collective-permute-start = (bf16[3,4096]{1,0:T(4,128)(2,1)S(1)}, bf16[3,4096]{1,0:T(4,128)(2,1)S(1)}, u32[]{:S(2)}, u32[]{:S(2)}) collective-permute-start(bf16[3,4096]{1,0:T(4,128)(2,1)S(1)} %concatenate.3), channel_id=1, source_target_pairs={{0,2},{2,4},{4,6},{6,8},{8,10},{10,12},{12,14},{1,3},{3,5},{5,7},{... | collective-permute-start | bytes 73736 | tf_op jit(solution)/shard_map/ppermute | solution.py:301
  6.4 1.6 %collective-permute-done.edge_ref = bf16[3,4096]{1,0:T(4,128)(2,1)S(1)} collective-permute-done((bf16[3,4096]{1,0:T(4,128)(2,1)S(1)}, bf16[3,4096]{1,0:T(4,128)(2,1)S(1)}, u32[]{:S(2)}, u32[]{:S(2)}) %collective-permute-start) | collective-permute-done | bytes 24608 | tf_op jit(solution)/shard_map/ppermute | solution.py:301
  8.0 0.5 slice.17
  9.2 1.6 %copy-done = bf16[256,4096]{1,0:T(8,128)(2,1)S(1)} copy-done((bf16[256,4096]{1,0:T(8,128)(2,1)S(1)}, bf16[256,4096]{1,0:T(8,128)(2,1)}, u32[]{:S(2)}) %copy-start) | copy-done | bytes 2097176
  10.8 0.7 copy-done.2
  11.5 0.9 %copy-done.4 = f32[3,3,4096]{2,1,0:T(4,128)S(1)} copy-done((f32[3,3,4096]{2,1,0:T(4,128)S(1)}, f32[3,3,4096]{2,1,0:T(4,128)}, u32[]{:S(2)}) %copy-start.4) | copy-done | bytes 147480
  12.5 4.1 %states.1 = (bf16[16,4224]{1,0:T(8,128)(2,1)S(1)}, bf16[16,4096]{1,0:T(8,128)(2,1)S(1)}) custom-call(s32[3]{0:T(128)S(1)} %pad_add_fusion.scal, bf16[256,4096]{1,0:T(8,128)(2,1)S(1)} %copy-done, bf16[3,4096]{1,0:T(4,128)(2,1)S(1)} %collective-permute-done.edge_ref, f32[3,3,4096]{2,1,0:T(4,128)S(1)} %copy-done.4, f32[8,16]{1,0:T(8,128)S(1)} %copy-done.2), custom_call_target="tpu_custom_call" | custom-call | flops 2000000000 | bytes 2097152 | tf_op jit(solution)/shard_map/states/pallas_call | solution.py:326
  16.5 2.4 %collective-permute-start.1 = (bf16[16,4224]{1,0:T(8,128)(2,1)S(1)}, bf16[16,4224]{1,0:T(8,128)(2,1)S(1)}, u32[]{:S(2)}, u32[]{:S(2)}) collective-permute-start(bf16[16,4224]{1,0:T(8,128)(2,1)S(1)} %get-tuple-element.34.mine_ref), channel_id=1, source_target_pairs={{0,2},{2,0},{4,6},{6,4},{8,10},{10,8},{12,14},{14,12},{1,3},{3,1},... | collective-permute-start | bytes 405512 | tf_op jit(solution)/shard_map/ppermute | solution.py:340
  18.9 3.0 %collective-permute-done.1.other_ref = bf16[16,4224]{1,0:T(8,128)(2,1)S(1)} collective-permute-done((bf16[16,4224]{1,0:T(8,128)(2,1)S(1)}, bf16[16,4224]{1,0:T(8,128)(2,1)S(1)}, u32[]{:S(2)}, u32[]{:S(2)}) %collective-permute-start.1) | collective-permute-done | bytes 135200 | tf_op jit(solution)/shard_map/ppermute | solution.py:340
  22.2 0.7 pair.1
  22.9 4.9 %collective-permute-start.3 = (bf16[32,4224]{1,0:T(8,128)(2,1)S(1)}, bf16[32,4224]{1,0:T(8,128)(2,1)S(1)}, u32[]{:S(2)}, u32[]{:S(2)}) collective-permute-start(bf16[32,4224]{1,0:T(8,128)(2,1)S(1)} %pair.1), channel_id=1, source_target_pairs={{0,4},{4,8},{8,12},{1,5},{5,9},{9,13},{16,20},{20,24},{24,28},{17,... | collective-permute-start | bytes 811016 | tf_op jit(solution)/shard_map/ppermute | solution.py:352
  27.9 4.6 %collective-permute-start.4 = (bf16[16,4224]{1,0:T(8,128)(2,1)S(1)}, bf16[16,4224]{1,0:T(8,128)(2,1)S(1)}, u32[]{:S(2)}, u32[]{:S(2)}) collective-permute-start(bf16[16,4224]{1,0:T(8,128)(2,1)S(1)} %slice.18), channel_id=1, source_target_pairs={{0,8},{4,12},{1,9},{5,13},{16,24},{20,28},{17,25},{21,29}} | collective-permute-start | bytes 405512 | tf_op jit(solution)/shard_map/ppermute | solution.py:354
  32.5 1.3 %collective-permute-start.5 = (bf16[16,4224]{1,0:T(8,128)(2,1)S(1)}, bf16[16,4224]{1,0:T(8,128)(2,1)S(1)}, u32[]{:S(2)}, u32[]{:S(2)}) collective-permute-start(bf16[16,4224]{1,0:T(8,128)(2,1)S(1)} %slice.18), channel_id=1, source_target_pairs={{0,12},{1,13},{16,28},{17,29}} | collective-permute-start | bytes 405512 | tf_op jit(solution)/shard_map/ppermute | solution.py:354
  33.8 1.4 %collective-permute-start.2 = (bf16[131,4096]{1,0:T(8,128)(2,1)S(1)}, bf16[131,4096]{1,0:T(8,128)(2,1)S(1)}, u32[]{:S(2)}, u32[]{:S(2)}) collective-permute-start(bf16[131,4096]{1,0:T(8,128)(2,1)S(1)} %slice.15), channel_id=1, source_target_pairs={{0,2},{2,4},{4,6},{6,8},{8,10},{10,12},{12,14},{1,3},{3,5},{5,7},{... | collective-permute-start | bytes 3219464 | tf_op jit(solution)/shard_map/ppermute | solution.py:301
  35.2 4.3 %tables.1 = (bf16[8,256,256]{2,1,0:T(8,128)(2,1)S(1)}, bf16[8,256,256]{2,1,0:T(8,128)(2,1)S(1)}, bf16[8,144,144]{2,1,0:T(8,128)(2,1)S(1)}, bf16[8,144,144]{2,1,0...) custom-call(s32[3]{0:T(128)S(1)} %pad_add_fusion.scal, ...), custom_call_target="tpu_custom_call" | custom-call | flops 8000000000 | bytes 4194304 | tf_op jit(solution)/shard_map/tables/pallas_call | solution.py:382
  39.8 2.7 %collective-permute-start.6 = (bf16[16,4096]{1,0:T(8,128)(2,1)S(1)}, bf16[16,4096]{1,0:T(8,128)(2,1)S(1)}, u32[]{:S(2)}, u32[]{:S(2)}) collective-permute-start(bf16[16,4096]{1,0:T(8,128)(2,1)S(1)} %get-tuple-element.47), channel_id=1, source_target_pairs={{0,2},{2,4},{4,6},{6,8},{8,10},{10,12},{12,14},{1,3},{3,5},{5,7},{... | collective-permute-start | bytes 393224 | tf_op jit(solution)/shard_map/ppermute | solution.py:301
  42.5 4.6 %collective-permute-start.7 = (bf16[16,4096]{1,0:T(8,128)(2,1)S(1)}, bf16[16,4096]{1,0:T(8,128)(2,1)S(1)}, u32[]{:S(2)}, u32[]{:S(2)}) collective-permute-start(bf16[16,4096]{1,0:T(8,128)(2,1)S(1)} %get-tuple-element.48), channel_id=1, source_target_pairs={{0,2},{4,6},{8,10},{12,14},{1,3},{5,7},{9,11},{13,15},{16,18},{20,... | collective-permute-start | bytes 393224 | tf_op jit(solution)/shard_map/ppermute | solution.py:368
  47.2 6.0 %near.1 = (f32[256,4096]{1,0:T(8,128)S(1)}, f32[256,4096]{1,0:T(8,128)S(1)}) custom-call(s32[3]{0:T(128)S(1)} %pad_add_fusion.scal, bf16[256,4096]{1,0:T(8,128)(2,1)S(1)} %copy-done.1, bf16[3,4096]{1,0:T(4,128)(2,1)S(1)} %collective-permute-done.edge_ref, f32[3,3,4096]{2,1,0:T(4,128)S(1)} %copy-done.5, bf16[8,256,256]{2,1,0:T(8,128)(2,1)S(1)} %get-tuple-element.30.t_ref, ...), custom_call_target="tpu_custom_call" | custom-call | flops 8000000000 | bytes 8388608 | tf_op jit(solution)/shard_map/near/pallas_call | solution.py:393
  53.2 7.4 %collective-permute-done.6.part_ref = bf16[16,4096]{1,0:T(8,128)(2,1)S(1)} collective-permute-done((bf16[16,4096]{1,0:T(8,128)(2,1)S(1)}, bf16[16,4096]{1,0:T(8,128)(2,1)S(1)}, u32[]{:S(2)}, u32[]{:S(2)}) %collective-permute-start.6) | collective-permute-done | bytes 131104 | tf_op jit(solution)/shard_map/ppermute | solution.py:301
  60.6 1.4 %collective-permute-done.7.sent_ref = bf16[16,4096]{1,0:T(8,128)(2,1)S(1)} collective-permute-done((bf16[16,4096]{1,0:T(8,128)(2,1)S(1)}, bf16[16,4096]{1,0:T(8,128)(2,1)S(1)}, u32[]{:S(2)}, u32[]{:S(2)}) %collective-permute-start.7) | collective-permute-done | bytes 131104 | tf_op jit(solution)/shard_map/ppermute | solution.py:368
  62.0 0.8 %place.1 = (bf16[48,4096]{1,0:T(8,128)(2,1)S(1)}, bf16[48,4096]{1,0:T(8,128)(2,1)S(1)}) custom-call(s32[3]{0:T(128)S(1)} %pad_add_fusion.scal, bf16[16,4224]{1,0:T(8,128)(2,1)S(1)} %collective-permute-done.1.other_ref, bf16[16,4096]{1,0:T(8,128)(2,1)S(1)} %collective-permute-done.6.part_ref, bf16[16,4096]{1,0:T(8,128)(2,1)S(1)} %collective-permute-done.7.sent_ref, ...), custom_call_target="tpu_custom_call" | custom-call | tf_op jit(solution)/shard_map/place/pallas_call | solution.py:369
  62.8 5.0 %near_tail.1 = (f32[144,4096]{1,0:T(8,128)S(1)}, f32[144,4096]{1,0:T(8,128)S(1)}) custom-call(s32[3]{0:T(128)S(1)} %pad_add_fusion.scal, bf16[131,4096]{1,0:T(8,128)(2,1)S(1)} %collective-permute-done.2.tail_ref, f32[3,3,4096]{2,1,0:T(4,128)S(1)} %copy-done.5, bf16[8,144,144]{2,1,0:T(8,128)(2,1)S(1)} %get-tuple-element.38.t_ref, ...), custom_call_target="tpu_custom_call" | custom-call | flops 4000000000 | bytes 4194304 | tf_op jit(solution)/shard_map/near_tail/pallas_call | solution.py:407
  67.8 9.7 %final.1 = bf16[256,4096]{1,0:T(8,128)(2,1)} custom-call(s32[3]{0:T(128)S(1)} %pad_add_fusion.scal, f32[256,4096]{1,0:T(8,128)S(1)} %get-tuple-element.32.q_ref, f32[256,4096]{1,0:T(8,128)S(1)} %get-tuple-element.33.z_ref, f32[144,4096]{1,0:T(8,128)S(1)} %get-tuple-element.40.qt_ref, f32[144,4096]{1,0:T(8,128)S(1)} %get-tuple-element.41.zt_ref, ...), custom_call_target="tpu_custom_call" | custom-call | flops 8000000000 | bytes 16777216 | tf_op jit(solution)/shard_map/final/pallas_call | solution.py:420
  (25 shorter events, 0.7 us)
Async XLA Ops:
  1.5 6.4 %collective-permute-start = (bf16[3,4096]{1,0:T(4,128)(2,1)S(1)}, bf16[3,4096]{1,0:T(4,128)(2,1)S(1)}, u32[]{:S(2)}, u32[]{:S(2)}) collective-permute-start(bf16[3,4096]{1,0:T(4,128)(2,1)S(1)} %concatenate.3), channel_id=1, source_target_pairs={{0,2},{2,4},{4,6},{6,8},{8,10},{10,12},{12,14},{1,3},{3,5},{5,7},{... | collective-permute-start | bytes 73736 | tf_op jit(solution)/shard_map/ppermute | solution.py:301
  9.2 1.6 %copy-start = (bf16[256,4096]{1,0:T(8,128)(2,1)S(1)}, bf16[256,4096]{1,0:T(8,128)(2,1)}, u32[]{:S(2)}) copy-start(bf16[256,4096]{1,0:T(8,128)(2,1)} %x_ref.3) | copy-start | bytes 6291460
  10.8 0.7 copy-start.2
  11.5 0.9 %copy-start.4 = (f32[3,3,4096]{2,1,0:T(4,128)S(1)}, f32[3,3,4096]{2,1,0:T(4,128)}, u32[]{:S(2)}) copy-start(f32[3,3,4096]{2,1,0:T(4,128)} %w_ref.6) | copy-start | bytes 442372
  12.5 6.5 %copy-start.8 = (bf16[8,128]{1,0:T(8,128)(2,1)S(1)}, bf16[8,128]{1,0:T(8,128)(2,1)}, u32[]{:S(2)}) copy-start(bf16[8,128]{1,0:T(8,128)(2,1)} %param.13) | copy-start | bytes 6148
  16.5 18.7 %copy-start.7 = (f32[8,16]{1,0:T(8,128)S(1)}, f32[8,16]{1,0:T(8,128)}, u32[]{:S(2)}) copy-start(f32[8,16]{1,0:T(8,128)} %res_ref.1) | copy-start | bytes 1540
  16.5 5.4 %collective-permute-start.1 = (bf16[16,4224]{1,0:T(8,128)(2,1)S(1)}, bf16[16,4224]{1,0:T(8,128)(2,1)S(1)}, u32[]{:S(2)}, u32[]{:S(2)}) collective-permute-start(bf16[16,4224]{1,0:T(8,128)(2,1)S(1)} %get-tuple-element.34.mine_ref), channel_id=1, source_target_pairs={{0,2},{2,0},{4,6},{6,4},{8,10},{10,8},{12,14},{14,12},{1,3},{3,1},... | collective-permute-start | bytes 405512 | tf_op jit(solution)/shard_map/ppermute | solution.py:340
  22.9 16.6 %collective-permute-start.3 = (bf16[32,4224]{1,0:T(8,128)(2,1)S(1)}, bf16[32,4224]{1,0:T(8,128)(2,1)S(1)}, u32[]{:S(2)}, u32[]{:S(2)}) collective-permute-start(bf16[32,4224]{1,0:T(8,128)(2,1)S(1)} %pair.1), channel_id=1, source_target_pairs={{0,4},{4,8},{8,12},{1,5},{5,9},{9,13},{16,20},{20,24},{24,28},{17,... | collective-permute-start | bytes 811016 | tf_op jit(solution)/shard_map/ppermute | solution.py:352
  27.9 19.2 %copy-start.1 = (bf16[256,4096]{1,0:T(8,128)(2,1)S(1)}, bf16[256,4096]{1,0:T(8,128)(2,1)}, u32[]{:S(2)}) copy-start(bf16[256,4096]{1,0:T(8,128)(2,1)} %x_ref.3) | copy-start | bytes 6291460
  27.9 19.2 %copy-start.5 = (f32[3,3,4096]{2,1,0:T(4,128)S(1)}, f32[3,3,4096]{2,1,0:T(4,128)}, u32[]{:S(2)}) copy-start(f32[3,3,4096]{2,1,0:T(4,128)} %w_ref.6) | copy-start | bytes 442372
  27.9 11.6 %collective-permute-start.4 = (bf16[16,4224]{1,0:T(8,128)(2,1)S(1)}, bf16[16,4224]{1,0:T(8,128)(2,1)S(1)}, u32[]{:S(2)}, u32[]{:S(2)}) collective-permute-start(bf16[16,4224]{1,0:T(8,128)(2,1)S(1)} %slice.18), channel_id=1, source_target_pairs={{0,8},{4,12},{1,9},{5,13},{16,24},{20,28},{17,25},{21,29}} | collective-permute-start | bytes 405512 | tf_op jit(solution)/shard_map/ppermute | solution.py:354
  32.5 7.0 %collective-permute-start.5 = (bf16[16,4224]{1,0:T(8,128)(2,1)S(1)}, bf16[16,4224]{1,0:T(8,128)(2,1)S(1)}, u32[]{:S(2)}, u32[]{:S(2)}) collective-permute-start(bf16[16,4224]{1,0:T(8,128)(2,1)S(1)} %slice.18), channel_id=1, source_target_pairs={{0,12},{1,13},{16,28},{17,29}} | collective-permute-start | bytes 405512 | tf_op jit(solution)/shard_map/ppermute | solution.py:354
  33.8 28.9 %collective-permute-start.2 = (bf16[131,4096]{1,0:T(8,128)(2,1)S(1)}, bf16[131,4096]{1,0:T(8,128)(2,1)S(1)}, u32[]{:S(2)}, u32[]{:S(2)}) collective-permute-start(bf16[131,4096]{1,0:T(8,128)(2,1)S(1)} %slice.15), channel_id=1, source_target_pairs={{0,2},{2,4},{4,6},{6,8},{8,10},{10,12},{12,14},{1,3},{3,5},{5,7},{... | collective-permute-start | bytes 3219464 | tf_op jit(solution)/shard_map/ppermute | solution.py:301
  39.8 20.8 %collective-permute-start.6 = (bf16[16,4096]{1,0:T(8,128)(2,1)S(1)}, bf16[16,4096]{1,0:T(8,128)(2,1)S(1)}, u32[]{:S(2)}, u32[]{:S(2)}) collective-permute-start(bf16[16,4096]{1,0:T(8,128)(2,1)S(1)} %get-tuple-element.47), channel_id=1, source_target_pairs={{0,2},{2,4},{4,6},{6,8},{8,10},{10,12},{12,14},{1,3},{3,5},{5,7},{... | collective-permute-start | bytes 393224 | tf_op jit(solution)/shard_map/ppermute | solution.py:301
  42.5 19.5 %collective-permute-start.7 = (bf16[16,4096]{1,0:T(8,128)(2,1)S(1)}, bf16[16,4096]{1,0:T(8,128)(2,1)S(1)}, u32[]{:S(2)}, u32[]{:S(2)}) collective-permute-start(bf16[16,4096]{1,0:T(8,128)(2,1)S(1)} %get-tuple-element.48), channel_id=1, source_target_pairs={{0,2},{4,6},{8,10},{12,14},{1,3},{5,7},{9,11},{13,15},{16,18},{20,... | collective-permute-start | bytes 393224 | tf_op jit(solution)/shard_map/ppermute | solution.py:368
  47.1 14.8 %copy-start.3 = (f32[8,16]{1,0:T(8,128)S(1)}, f32[8,16]{1,0:T(8,128)}, u32[]{:S(2)}) copy-start(f32[8,16]{1,0:T(8,128)} %dec_ref.9) | copy-start | bytes 1540
  62.8 5.0 %copy-start.6 = (f32[3,3,4096]{2,1,0:T(4,128)S(1)}, f32[3,3,4096]{2,1,0:T(4,128)}, u32[]{:S(2)}) copy-start(f32[3,3,4096]{2,1,0:T(4,128)} %w_ref.7) | copy-start | bytes 442372

commit v3 on v2

v3 whole, which is shorter than its diff:
```python
import functools
import math

import jax
import jax.numpy as jnp
from jax import lax
from jax.experimental import pallas as pl
from jax.experimental.pallas import tpu as pltpu
from jax.sharding import PartitionSpec as P

F32 = jnp.float32
BF = jnp.bfloat16
WIN = 144
LANE = 128
CHUNK = 32
SMEM = pltpu.SMEM


def dot(a, b):
    return lax.dot_general(a, b, (((1,), (0,)), ((), ())), preferred_element_type=F32)


def iota(shape, dim):
    return lax.broadcasted_iota(jnp.int32, shape, dim)


def column(row):
    n = row.shape[1]
    return jnp.sum(
        jnp.where(iota((n, n), 0) == iota((n, n), 1), row, 0.0), axis=1, keepdims=True
    )


def one(cond):
    return jnp.where(cond, 1.0, 0.0).astype(BF)


def weights_of(w_ref, cols):
    return [[w_ref[b, o : o + 1, cols] for o in range(3)] for b in range(3)]


def combine(w, taps):
    return w[0] * taps[0] + w[1] * taps[1] + w[2] * taps[2]


def taps_at(ref, mask_ref, at, cols):
    rows = ref[at.start : at.stop + 8, cols]
    return (
        rows[8:],
        pltpu.roll(rows, 1, 0)[8:] * mask_ref[0, at, :],
        pltpu.roll(rows, 2, 0)[8:] * mask_ref[1, at, :],
    )


def chunks(first, last, rows=CHUNK):
    return [slice(r, min(r + rows, last)) for r in range(first, last, rows)]


def tiles(lanes):
    return [slice(c, c + LANE) for c in range(0, lanes, LANE)]


def spans(count, lanes):
    return [(i, slice(i * lanes, (i + 1) * lanes)) for i in range(count)]


def write_masks(ref, offset, own, prior, length):
    rows = ref.shape[1]
    t = iota((rows, LANE), 0) - offset
    before = jnp.where(prior < length, prior, -length) - length
    one_back = (t != own) & (t != before)
    two_back = one_back & (t - 1 != own) & (t - 1 != before)
    ref[0] = jnp.where(one_back, 1.0, 0.0)
    ref[1] = jnp.where(two_back, 1.0, 0.0)


def split(v):
    hi = v.astype(BF)
    return hi, (v - hi.astype(F32)).astype(BF)


def states_kernel(
    cut, modes, lanes, scal, x_ref, edge_ref, w_ref, dec_ref, out_ref, part_ref, q_ref, u_ref,
    mask_ref, x_scr,
):
    length, width = x_ref.shape
    own, prior = scal[0], scal[1]
    write_masks(mask_ref, 0, own, prior, length)
    flag = jnp.full((modes, LANE), own, jnp.int32).astype(F32)
    out_ref[:, width:] = flag.astype(BF)

    p = iota((modes, length), 1)
    lag = (length - 1 - p).astype(F32)
    lag_cut = jnp.maximum(cut - 1 - p, 0).astype(F32)
    reach = (p >= own) | (own >= length)
    reach_cut = (p < cut) & ((p >= own) | (own >= cut))
    for i, cols in spans(width // lanes, lanes):
        scr = x_scr.at[i % x_scr.shape[0]]
        scr[6:8, :] = edge_ref[:, cols].astype(F32)[:2]
        scr[8 : 8 + length, :] = x_ref[:, cols].astype(F32)
        for tile in tiles(lanes):
            here = slice(cols.start + tile.start, cols.start + tile.stop)
            w = weights_of(w_ref, here)
            for at in chunks(0, length):
                taps = taps_at(scr, mask_ref, at, tile)
                u_ref[at, here] = (combine(w[1], taps) * combine(w[2], taps)).astype(BF)
                q_ref[at, here] = combine(w[0], taps)
        dec = column(dec_ref[i : i + 1, :])
        full = jnp.where(reach, jnp.exp(-dec * lag), 0.0)
        part = jnp.where(reach_cut, jnp.exp(-dec * lag_cut), 0.0)
        hi, lo = split(jnp.concatenate([full, part], 0))
        both = dot(jnp.concatenate([hi, lo], 0), u_ref[:, cols])
        state = both[: 2 * modes] + both[2 * modes :]
        out_ref[:, cols] = state[:modes].astype(BF)
        part_ref[:, cols] = state[modes:].astype(BF)


def pair_kernel(modes, length, scal, mine_ref, other_ref, dec_ref, out_ref):
    groups = dec_ref.shape[0]
    width = mine_ref.shape[1] - LANE
    lanes = width // groups
    even = scal[2] == 0
    end = slice(width, width + LANE)

    def pick(cols):
        a, b = mine_ref[:, cols].astype(F32), other_ref[:, cols].astype(F32)
        return jnp.where(even, a, b), jnp.where(even, b, a)

    top, low = slice(0, modes), slice(modes, 2 * modes)
    f_bound, s_bound = pick(end)
    free_f = jnp.where(f_bound >= length, 1.0, 0.0)
    free_s = jnp.where(s_bound >= length, 1.0, 0.0)
    out_ref[top, end] = (free_f * free_s).astype(BF)
    out_ref[low, end] = free_f.astype(BF)
    for g in range(groups):
        cols = slice(g * lanes, (g + 1) * lanes)
        dec = column(dec_ref[g : g + 1, :])
        first, second = pick(cols)
        out_ref[top, cols] = (second + jnp.exp(-dec * length) * free_s[:, :1] * first).astype(BF)
        out_ref[low, cols] = first.astype(BF)


def carry_kernel(modes, length, near_ref, dec_ref, *refs):
    far, (send_ref, own_ref, late_ref) = refs[:-3], refs[-3:]
    groups = dec_ref.shape[0]
    width = own_ref.shape[1]
    lanes = width // groups
    top, low = slice(0, modes), slice(modes, 2 * modes)
    near_free = near_ref[top, width : width + LANE].astype(F32)[:, :1]
    late_free = near_ref[low, width : width + LANE].astype(F32)[:, :1]
    far_free = [f[:, width : width + LANE].astype(F32)[:, :1] for f in far]
    for g in range(groups):
        cols = slice(g * lanes, (g + 1) * lanes)
        dec = column(dec_ref[g : g + 1, :])
        once = jnp.exp(-dec * length)
        pair = jnp.exp(-dec * (2 * length))
        behind = jnp.zeros((modes, lanes), F32)
        for f, free in zip(far[::-1], far_free[::-1]):
            behind = f[:, cols].astype(F32) + pair * free * behind
        whole = near_ref[top, cols].astype(F32) + pair * near_free * behind
        send_ref[:, cols] = whole.astype(BF)
        own_ref[:, cols] = whole
        late_ref[:, cols] = near_ref[low, cols].astype(F32) + once * late_free * behind


def place_kernel(
    cut, modes, length, scal, other_ref, part_ref, sent_ref, even_own, even_late, dec_ref,
    own_ref, win_ref,
):
    groups = dec_ref.shape[0]
    lanes = own_ref.shape[1] // groups
    even = scal[2] == 0
    prior = scal[1]
    pass_own = jnp.where(prior >= length, 1.0, 0.0)
    pass_cut = jnp.where(prior >= cut, 1.0, 0.0)
    for g in range(groups):
        cols = slice(g * lanes, (g + 1) * lanes)
        dec = column(dec_ref[g : g + 1, :])
        sent = sent_ref[:, cols].astype(F32)
        odd_own = other_ref[:, cols].astype(F32) + jnp.exp(-dec * length) * pass_own * sent
        before = jnp.where(even, even_late[:, cols], sent)
        own = jnp.where(even, even_own[:, cols], odd_own)
        win = part_ref[: dec_ref.shape[1], cols].astype(F32) + jnp.exp(-dec * cut) * pass_cut * before
        for ref, v in ((own_ref, own), (win_ref, win)):
            hi, lo = split(v)
            ref[:, cols] = jnp.concatenate([hi, lo, hi], 0)


def tables_kernel(cut, modes, length, scal, dec_ref, res_ref, mr_ref, *outs):
    t_own, t_win, r_own, r_win, b_win, b_own = outs
    g = pl.program_id(0)
    own, prior = scal[0], scal[1]
    wide = 2 * length
    base = length - WIN
    dec_row = dec_ref[pl.ds(g, 1), :]
    weight_row = res_ref[pl.ds(g, 1), :] * jnp.sqrt(
        jnp.maximum(1.0 - jnp.exp(-2.0 * dec_row), 0.0)
    ) / math.sqrt(modes)
    small = 2.0 * dec_row
    series = small * (1.0 - small * (0.5 - small * (1.0 / 6 - small * (1.0 / 24))))
    weight_row = jnp.where(
        small < 0.05,
        res_ref[pl.ds(g, 1), :] * jnp.sqrt(series) / math.sqrt(modes),
        weight_row,
    )
    dec, weight = column(dec_row), column(weight_row)
    back = iota((modes, wide), 1)
    back = jnp.where(back == 0, 0, wide - back).astype(F32)
    taps = jnp.sum(weight * jnp.exp(-dec * back), axis=0, keepdims=True)
    full = pltpu.roll(jnp.broadcast_to(taps, (length, wide)), 0, 1, stride=1, stride_axis=0)
    t, p = iota((length, length), 0), iota((length, length), 1)
    seen = (p <= t) & ((p >= own) == (t >= own))
    t_own[:length, :], t_own[length:, :] = split(jnp.where(seen, full[:, :length], 0.0))
    tw, pw = iota((WIN, WIN), 0) + base, iota((WIN, WIN), 1) + base
    seen = (pw <= tw) & (pw >= cut) & ((pw >= prior) == (tw >= prior))
    t_win[:WIN, :], t_win[WIN:, :] = split(jnp.where(seen, full[:WIN, :WIN], 0.0))

    tl = iota((modes, length), 1)
    rise = jnp.where(tl < own, weight * jnp.exp(-dec * (tl + 1).astype(F32)), 0.0)
    wl = tl + base
    lag = jnp.maximum(wl - cut + 1, 0)
    fits = (wl >= cut) & ((prior < cut) | (prior > wl))
    rise_w = jnp.where(fits, weight * jnp.exp(-dec * lag.astype(F32)), 0.0)
    for ref, v, rows in ((r_own, rise, length), (r_win, rise_w, WIN)):
        hi = v.astype(BF).astype(F32)
        stack = jnp.concatenate([hi, hi, v - hi, jnp.zeros((LANE - 3 * modes, length), F32)], 0)
        ref[...] = jnp.transpose(stack)[:rows, : 3 * modes].astype(BF)

    count = mr_ref.shape[1]
    o, n = iota((count, wide), 0), iota((count, wide), 1)
    back = dot(mr_ref[...], one(((n == 0) & (o == 0)) | ((n > 0) & (wide - n == o))))
    band = pltpu.roll(
        jnp.broadcast_to(back, (WIN + length, wide)), 0, 1, stride=1, stride_axis=0
    )
    seen = (p <= t) & ((p >= own) == (t >= own))
    b_own[...] = jnp.where(seen, band[:length, :length], 0.0).astype(BF)
    tb, pb = iota((length, WIN), 0), iota((length, WIN), 1) + base
    seen = (tb < own) & ((prior >= length) | (pb >= prior))
    b_win[...] = jnp.where(seen, band[WIN : WIN + length, :WIN], 0.0).astype(BF)


def tail_kernel(
    modes, length, lanes, scal, tail_ref, w_ref, q_ref, u_ref, mask_ref, x_scr
):
    rows = tail_ref.shape[0] - modes

    write_masks(mask_ref, WIN, scal[0], scal[1], length)
    x_scr[:, : 8 + WIN - rows, :] = jnp.zeros(
        (x_scr.shape[0], 8 + WIN - rows, x_scr.shape[2]), F32
    )

    for i, cols in spans(tail_ref.shape[1] // lanes, lanes):
        scr = x_scr.at[i]
        scr[8 + WIN - rows : 8 + WIN, :] = tail_ref[modes:, cols].astype(F32)
        for tile in tiles(lanes):
            here = slice(cols.start + tile.start, cols.start + tile.stop)
            w = weights_of(w_ref, here)
            for at in chunks(0, WIN):
                taps = taps_at(scr, mask_ref, at, tile)
                u_ref[at, here] = (combine(w[1], taps) * combine(w[2], taps)).astype(BF)
                q_ref[at, here] = combine(w[0], taps)


def final_kernel(
    lanes, scal, q_ref, u_ref, qt_ref, ut_ref, t_ref, tt_ref, r_ref, rt_ref, st_ref, stt_ref,
    w_ref, bt_ref, b_ref, out_ref, mask_ref, y_scr, w_scr, q_scr, z_scr, o_scr, sems,
):
    length = q_ref.shape[0]

    write_masks(mask_ref, WIN, scal[0], scal[1], length)
    y_scr[:, :8, :] = jnp.zeros((y_scr.shape[0], 8, y_scr.shape[2]), F32)
    copies = []
    for i, cols in spans(q_ref.shape[1] // lanes, lanes):
        k = i % y_scr.shape[0]
        ys, ws, qs, zs = y_scr.at[k], w_scr.at[k], q_scr.at[k], z_scr.at[k]
        near = dot(tt_ref[i], ut_ref[:, cols])
        zs[:WIN, :] = near[:WIN] + near[WIN:] + dot(rt_ref[i], stt_ref[:, cols])
        near = dot(t_ref[i], u_ref[:, cols])
        zs[WIN:, :] = near[:length] + near[length:] + dot(r_ref[i], st_ref[:, cols])
        for tile in tiles(lanes):
            here = slice(cols.start + tile.start, cols.start + tile.stop)
            for at in chunks(0, WIN) + chunks(WIN, WIN + length):
                if at.start < WIN:
                    q = qt_ref[at, here]
                else:
                    q = q_ref[at.start - WIN : at.stop - WIN, here]
                y = (q * zs[at, tile]).astype(BF).astype(F32)
                ys[8 + at.start : 8 + at.stop, tile] = y
            w = weights_of(w_ref, here)
            for at in chunks(0, WIN) + chunks(WIN, WIN + length):
                taps = taps_at(ys, mask_ref, at, tile)
                ws[at, tile] = (combine(w[1], taps) * combine(w[2], taps)).astype(BF)
                if at.start >= WIN:
                    qs[at.start - WIN : at.stop - WIN, tile] = combine(w[0], taps)
        z = dot(bt_ref[i], ws[:WIN, :]) + dot(b_ref[i], ws[WIN:, :])
        o_scr[i] = (qs[...] * z).astype(BF)
        copies.append(pltpu.make_async_copy(o_scr.at[i], out_ref.at[:, cols], sems.at[i]))
        copies[-1].start()
    for copy in copies:
        copy.wait()


def per_device(inputs, bounds, feat_first, li_decay, li_residue, feat_second, mr_filter):
    length, channels = inputs.shape
    groups, modes = li_decay.shape
    lanes = channels // groups
    filter_len = mr_filter.shape[1]
    rows = filter_len + 3
    cut = length - rows + 2
    size = lax.axis_size("seq")
    place = lax.axis_index("seq")

    def behind(array, by):
        return lax.ppermute(array, "seq", [(i, i + by) for i in range(size - by)])

    own_row = jnp.broadcast_to(bounds.astype(BF)[:, None], (1, channels))
    edge = behind(jnp.concatenate([inputs[length - 2 :], own_row], 0), 1)
    prior = jnp.where(place == 0, length, edge[2, 0].astype(F32).astype(jnp.int32))
    scal = jnp.stack([bounds[0], prior, (place % 2).astype(jnp.int32)])

    sm = pl.BlockSpec(memory_space=SMEM)
    whole = pl.BlockSpec(memory_space=pltpu.VMEM)
    params = pltpu.CompilerParams(vmem_limit_bytes=24 * 1024 * 1024)
    count = 2 if groups % 2 == 0 else 1
    steps, wide = groups // count, lanes * count

    def block(*shape):
        return pl.BlockSpec(shape, lambda g: (0,) * (len(shape) - 1) + (g,))

    def table(*shape):
        return pl.BlockSpec((count,) + shape, lambda g: (g, 0, 0))

    def single(*shape):
        return pl.BlockSpec((None,) + shape, lambda g: (g, 0, 0))

    def fixed(*shape):
        return pl.BlockSpec(shape, lambda g: (0,) * len(shape))

    mine, part, q_own, u_own = pl.pallas_call(
        functools.partial(states_kernel, cut, modes, lanes),
        in_specs=[sm] + [whole] * 4,
        out_specs=[whole] * 4,
        out_shape=[
            jax.ShapeDtypeStruct((modes, channels + LANE), BF),
            jax.ShapeDtypeStruct((modes, channels), BF),
            jax.ShapeDtypeStruct((length, channels), F32),
            jax.ShapeDtypeStruct((length, channels), BF),
        ],
        scratch_shapes=[
            pltpu.VMEM((2, length, LANE), F32), pltpu.VMEM((count, 8 + length, lanes), F32),
        ],
        compiler_params=params,
        cost_estimate=pl.CostEstimate(flops=10**8, bytes_accessed=2**16, transcendentals=0),
        name="states",
    )(scal, inputs, edge, feat_first, li_decay)
    other = lax.ppermute(mine, "seq", [(i, i ^ 1) for i in range(size)])
    inputs_late, part, other = lax.optimization_barrier((inputs, part, other))
    message = jnp.concatenate([part, inputs_late[length - rows :]], 0)
    message, other = lax.optimization_barrier((message, other))
    tail = behind(message, 1)
    pair = pl.pallas_call(
        functools.partial(pair_kernel, modes, length),
        in_specs=[sm] + [whole] * 3,
        out_specs=whole,
        out_shape=jax.ShapeDtypeStruct((2 * modes, channels + LANE), BF),
        compiler_params=params,
        name="pair",
    )(scal, mine, other, li_decay)
    near = lax.ppermute(pair, "seq", [(i, i + 2) for i in range(0, size - 2, 2)])
    far = [
        lax.ppermute(pair[:modes], "seq", [(i, i + by) for i in range(0, size - by, 2)])
        for by in range(4, size, 2)
    ]
    state_shape = jax.ShapeDtypeStruct((modes, channels), F32)
    send, even_own, even_late = pl.pallas_call(
        functools.partial(carry_kernel, modes, length),
        in_specs=[whole] * (2 + len(far)),
        out_specs=[whole] * 3,
        out_shape=[jax.ShapeDtypeStruct((modes, channels), BF), state_shape, state_shape],
        compiler_params=params,
        name="carry",
    )(near, li_decay, *far)
    sent = lax.ppermute(send, "seq", [(i, i + 1) for i in range(0, size, 2)])
    own_state, win_state = pl.pallas_call(
        functools.partial(place_kernel, cut, modes, length),
        in_specs=[sm] + [whole] * 6,
        out_specs=[whole] * 2,
        out_shape=[jax.ShapeDtypeStruct((3 * modes, channels), BF)] * 2,
        compiler_params=params,
        name="place",
    )(scal, other, tail, sent, even_own, even_late, li_decay)

    shapes = [
        (2 * length, length), (2 * WIN, WIN), (length, 3 * modes), (WIN, 3 * modes),
        (length, WIN), (length, length),
    ]
    t_own, t_win, r_own, r_win, b_win, b_own = pl.pallas_call(
        functools.partial(tables_kernel, cut, modes, length),
        grid=(groups,),
        in_specs=[sm, fixed(groups, modes), fixed(groups, modes), single(1, filter_len)],
        out_specs=[single(*s) for s in shapes],
        out_shape=[jax.ShapeDtypeStruct((groups,) + s, BF) for s in shapes],
        compiler_params=params,
        cost_estimate=pl.CostEstimate(flops=10**8, bytes_accessed=2**16, transcendentals=0),
        name="tables",
    )(scal, li_decay, li_residue, mr_filter.reshape(groups, 1, filter_len))

    q_win, u_win = pl.pallas_call(
        functools.partial(tail_kernel, modes, length, lanes),
        in_specs=[sm, whole, whole],
        out_specs=[whole] * 2,
        out_shape=[
            jax.ShapeDtypeStruct((WIN, channels), F32),
            jax.ShapeDtypeStruct((WIN, channels), BF),
        ],
        scratch_shapes=[
            pltpu.VMEM((2, WIN, LANE), F32), pltpu.VMEM((groups, 8 + WIN, lanes), F32),
        ],
        compiler_params=params,
        cost_estimate=pl.CostEstimate(flops=10**8, bytes_accessed=2**16, transcendentals=0),
        name="tail",
    )(scal, tail, feat_first)
    full = WIN + length
    return pl.pallas_call(
        functools.partial(final_kernel, lanes),
        in_specs=[sm] + [whole] * 13,
        out_specs=pl.BlockSpec(memory_space=pl.ANY),
        out_shape=jax.ShapeDtypeStruct((length, channels), BF),
        scratch_shapes=[
            pltpu.VMEM((2, full, LANE), F32), pltpu.VMEM((count, 8 + full, lanes), F32),
            pltpu.VMEM((count, full, lanes), BF), pltpu.VMEM((count, length, lanes), F32),
            pltpu.VMEM((count, full, lanes), F32), pltpu.VMEM((groups, length, lanes), BF),
            pltpu.SemaphoreType.DMA((groups,)),
        ],
        compiler_params=params,
        cost_estimate=pl.CostEstimate(flops=10**8, bytes_accessed=2**16, transcendentals=0),
        name="final",
    )(
        scal, q_own, u_own, q_win, u_win, t_own, t_win, r_own, r_win, own_state, win_state,
        feat_second, b_win, b_own,
    )


def solution(mesh):
    in_specs = (
        P(("groups", "seq"), "chan"),
        P(("groups", "seq")),
        P(None, None, "chan"),
        P("chan", None),
        P("chan", None),
        P(None, None, "chan"),
        P("chan", None),
    )
    out_specs = P(("groups", "seq"), "chan")
    return jax.shard_map(
        per_device, mesh=mesh, in_specs=in_specs, out_specs=out_specs, check_vma=False
    )
```

time: 77.9 us -> 66.8 us (0.86)
  Pallas kernels: 30.9 us -> 23.5 us
  starting transfers between devices: 26.7 us -> 21.4 us
  waiting for transfers between devices: 13.3 us -> 14.6 us
    pallas_call x4 -> x3, Pallas kernels: 24.8 us -> 17.4 us  [the longest x1 10.1 us: per_device(): pl.pallas_call(functools.partial(final_kernel, lanes), in_specs=[sm] + [w...]
    ppermute x2, waiting for transfers between devices: 0.01 us -> 4.22 us  [per_device(): lax.ppermute(pair[:modes], 'seq', [(i, i + by) for i in range(0, size - b...]
    ppermute x1, starting transfers between devices: 4.61 us -> 1.48 us  [per_device(): sent = lax.ppermute(send, 'seq', [(i, i + 1) for i in range(0, size, 2)])]
    ppermute x3 -> x2, waiting for transfers between devices: 8.94 us -> 7.37 us  [behind(): return lax.ppermute(array, 'seq', [(i, i + by) for i in range(size - by)])]
    ppermute x1, starting transfers between devices: 4.93 us -> 3.42 us  [per_device(): lax.ppermute(pair, 'seq', [(i, i + 2) for i in range(0, size - 2, 2)])]
    ppermute x1, waiting for transfers between devices: 1.4 us -> 0.01 us  [per_device(): sent = lax.ppermute(send, 'seq', [(i, i + 1) for i in range(0, size, 2)])]
    ppermute x3 -> x2, starting transfers between devices: 8.88 us -> 8.85 us  [behind(): return lax.ppermute(array, 'seq', [(i, i + by) for i in range(size - by)])]
    unnamed x18 -> x14, local copies, waits for them, and re-layouts: 3.24 us -> 3.23 us
  transfers between devices with their start and end apart: 8 -> 7, of which waited for: 4 -> 5; matrix products, arithmetic and copies ran while one was open for 0% -> 0% of each run, Pallas kernels for 15% -> 12%
where the time goes in v3:
time: 66.8 us; the launch traced here: 66.4 us
  Pallas kernels  23.5 us (35%)
  starting transfers between devices  21.4 us (32%)
  waiting for transfers between devices  14.6 us (22%)
  local copies, waits for them, and re-layouts  4.99 us (7%)
  between operations  1.74 us (3%)
    pallas_call x1, Pallas kernels, per_device(): pl.pallas_call(functools.partial(final_kernel, lanes), in_specs=[sm] + [w...  10.1 us
    ppermute x2, starting transfers between devices, behind(): return lax.ppermute(array, 'seq', [(i, i + by) for i in range(size - by)])  8.85 us
    ppermute x2, waiting for transfers between devices, behind(): return lax.ppermute(array, 'seq', [(i, i + by) for i in range(size - by)])  7.37 us
    ppermute x2, starting transfers between devices, per_device(): lax.ppermute(pair[:modes], 'seq', [(i, i + by) for i in range(0, size - b...  5.29 us
    pallas_call x1, Pallas kernels, per_device(): pl.pallas_call(functools.partial(states_kernel, cut, modes, lanes), in_sp...  4.76 us
    pallas_call x1, Pallas kernels, per_device(): pl.pallas_call(functools.partial(tables_kernel, cut, modes, length), grid...  4.28 us
    ppermute x2, waiting for transfers between devices, per_device(): lax.ppermute(pair[:modes], 'seq', [(i, i + by) for i in range(0, size - b...  4.22 us
    ppermute x1, starting transfers between devices, per_device(): lax.ppermute(pair, 'seq', [(i, i + 2) for i in range(0, size - 2, 2)])  3.42 us
  transfers between devices with their start and end apart: 7, of which 5 were waited for; matrix products, arithmetic and copies ran while one was open for 0% of the time, Pallas kernels for 12%

profile of v3, /device:TPU:0, one launch (start us, length us, event | category | flops | bytes accessed | tf_op | source)
XLA Modules:
  0.0 66.4 jit_solution(1315845024320615092)
XLA Ops:
  0.7 0.9 %slice.13 = bf16[2,4096]{1,0:T(2,128)(2,1)S(1)} slice(bf16[256,4096]{1,0:T(8,128)(2,1)} %x_ref.1), slice={[254:256], [0:4096]} | slice | bytes 32768 | tf_op jit(solution)/shard_map/slice | solution.py:317
  1.5 4.8 %collective-permute-start = (bf16[3,4096]{1,0:T(4,128)(2,1)S(1)}, bf16[3,4096]{1,0:T(4,128)(2,1)S(1)}, u32[]{:S(2)}, u32[]{:S(2)}) collective-permute-start(bf16[3,4096]{1,0:T(4,128)(2,1)S(1)} %concatenate.6), channel_id=1, source_target_pairs={{0,2},{2,4},{4,6},{6,8},{8,10},{10,12},{12,14},{1,3},{3,5},{5,7},{... | collective-permute-start | bytes 73736 | tf_op jit(solution)/shard_map/ppermute | solution.py:314
  6.4 1.6 %collective-permute-done.edge_ref = bf16[3,4096]{1,0:T(4,128)(2,1)S(1)} collective-permute-done((bf16[3,4096]{1,0:T(4,128)(2,1)S(1)}, bf16[3,4096]{1,0:T(4,128)(2,1)S(1)}, u32[]{:S(2)}, u32[]{:S(2)}) %collective-permute-start) | collective-permute-done | bytes 24608 | tf_op jit(solution)/shard_map/ppermute | solution.py:314
  8.0 0.6 slice.17
  9.4 1.6 %copy-done = bf16[256,4096]{1,0:T(8,128)(2,1)S(1)} copy-done((bf16[256,4096]{1,0:T(8,128)(2,1)S(1)}, bf16[256,4096]{1,0:T(8,128)(2,1)}, u32[]{:S(2)}) %copy-start) | copy-done | bytes 2097176
  11.0 0.9 %copy-done.1 = f32[3,3,4096]{2,1,0:T(4,128)S(1)} copy-done((f32[3,3,4096]{2,1,0:T(4,128)S(1)}, f32[3,3,4096]{2,1,0:T(4,128)}, u32[]{:S(2)}) %copy-start.1) | copy-done | bytes 147480
  11.9 0.7 %copy-done.3 = f32[8,16]{1,0:T(8,128)S(1)} copy-done((f32[8,16]{1,0:T(8,128)S(1)}, f32[8,16]{1,0:T(8,128)}, u32[]{:S(2)}) %copy-start.3) | copy-done | bytes 536
  12.6 4.8 %states.1 = (bf16[16,4224]{1,0:T(8,128)(2,1)S(1)}, bf16[16,4096]{1,0:T(8,128)(2,1)S(1)}, f32[256,4096]{1,0:T(8,128)S(1)}, bf16[256,4096]{1,0:T(8,128)(2,1)S(1)}) custom-call(s32[3]{0:T(128)S(1)} %pad_add_fusion.scal, bf16[256,4096]{1,0:T(8,128)(2,1)S(1)} %copy-done, bf16[3,4096]{1,0:T(4,128)(2,1)S(1)} %collective-permute-done.edge_ref, ...), custom_call_target="tpu_custom_call" | custom-call | flops 100000000 | bytes 65536 | tf_op jit(solution)/shard_map/states/pallas_call | solution.py:339
  17.3 2.4 %collective-permute-start.1 = (bf16[16,4224]{1,0:T(8,128)(2,1)S(1)}, bf16[16,4224]{1,0:T(8,128)(2,1)S(1)}, u32[]{:S(2)}, u32[]{:S(2)}) collective-permute-start(bf16[16,4224]{1,0:T(8,128)(2,1)S(1)} %get-tuple-element.30.mine_ref), channel_id=1, source_target_pairs={{0,2},{2,0},{4,6},{6,4},{8,10},{10,8},{12,14},{14,12},{1,3},{3,1},... | collective-permute-start | bytes 405512 | tf_op jit(solution)/shard_map/ppermute | solution.py:356
  19.7 3.0 %collective-permute-done.1.other_ref = bf16[16,4224]{1,0:T(8,128)(2,1)S(1)} collective-permute-done((bf16[16,4224]{1,0:T(8,128)(2,1)S(1)}, bf16[16,4224]{1,0:T(8,128)(2,1)S(1)}, u32[]{:S(2)}, u32[]{:S(2)}) %collective-permute-start.1) | collective-permute-done | bytes 135200 | tf_op jit(solution)/shard_map/ppermute | solution.py:356
  23.1 4.0 %collective-permute-start.2 = (bf16[147,4096]{1,0:T(8,128)(2,1)S(1)}, bf16[147,4096]{1,0:T(8,128)(2,1)S(1)}, u32[]{:S(2)}, u32[]{:S(2)}) collective-permute-start(bf16[147,4096]{1,0:T(8,128)(2,1)S(1)} %pad_maximum_fusion), channel_id=1, source_target_pairs={{0,2},{2,4},{4,6},{6,8},{8,10},{10,12},{12,14},{1,3},{3,5},{5,7},{... | collective-permute-start | bytes 3612680 | tf_op jit(solution)/shard_map/ppermute | solution.py:314
  27.2 0.7 %pair.1 = bf16[32,4224]{1,0:T(8,128)(2,1)S(1)} custom-call(s32[3]{0:T(128)S(1)} %pad_add_fusion.scal, bf16[16,4224]{1,0:T(8,128)(2,1)S(1)} %get-tuple-element.30.mine_ref, bf16[16,4224]{1,0:T(8,128)(2,1)S(1)} %collective-permute-done.1.other_ref, f32[8,16]{1,0:T(8,128)S(1)} %copy-done.3), custom_call_target="tpu_custom_call" | custom-call | tf_op jit(solution)/shard_map/pair/pallas_call | solution.py:361
  27.9 3.4 %collective-permute-start.3 = (bf16[32,4224]{1,0:T(8,128)(2,1)S(1)}, bf16[32,4224]{1,0:T(8,128)(2,1)S(1)}, u32[]{:S(2)}, u32[]{:S(2)}) collective-permute-start(bf16[32,4224]{1,0:T(8,128)(2,1)S(1)} %pair.1), channel_id=1, source_target_pairs={{0,4},{4,8},{8,12},{1,5},{5,9},{9,13},{16,20},{20,24},{24,28},{17,... | collective-permute-start | bytes 811016 | tf_op jit(solution)/shard_map/ppermute | solution.py:369
  31.4 3.4 %collective-permute-start.5 = (bf16[16,4224]{1,0:T(8,128)(2,1)S(1)}, bf16[16,4224]{1,0:T(8,128)(2,1)S(1)}, u32[]{:S(2)}, u32[]{:S(2)}) collective-permute-start(bf16[16,4224]{1,0:T(8,128)(2,1)S(1)} %slice.18), channel_id=1, source_target_pairs={{0,12},{1,13},{16,28},{17,29}} | collective-permute-start | bytes 405512 | tf_op jit(solution)/shard_map/ppermute | solution.py:371
  34.8 1.8 %collective-permute-start.4 = (bf16[16,4224]{1,0:T(8,128)(2,1)S(1)}, bf16[16,4224]{1,0:T(8,128)(2,1)S(1)}, u32[]{:S(2)}, u32[]{:S(2)}) collective-permute-start(bf16[16,4224]{1,0:T(8,128)(2,1)S(1)} %slice.18), channel_id=1, source_target_pairs={{0,8},{4,12},{1,9},{5,13},{16,24},{20,28},{17,25},{21,29}} | collective-permute-start | bytes 405512 | tf_op jit(solution)/shard_map/ppermute | solution.py:371
  36.7 2.8 %collective-permute-done.5.refs_1_ = bf16[16,4224]{1,0:T(8,128)(2,1)S(1)} collective-permute-done((bf16[16,4224]{1,0:T(8,128)(2,1)S(1)}, bf16[16,4224]{1,0:T(8,128)(2,1)S(1)}, u32[]{:S(2)}, u32[]{:S(2)}) %collective-permute-start.5) | collective-permute-done | bytes 135200 | tf_op jit(solution)/shard_map/ppermute | solution.py:371
  39.4 1.4 %collective-permute-done.4.refs_0_ = bf16[16,4224]{1,0:T(8,128)(2,1)S(1)} collective-permute-done((bf16[16,4224]{1,0:T(8,128)(2,1)S(1)}, bf16[16,4224]{1,0:T(8,128)(2,1)S(1)}, u32[]{:S(2)}, u32[]{:S(2)}) %collective-permute-start.4) | collective-permute-done | bytes 135200 | tf_op jit(solution)/shard_map/ppermute | solution.py:371
  40.9 0.3 carry.1
  41.2 1.5 %collective-permute-start.6 = (bf16[16,4096]{1,0:T(8,128)(2,1)S(1)}, bf16[16,4096]{1,0:T(8,128)(2,1)S(1)}, u32[]{:S(2)}, u32[]{:S(2)}) collective-permute-start(bf16[16,4096]{1,0:T(8,128)(2,1)S(1)} %get-tuple-element.42), channel_id=1, source_target_pairs={{0,2},{4,6},{8,10},{12,14},{1,3},{5,7},{9,11},{13,15},{16,18},{20,... | collective-permute-start | bytes 393224 | tf_op jit(solution)/shard_map/ppermute | solution.py:383
  42.7 4.3 %tables.1 = (bf16[8,512,256]{2,1,0:T(8,128)(2,1)S(1)}, bf16[8,288,144]{2,1,0:T(8,128)(2,1)S(1)}, bf16[8,256,48]{2,1,0:T(8,128)(2,1)S(1)}, bf16[8,144,48]{2,1,0:T...) custom-call(s32[3]{0:T(128)S(1)} %pad_add_fusion.scal, f32[8,16]{1,0:T(8,128)S(1)} %copy-done.4, ...), custom_call_target="tpu_custom_call" | custom-call | flops 100000000 | bytes 65536 | tf_op jit(solution)/shard_map/tables/pallas_call | solution.py:397
  47.0 5.8 %collective-permute-done.2.tail_ref.part_ref = bf16[147,4096]{1,0:T(8,128)(2,1)S(1)} collective-permute-done((bf16[147,4096]{1,0:T(8,128)(2,1)S(1)}, bf16[147,4096]{1,0:T(8,128)(2,1)S(1)}, u32[]{:S(2)}, u32[]{:S(2)}) %collective-permute-start.2) | collective-permute-done | bytes 1204256 | tf_op jit(solution)/shard_map/ppermute | solution.py:314
  52.8 2.6 %tail.1 = (f32[144,4096]{1,0:T(8,128)S(1)}, bf16[144,4096]{1,0:T(8,128)(2,1)S(1)}) custom-call(s32[3]{0:T(128)S(1)} %pad_add_fusion.scal, bf16[147,4096]{1,0:T(8,128)(2,1)S(1)} %collective-permute-done.2.tail_ref.part_ref, f32[3,3,4096]{2,1,0:T(4,128)S(1)} %copy-done.1), custom_call_target="tpu_custom_call" | custom-call | flops 100000000 | bytes 65536 | tf_op jit(solution)/shard_map/tail/pallas_call | solution.py:408
  55.4 0.8 %place.1 = (bf16[48,4096]{1,0:T(8,128)(2,1)S(1)}, bf16[48,4096]{1,0:T(8,128)(2,1)S(1)}) custom-call(s32[3]{0:T(128)S(1)} %pad_add_fusion.scal, bf16[16,4224]{1,0:T(8,128)(2,1)S(1)} %collective-permute-done.1.other_ref, bf16[147,4096]{1,0:T(8,128)(2,1)S(1)} %collective-permute-done.2.tail_ref.part_ref, bf16[16,4096]{1,0:T(8,128)(2,1)S(1)} %collective-permute-done.6.sent_ref, ...), custom_call_target="tpu_custom_call" | custom-call | tf_op jit(solution)/shard_map/place/pallas_call | solution.py:384
  56.2 10.1 %final.1 = bf16[256,4096]{1,0:T(8,128)(2,1)} custom-call(s32[3]{0:T(128)S(1)} %pad_add_fusion.scal, f32[256,4096]{1,0:T(8,128)S(1)} %get-tuple-element.27.q_ref, bf16[256,4096]{1,0:T(8,128)(2,1)S(1)} %get-tuple-element.28.u_ref, f32[144,4096]{1,0:T(8,128)S(1)} %get-tuple-element.35.qt_ref, bf16[144,4096]{1,0:T(8,128)(2,1)S(1)} %get-tuple-element.36.ut_ref, ...), custom_call_target="tpu_custom_call" | custom-call | flops 100000000 | bytes 65536 | tf_op jit(solution)/shard_map/final/pallas_call | solution.py:424
  (19 shorter events, 0.5 us)
Async XLA Ops:
  1.5 6.4 %collective-permute-start = (bf16[3,4096]{1,0:T(4,128)(2,1)S(1)}, bf16[3,4096]{1,0:T(4,128)(2,1)S(1)}, u32[]{:S(2)}, u32[]{:S(2)}) collective-permute-start(bf16[3,4096]{1,0:T(4,128)(2,1)S(1)} %concatenate.6), channel_id=1, source_target_pairs={{0,2},{2,4},{4,6},{6,8},{8,10},{10,12},{12,14},{1,3},{3,5},{5,7},{... | collective-permute-start | bytes 73736 | tf_op jit(solution)/shard_map/ppermute | solution.py:314
  9.4 1.6 %copy-start = (bf16[256,4096]{1,0:T(8,128)(2,1)S(1)}, bf16[256,4096]{1,0:T(8,128)(2,1)}, u32[]{:S(2)}) copy-start(bf16[256,4096]{1,0:T(8,128)(2,1)} %x_ref.1) | copy-start | bytes 6291460
  10.9 0.9 %copy-start.1 = (f32[3,3,4096]{2,1,0:T(4,128)S(1)}, f32[3,3,4096]{2,1,0:T(4,128)}, u32[]{:S(2)}) copy-start(f32[3,3,4096]{2,1,0:T(4,128)} %w_ref.4) | copy-start | bytes 442372
  11.9 0.7 %copy-start.3 = (f32[8,16]{1,0:T(8,128)S(1)}, f32[8,16]{1,0:T(8,128)}, u32[]{:S(2)}) copy-start(f32[8,16]{1,0:T(8,128)} %dec_ref.9) | copy-start | bytes 1540
  17.3 5.4 %collective-permute-start.1 = (bf16[16,4224]{1,0:T(8,128)(2,1)S(1)}, bf16[16,4224]{1,0:T(8,128)(2,1)S(1)}, u32[]{:S(2)}, u32[]{:S(2)}) collective-permute-start(bf16[16,4224]{1,0:T(8,128)(2,1)S(1)} %get-tuple-element.30.mine_ref), channel_id=1, source_target_pairs={{0,2},{2,0},{4,6},{6,4},{8,10},{10,8},{12,14},{14,12},{1,3},{3,1},... | collective-permute-start | bytes 405512 | tf_op jit(solution)/shard_map/ppermute | solution.py:356
  23.0 17.9 %copy-start.4 = (f32[8,16]{1,0:T(8,128)S(1)}, f32[8,16]{1,0:T(8,128)}, u32[]{:S(2)}) copy-start(f32[8,16]{1,0:T(8,128)} %dec_ref.9) | copy-start | bytes 1540
  23.0 19.7 %copy-start.6 = (bf16[8,128]{1,0:T(8,128)(2,1)S(1)}, bf16[8,128]{1,0:T(8,128)(2,1)}, u32[]{:S(2)}) copy-start(bf16[8,128]{1,0:T(8,128)(2,1)} %param.13) | copy-start | bytes 6148
  23.0 19.7 %copy-start.5 = (f32[8,16]{1,0:T(8,128)S(1)}, f32[8,16]{1,0:T(8,128)}, u32[]{:S(2)}) copy-start(f32[8,16]{1,0:T(8,128)} %res_ref.1) | copy-start | bytes 1540
  23.1 29.7 %collective-permute-start.2 = (bf16[147,4096]{1,0:T(8,128)(2,1)S(1)}, bf16[147,4096]{1,0:T(8,128)(2,1)S(1)}, u32[]{:S(2)}, u32[]{:S(2)}) collective-permute-start(bf16[147,4096]{1,0:T(8,128)(2,1)S(1)} %pad_maximum_fusion), channel_id=1, source_target_pairs={{0,2},{2,4},{4,6},{6,8},{8,10},{10,12},{12,14},{1,3},{3,5},{5,7},{... | collective-permute-start | bytes 3612680 | tf_op jit(solution)/shard_map/ppermute | solution.py:314
  27.9 13.0 %collective-permute-start.3 = (bf16[32,4224]{1,0:T(8,128)(2,1)S(1)}, bf16[32,4224]{1,0:T(8,128)(2,1)S(1)}, u32[]{:S(2)}, u32[]{:S(2)}) collective-permute-start(bf16[32,4224]{1,0:T(8,128)(2,1)S(1)} %pair.1), channel_id=1, source_target_pairs={{0,4},{4,8},{8,12},{1,5},{5,9},{9,13},{16,20},{20,24},{24,28},{17,... | collective-permute-start | bytes 811016 | tf_op jit(solution)/shard_map/ppermute | solution.py:369
  31.3 24.9 %copy-start.2 = (f32[3,3,4096]{2,1,0:T(4,128)S(1)}, f32[3,3,4096]{2,1,0:T(4,128)}, u32[]{:S(2)}) copy-start(f32[3,3,4096]{2,1,0:T(4,128)} %w_ref.5) | copy-start | bytes 442372
  31.4 8.1 %collective-permute-start.5 = (bf16[16,4224]{1,0:T(8,128)(2,1)S(1)}, bf16[16,4224]{1,0:T(8,128)(2,1)S(1)}, u32[]{:S(2)}, u32[]{:S(2)}) collective-permute-start(bf16[16,4224]{1,0:T(8,128)(2,1)S(1)} %slice.18), channel_id=1, source_target_pairs={{0,12},{1,13},{16,28},{17,29}} | collective-permute-start | bytes 405512 | tf_op jit(solution)/shard_map/ppermute | solution.py:371
  34.8 6.1 %collective-permute-start.4 = (bf16[16,4224]{1,0:T(8,128)(2,1)S(1)}, bf16[16,4224]{1,0:T(8,128)(2,1)S(1)}, u32[]{:S(2)}, u32[]{:S(2)}) collective-permute-start(bf16[16,4224]{1,0:T(8,128)(2,1)S(1)} %slice.18), channel_id=1, source_target_pairs={{0,8},{4,12},{1,9},{5,13},{16,24},{20,28},{17,25},{21,29}} | collective-permute-start | bytes 405512 | tf_op jit(solution)/shard_map/ppermute | solution.py:371
  41.2 14.2 %collective-permute-start.6 = (bf16[16,4096]{1,0:T(8,128)(2,1)S(1)}, bf16[16,4096]{1,0:T(8,128)(2,1)S(1)}, u32[]{:S(2)}, u32[]{:S(2)}) collective-permute-start(bf16[16,4096]{1,0:T(8,128)(2,1)S(1)} %get-tuple-element.42), channel_id=1, source_target_pairs={{0,2},{4,6},{8,10},{12,14},{1,3},{5,7},{9,11},{13,15},{16,18},{20,... | collective-permute-start | bytes 393224 | tf_op jit(solution)/shard_map/ppermute | solution.py:383

commit v4 on v3

--- a/solution.py
+++ b/solution.py
@@ -49,6 +49,15 @@
         rows[8:],
         pltpu.roll(rows, 1, 0)[8:] * mask_ref[0, at, :],
         pltpu.roll(rows, 2, 0)[8:] * mask_ref[1, at, :],
+    )
+
+
+def taps_of(prev, rows, mask_ref, at):
+    both = jnp.concatenate([prev, rows], 0)
+    return (
+        rows,
+        pltpu.roll(both, 1, 0)[8:] * mask_ref[0, at, :],
+        pltpu.roll(both, 2, 0)[8:] * mask_ref[1, at, :],
     )
 
 
@@ -79,12 +88,31 @@
     return hi, (v - hi.astype(F32)).astype(BF)
 
 
+def load_kernel(bounds, x_ref, w_ref, dec_ref, x_out, w_out, dec_out, edge_out, sems):
+    pairs = ((x_ref, x_out), (w_ref, w_out), (dec_ref, dec_out))
+    copies = [pltpu.make_async_copy(a, b, sems.at[i]) for i, (a, b) in enumerate(pairs)]
+    for copy in copies:
+        copy.start()
+    for copy in copies:
+        copy.wait()
+    length, width = x_out.shape
+    last = x_out[length - 16 :, :].astype(F32)[14:]
+    own = jnp.full((1, width), bounds[0], jnp.int32).astype(F32)
+    edge_out[...] = jnp.concatenate([last, own], 0).astype(BF)
+
+
 def states_kernel(
-    cut, modes, lanes, scal, x_ref, edge_ref, w_ref, dec_ref, out_ref, part_ref, q_ref, u_ref,
-    mask_ref, x_scr,
+    cut, modes, lanes, bounds, x_ref, edge_ref, w_ref, dec_ref, out_ref, part_ref, q_ref, u_ref,
+    scal_ref, mask_ref,
 ):
     length, width = x_ref.shape
-    own, prior = scal[0], scal[1]
+    own = bounds[0]
+    place = lax.axis_index("seq")
+    told = jnp.max(edge_ref[...].astype(F32)[2:3, :LANE]).astype(jnp.int32)
+    prior = jnp.where(place == 0, length, told)
+    scal_ref[0] = own
+    scal_ref[1] = prior
+    scal_ref[2] = place % 2
     write_masks(mask_ref, 0, own, prior, length)
     flag = jnp.full((modes, LANE), own, jnp.int32).astype(F32)
     out_ref[:, width:] = flag.astype(BF)
@@ -95,14 +123,15 @@
     reach = (p >= own) | (own >= length)
     reach_cut = (p < cut) & ((p >= own) | (own >= cut))
     for i, cols in spans(width // lanes, lanes):
-        scr = x_scr.at[i % x_scr.shape[0]]
-        scr[6:8, :] = edge_ref[:, cols].astype(F32)[:2]
-        scr[8 : 8 + length, :] = x_ref[:, cols].astype(F32)
         for tile in tiles(lanes):
             here = slice(cols.start + tile.start, cols.start + tile.stop)
             w = weights_of(w_ref, here)
+            edge = edge_ref[:, here].astype(F32)
+            prev = jnp.concatenate([jnp.zeros((6, LANE), F32), edge[:2]], 0)
             for at in chunks(0, length):
-                taps = taps_at(scr, mask_ref, at, tile)
+                x = x_ref[at, here].astype(F32)
+                taps = taps_of(prev, x, mask_ref, at)
+                prev = x[-8:]
                 u_ref[at, here] = (combine(w[1], taps) * combine(w[2], taps)).astype(BF)
                 q_ref[at, here] = combine(w[0], taps)
         dec = column(dec_ref[i : i + 1, :])
@@ -240,7 +269,7 @@
 
 
 def tail_kernel(
-    modes, length, lanes, scal, tail_ref, w_ref, q_ref, u_ref, mask_ref, x_scr
+    modes, length, lanes, scal, tail_ref, w_ref, t_ref, q_ref, z_ref, mask_ref, x_scr, u_scr
 ):
     rows = tail_ref.shape[0] - modes
 
@@ -250,45 +279,52 @@
     )
 
     for i, cols in spans(tail_ref.shape[1] // lanes, lanes):
-        scr = x_scr.at[i]
+        scr, us = x_scr.at[i], u_scr.at[i]
         scr[8 + WIN - rows : 8 + WIN, :] = tail_ref[modes:, cols].astype(F32)
         for tile in tiles(lanes):
             here = slice(cols.start + tile.start, cols.start + tile.stop)
             w = weights_of(w_ref, here)
             for at in chunks(0, WIN):
                 taps = taps_at(scr, mask_ref, at, tile)
-                u_ref[at, here] = (combine(w[1], taps) * combine(w[2], taps)).astype(BF)
+                us[at, tile] = (combine(w[1], taps) * combine(w[2], taps)).astype(BF)
                 q_ref[at, here] = combine(w[0], taps)
+        near = dot(t_ref[i], us[...])
+        z_ref[:, cols] = near[:WIN] + near[WIN:]
+
+
+def near_kernel(lanes, u_ref, t_ref, z_ref):
+    length = u_ref.shape[0]
+    for i, cols in spans(u_ref.shape[1] // lanes, lanes):
+        near = dot(t_ref[i], u_ref[:, cols])
+        z_ref[:, cols] = near[:length] + near[length:]
 
 
 def final_kernel(
-    lanes, scal, q_ref, u_ref, qt_ref, ut_ref, t_ref, tt_ref, r_ref, rt_ref, st_ref, stt_ref,
-    w_ref, bt_ref, b_ref, out_ref, mask_ref, y_scr, w_scr, q_scr, z_scr, o_scr, sems,
+    lanes, scal, q_ref, z_ref, qt_ref, zt_ref, r_ref, rt_ref, st_ref, stt_ref,
+    w_ref, bt_ref, b_ref, out_ref, mask_ref, w_scr, q_scr, z_scr, o_scr, sems,
 ):
     length = q_ref.shape[0]
 
     write_masks(mask_ref, WIN, scal[0], scal[1], length)
-    y_scr[:, :8, :] = jnp.zeros((y_scr.shape[0], 8, y_scr.shape[2]), F32)
     copies = []
     for i, cols in spans(q_ref.shape[1] // lanes, lanes):
-        k = i % y_scr.shape[0]
-        ys, ws, qs, zs = y_scr.at[k], w_scr.at[k], q_scr.at[k], z_scr.at[k]
-        near = dot(tt_ref[i], ut_ref[:, cols])
-        zs[:WIN, :] = near[:WIN] + near[WIN:] + dot(rt_ref[i], stt_ref[:, cols])
-        near = dot(t_ref[i], u_ref[:, cols])
-        zs[WIN:, :] = near[:length] + near[length:] + dot(r_ref[i], st_ref[:, cols])
+        k = i % w_scr.shape[0]
+        ws, qs, zs = w_scr.at[k], q_scr.at[k], z_scr.at[k]
+        zs[:WIN, :] = dot(rt_ref[i], stt_ref[:, cols])
+        zs[WIN:, :] = dot(r_ref[i], st_ref[:, cols])
         for tile in tiles(lanes):
             here = slice(cols.start + tile.start, cols.start + tile.stop)
+            w = weights_of(w_ref, here)
+            prev = jnp.zeros((8, LANE), F32)
             for at in chunks(0, WIN) + chunks(WIN, WIN + length):
                 if at.start < WIN:
-                    q = qt_ref[at, here]
+                    q, z = qt_ref[at, here], zt_ref[at, here]
                 else:
-                    q = q_ref[at.start - WIN : at.stop - WIN, here]
-                y = (q * zs[at, tile]).astype(BF).astype(F32)
-                ys[8 + at.start : 8 + at.stop, tile] = y
-            w = weights_of(w_ref, here)
-            for at in chunks(0, WIN) + chunks(WIN, WIN + length):
-                taps = taps_at(ys, mask_ref, at, tile)
+                    part = slice(at.start - WIN, at.stop - WIN)
+                    q, z = q_ref[part, here], z_ref[part, here]
+                y = (q * (z + zs[at, tile])).astype(BF).astype(F32)
+                taps = taps_of(prev, y, mask_ref, at)
+                prev = y[-8:]
                 ws[at, tile] = (combine(w[1], taps) * combine(w[2], taps)).astype(BF)
                 if at.start >= WIN:
                     qs[at.start - WIN : at.stop - WIN, tile] = combine(w[0], taps)
@@ -308,15 +344,9 @@
     rows = filter_len + 3
     cut = length - rows + 2
     size = lax.axis_size("seq")
-    place = lax.axis_index("seq")
 
     def behind(array, by):
         return lax.ppermute(array, "seq", [(i, i + by) for i in range(size - by)])
-
-    own_row = jnp.broadcast_to(bounds.astype(BF)[:, None], (1, channels))
-    edge = behind(jnp.concatenate([inputs[length - 2 :], own_row], 0), 1)
-    prior = jnp.where(place == 0, length, edge[2, 0].astype(F32).astype(jnp.int32))
-    scal = jnp.stack([bounds[0], prior, (place % 2).astype(jnp.int32)])
 
     sm = pl.BlockSpec(memory_space=SMEM)
     whole = pl.BlockSpec(memory_space=pltpu.VMEM)
@@ -324,6 +354,18 @@
     count = 2 if groups % 2 == 0 else 1
     steps, wide = groups // count, lanes * count
 
+    hbm = pl.BlockSpec(memory_space=pl.ANY)
+    held, held_first, held_decay, edge = pl.pallas_call(
+        load_kernel,
+        in_specs=[sm] + [hbm] * 3,
+        out_specs=[whole] * 4,
+        out_shape=[jax.ShapeDtypeStruct(a.shape, a.dtype) for a in (inputs, feat_first, li_decay)]
+        + [jax.ShapeDtypeStruct((3, channels), BF)],
+        scratch_shapes=[pltpu.SemaphoreType.DMA((3,))],
+        compiler_params=pltpu.CompilerParams(vmem_limit_bytes=50 * 1024 * 1024),
+        name="load",
+    )(bounds, inputs, feat_first, li_decay)
+    edge = behind(edge, 1)
     def block(*shape):
         return pl.BlockSpec(shape, lambda g: (0,) * (len(shape) - 1) + (g,))
 
@@ -336,25 +378,26 @@
     def fixed(*shape):
         return pl.BlockSpec(shape, lambda g: (0,) * len(shape))
 
-    mine, part, q_own, u_own = pl.pallas_call(
+    mine, part, q_own, u_own, scal = pl.pallas_call(
         functools.partial(states_kernel, cut, modes, lanes),
         in_specs=[sm] + [whole] * 4,
-        out_specs=[whole] * 4,
+        out_specs=[whole] * 4 + [sm],
         out_shape=[
             jax.ShapeDtypeStruct((modes, channels + LANE), BF),
             jax.ShapeDtypeStruct((modes, channels), BF),
             jax.ShapeDtypeStruct((length, channels), F32),
             jax.ShapeDtypeStruct((length, channels), BF),
+            jax.ShapeDtypeStruct((3,), jnp.int32),
         ],
         scratch_shapes=[
-            pltpu.VMEM((2, length, LANE), F32), pltpu.VMEM((count, 8 + length, lanes), F32),
+            pltpu.VMEM((2, length, LANE), F32),
         ],
         compiler_params=params,
         cost_estimate=pl.CostEstimate(flops=10**8, bytes_accessed=2**16, transcendentals=0),
         name="states",
-    )(scal, inputs, edge, feat_first, li_decay)
+    )(bounds, held, edge, held_first, held_decay)
     other = lax.ppermute(mine, "seq", [(i, i ^ 1) for i in range(size)])
-    inputs_late, part, other = lax.optimization_barrier((inputs, part, other))
+    inputs_late, part, other = lax.optimization_barrier((held, part, other))
     message = jnp.concatenate([part, inputs_late[length - rows :]], 0)
     message, other = lax.optimization_barrier((message, other))
     tail = behind(message, 1)
@@ -365,7 +408,7 @@
         out_shape=jax.ShapeDtypeStruct((2 * modes, channels + LANE), BF),
         compiler_params=params,
         name="pair",
-    )(scal, mine, other, li_decay)
+    )(scal, mine, other, held_decay)
     near = lax.ppermute(pair, "seq", [(i, i + 2) for i in range(0, size - 2, 2)])
     far = [
         lax.ppermute(pair[:modes], "seq", [(i, i + by) for i in range(0, size - by, 2)])
@@ -379,7 +422,7 @@
         out_shape=[jax.ShapeDtypeStruct((modes, channels), BF), state_shape, state_shape],
         compiler_params=params,
         name="carry",
-    )(near, li_decay, *far)
+    )(near, held_decay, *far)
     sent = lax.ppermute(send, "seq", [(i, i + 1) for i in range(0, size, 2)])
     own_state, win_state = pl.pallas_call(
         functools.partial(place_kernel, cut, modes, length),
@@ -388,7 +431,7 @@
         out_shape=[jax.ShapeDtypeStruct((3 * modes, channels), BF)] * 2,
         compiler_params=params,
         name="place",
-    )(scal, other, tail, sent, even_own, even_late, li_decay)
+    )(scal, other, tail, sent, even_own, even_late, held_decay)
 
     shapes = [
         (2 * length, length), (2 * WIN, WIN), (length, 3 * modes), (WIN, 3 * modes),
@@ -405,29 +448,39 @@
         name="tables",
     )(scal, li_decay, li_residue, mr_filter.reshape(groups, 1, filter_len))
 
-    q_win, u_win = pl.pallas_call(
+    z_own = pl.pallas_call(
+        functools.partial(near_kernel, lanes),
+        in_specs=[whole] * 2,
+        out_specs=whole,
+        out_shape=jax.ShapeDtypeStruct((length, channels), F32),
+        compiler_params=params,
+        cost_estimate=pl.CostEstimate(flops=10**8, bytes_accessed=2**16, transcendentals=0),
+        name="near",
+    )(u_own, t_own)
+    q_win, z_win = pl.pallas_call(
         functools.partial(tail_kernel, modes, length, lanes),
-        in_specs=[sm, whole, whole],
+        in_specs=[sm] + [whole] * 3,
         out_specs=[whole] * 2,
         out_shape=[
             jax.ShapeDtypeStruct((WIN, channels), F32),
-            jax.ShapeDtypeStruct((WIN, channels), BF),
+            jax.ShapeDtypeStruct((WIN, channels), F32),
         ],
         scratch_shapes=[
             pltpu.VMEM((2, WIN, LANE), F32), pltpu.VMEM((groups, 8 + WIN, lanes), F32),
+            pltpu.VMEM((groups, WIN, lanes), BF),
         ],
         compiler_params=params,
         cost_estimate=pl.CostEstimate(flops=10**8, bytes_accessed=2**16, transcendentals=0),
         name="tail",
-    )(scal, tail, feat_first)
+    )(scal, tail, held_first, t_win)
     full = WIN + length
     return pl.pallas_call(
         functools.partial(final_kernel, lanes),
-        in_specs=[sm] + [whole] * 13,
+        in_specs=[sm] + [whole] * 11,
         out_specs=pl.BlockSpec(memory_space=pl.ANY),
         out_shape=jax.ShapeDtypeStruct((length, channels), BF),
         scratch_shapes=[
-            pltpu.VMEM((2, full, LANE), F32), pltpu.VMEM((count, 8 + full, lanes), F32),
+            pltpu.VMEM((2, full, LANE), F32),
             pltpu.VMEM((count, full, lanes), BF), pltpu.VMEM((count, length, lanes), F32),
             pltpu.VMEM((count, full, lanes), F32), pltpu.VMEM((groups, length, lanes), BF),
             pltpu.SemaphoreType.DMA((groups,)),
@@ -436,7 +489,7 @@
         cost_estimate=pl.CostEstimate(flops=10**8, bytes_accessed=2**16, transcendentals=0),
         name="final",
     )(
-        scal, q_own, u_own, q_win, u_win, t_own, t_win, r_own, r_win, own_state, win_state,
+        scal, q_own, z_own, q_win, z_win, r_own, r_win, own_state, win_state,
         feat_second, b_win, b_own,
     )
 

time: 66.8 us -> 63.9 us (0.957)
  local copies, waits for them, and re-layouts: 4.99 us -> 1.93 us
  Pallas kernels: 23.5 us -> 25.7 us
  waiting for transfers between devices: 14.6 us -> 12.9 us
  between operations: 1.74 us -> 1.01 us
    pallas_call x0 -> x2, Pallas kernels: none -> 2.9 us  [the longest x1 1.64 us: per_device(): pl.pallas_call(load_kernel, in_specs=[sm] + [hbm] * 3, out_specs=[whole]...]
    unnamed x14 -> x10, local copies, waits for them, and re-layouts: 3.23 us -> 1.62 us
    slice x2 -> x0, local copies, waits for them, and re-layouts: 1.45 us -> none  [the longest x1 0.86 us: per_device(): edge = behind(jnp.concatenate([inputs[length - 2:], own_row], 0), 1)]
    ppermute x2, waiting for transfers between devices: 7.37 us -> 5.94 us  [behind(): return lax.ppermute(array, 'seq', [(i, i + by) for i in range(size - by)])]
    pallas_call x1, Pallas kernels: 10.1 us -> 9.03 us  [per_device(): pl.pallas_call(functools.partial(final_kernel, lanes), in_specs=[sm] + [w...]
    pallas_call x1, Pallas kernels: 2.59 us -> 3.38 us  [per_device(): pl.pallas_call(functools.partial(tail_kernel, modes, length, lanes), in_s...]
  transfers between devices with their start and end apart: 7 -> 7, of which waited for: 5 -> 5; matrix products, arithmetic and copies ran while one was open for 0% -> 0% of each run, Pallas kernels for 12% -> 16%
where the time goes in v4:
time: 63.9 us; the launch traced here: 63.6 us
  Pallas kernels  25.7 us (40%)
  starting transfers between devices  21.9 us (34%)
  waiting for transfers between devices  12.9 us (20%)
  local copies, waits for them, and re-layouts  1.93 us (3%)
  between operations  1.01 us (2%)
    pallas_call x1, Pallas kernels, per_device(): pl.pallas_call(functools.partial(final_kernel, lanes), in_specs=[sm] + [w...  9.03 us
    ppermute x2, starting transfers between devices, behind(): return lax.ppermute(array, 'seq', [(i, i + by) for i in range(size - by)])  8.85 us
    ppermute x2, waiting for transfers between devices, behind(): return lax.ppermute(array, 'seq', [(i, i + by) for i in range(size - by)])  5.94 us
    ppermute x2, starting transfers between devices, per_device(): lax.ppermute(pair[:modes], 'seq', [(i, i + by) for i in range(0, size - b...  5.79 us
    pallas_call x1, Pallas kernels, per_device(): pl.pallas_call(functools.partial(states_kernel, cut, modes, lanes), in_sp...  4.33 us
    pallas_call x1, Pallas kernels, per_device(): pl.pallas_call(functools.partial(tables_kernel, cut, modes, length), grid...  4.28 us
    ppermute x2, waiting for transfers between devices, per_device(): lax.ppermute(pair[:modes], 'seq', [(i, i + by) for i in range(0, size - b...  3.92 us
    ppermute x1, starting transfers between devices, per_device(): lax.ppermute(pair, 'seq', [(i, i + 2) for i in range(0, size - 2, 2)])  3.42 us
  transfers between devices with their start and end apart: 7, of which 5 were waited for; matrix products, arithmetic and copies ran while one was open for 0% of the time, Pallas kernels for 16%

profile of v4, /device:TPU:0, one launch (start us, length us, event | category | flops | bytes accessed | tf_op | source)
XLA Modules:
  0.0 63.6 jit_solution(2902899305620431691)
XLA Ops:
  0.7 0.9 %copy-done.1 = f32[3,3,4096]{2,1,0:T(4,128)S(1)} copy-done((f32[3,3,4096]{2,1,0:T(4,128)S(1)}, f32[3,3,4096]{2,1,0:T(4,128)}, u32[]{:S(2)}) %copy-start.1) | copy-done | bytes 147480
  1.6 0.7 %copy-done.2 = f32[8,16]{1,0:T(8,128)S(1)} copy-done((f32[8,16]{1,0:T(8,128)S(1)}, f32[8,16]{1,0:T(8,128)}, u32[]{:S(2)}) %copy-start.2) | copy-done | bytes 536
  2.3 1.6 %load.1 = (bf16[256,4096]{1,0:T(8,128)(2,1)S(1)}, f32[3,3,4096]{2,1,0:T(4,128)S(1)}, f32[8,16]{1,0:T(8,128)S(1)}, bf16[3,4096]{1,0:T(4,128)(2,1)S(1)}) custom-call(s32[1]{0:T(128)S(6)} %copy.9.bounds, bf16[256,4096]{1,0:T(8,128)(2,1)} %x_ref.1, f32[3,3,4096]{2,1,0:T(4,128)S(1)} %copy-done.1, f32[8,16]{1,0:T(8,128)S(1)} %copy-done.2), custom_call_target="tpu_custom_call" | custom-call | tf_op jit(solution)/shard_map/load/pallas_call | solution.py:358
  3.9 4.8 %collective-permute-start = (bf16[3,4096]{1,0:T(4,128)(2,1)S(1)}, bf16[3,4096]{1,0:T(4,128)(2,1)S(1)}, u32[]{:S(2)}, u32[]{:S(2)}) collective-permute-start(bf16[3,4096]{1,0:T(4,128)(2,1)S(1)} %get-tuple-element.33), channel_id=1, source_target_pairs={{0,2},{2,4},{4,6},{6,8},{8,10},{10,12},{12,14},{1,3},{3,5},{5,7},{... | collective-permute-start | bytes 73736 | tf_op jit(solution)/shard_map/ppermute | solution.py:349
  8.8 1.6 %collective-permute-done.edge_ref = bf16[3,4096]{1,0:T(4,128)(2,1)S(1)} collective-permute-done((bf16[3,4096]{1,0:T(4,128)(2,1)S(1)}, bf16[3,4096]{1,0:T(4,128)(2,1)S(1)}, u32[]{:S(2)}, u32[]{:S(2)}) %collective-permute-start) | collective-permute-done | bytes 24608 | tf_op jit(solution)/shard_map/ppermute | solution.py:349
  10.4 4.3 %states.1 = (bf16[16,4224]{1,0:T(8,128)(2,1)S(1)}, bf16[16,4096]{1,0:T(8,128)(2,1)S(1)}, f32[256,4096]{1,0:T(8,128)S(1)}, bf16[256,4096]{1,0:T(8,128)(2,1)S(1)}, s32[3]{0:T(128)S(1)}) custom-call(s32[1]{0:T(128)S(6)} %copy.9.bounds, bf16[256,4096]{1,0:T(8,128)(2,1)S(1)} %get-tuple-element.43.x_ref, bf16[3,4096]{1,0:T(4,128)(2,1)S(1)} %collective-permute-done.edge_ref, ...), custom_call_target="tpu_custom_call" | custom-call | flops 100000000 | bytes 65536 | tf_op jit(solution)/shard_map/states/pallas_call | solution.py:381
  14.7 2.4 %collective-permute-start.1 = (bf16[16,4224]{1,0:T(8,128)(2,1)S(1)}, bf16[16,4224]{1,0:T(8,128)(2,1)S(1)}, u32[]{:S(2)}, u32[]{:S(2)}) collective-permute-start(bf16[16,4224]{1,0:T(8,128)(2,1)S(1)} %get-tuple-element.41.mine_ref), channel_id=1, source_target_pairs={{0,2},{2,0},{4,6},{6,4},{8,10},{10,8},{12,14},{14,12},{1,3},{3,1},... | collective-permute-start | bytes 405512 | tf_op jit(solution)/shard_map/ppermute | solution.py:399
  17.1 3.0 %collective-permute-done.1.other_ref = bf16[16,4224]{1,0:T(8,128)(2,1)S(1)} collective-permute-done((bf16[16,4224]{1,0:T(8,128)(2,1)S(1)}, bf16[16,4224]{1,0:T(8,128)(2,1)S(1)}, u32[]{:S(2)}, u32[]{:S(2)}) %collective-permute-start.1) | collective-permute-done | bytes 135200 | tf_op jit(solution)/shard_map/ppermute | solution.py:399
  20.1 0.3 slice.7
  20.5 4.0 %collective-permute-start.2 = (bf16[147,4096]{1,0:T(8,128)(2,1)S(1)}, bf16[147,4096]{1,0:T(8,128)(2,1)S(1)}, u32[]{:S(2)}, u32[]{:S(2)}) collective-permute-start(bf16[147,4096]{1,0:T(8,128)(2,1)S(1)} %pad_maximum_fusion), channel_id=1, source_target_pairs={{0,2},{2,4},{4,6},{6,8},{8,10},{10,12},{12,14},{1,3},{3,5},{5,7},{... | collective-permute-start | bytes 3612680 | tf_op jit(solution)/shard_map/ppermute | solution.py:349
  24.5 0.7 %pair.1 = bf16[32,4224]{1,0:T(8,128)(2,1)S(1)} custom-call(s32[3]{0:T(128)S(1)} %get-tuple-element.36.scal, bf16[16,4224]{1,0:T(8,128)(2,1)S(1)} %get-tuple-element.41.mine_ref, bf16[16,4224]{1,0:T(8,128)(2,1)S(1)} %collective-permute-done.1.other_ref, f32[8,16]{1,0:T(8,128)S(1)} %get-tuple-element.35.dec_ref), custom_call_target="tpu_custom_call" | custom-call | tf_op jit(solution)/shard_map/pair/pallas_call | solution.py:404
  25.3 3.4 %collective-permute-start.3 = (bf16[32,4224]{1,0:T(8,128)(2,1)S(1)}, bf16[32,4224]{1,0:T(8,128)(2,1)S(1)}, u32[]{:S(2)}, u32[]{:S(2)}) collective-permute-start(bf16[32,4224]{1,0:T(8,128)(2,1)S(1)} %pair.1), channel_id=1, source_target_pairs={{0,4},{4,8},{8,12},{1,5},{5,9},{9,13},{16,20},{20,24},{24,28},{17,... | collective-permute-start | bytes 811016 | tf_op jit(solution)/shard_map/ppermute | solution.py:412
  28.7 4.5 %collective-permute-start.4 = (bf16[16,4224]{1,0:T(8,128)(2,1)S(1)}, bf16[16,4224]{1,0:T(8,128)(2,1)S(1)}, u32[]{:S(2)}, u32[]{:S(2)}) collective-permute-start(bf16[16,4224]{1,0:T(8,128)(2,1)S(1)} %slice.9), channel_id=1, source_target_pairs={{0,8},{4,12},{1,9},{5,13},{16,24},{20,28},{17,25},{21,29}} | collective-permute-start | bytes 405512 | tf_op jit(solution)/shard_map/ppermute | solution.py:414
  33.2 1.3 %collective-permute-start.5 = (bf16[16,4224]{1,0:T(8,128)(2,1)S(1)}, bf16[16,4224]{1,0:T(8,128)(2,1)S(1)}, u32[]{:S(2)}, u32[]{:S(2)}) collective-permute-start(bf16[16,4224]{1,0:T(8,128)(2,1)S(1)} %slice.9), channel_id=1, source_target_pairs={{0,12},{1,13},{16,28},{17,29}} | collective-permute-start | bytes 405512 | tf_op jit(solution)/shard_map/ppermute | solution.py:414
  34.5 2.5 %collective-permute-done.4.refs_0_ = bf16[16,4224]{1,0:T(8,128)(2,1)S(1)} collective-permute-done((bf16[16,4224]{1,0:T(8,128)(2,1)S(1)}, bf16[16,4224]{1,0:T(8,128)(2,1)S(1)}, u32[]{:S(2)}, u32[]{:S(2)}) %collective-permute-start.4) | collective-permute-done | bytes 135200 | tf_op jit(solution)/shard_map/ppermute | solution.py:414
  37.0 1.4 %collective-permute-done.5.refs_1_ = bf16[16,4224]{1,0:T(8,128)(2,1)S(1)} collective-permute-done((bf16[16,4224]{1,0:T(8,128)(2,1)S(1)}, bf16[16,4224]{1,0:T(8,128)(2,1)S(1)}, u32[]{:S(2)}, u32[]{:S(2)}) %collective-permute-start.5) | collective-permute-done | bytes 135200 | tf_op jit(solution)/shard_map/ppermute | solution.py:414
  38.5 0.3 carry.1
  38.7 1.5 %collective-permute-start.6 = (bf16[16,4096]{1,0:T(8,128)(2,1)S(1)}, bf16[16,4096]{1,0:T(8,128)(2,1)S(1)}, u32[]{:S(2)}, u32[]{:S(2)}) collective-permute-start(bf16[16,4096]{1,0:T(8,128)(2,1)S(1)} %get-tuple-element.52), channel_id=1, source_target_pairs={{0,2},{4,6},{8,10},{12,14},{1,3},{5,7},{9,11},{13,15},{16,18},{20,... | collective-permute-start | bytes 393224 | tf_op jit(solution)/shard_map/ppermute | solution.py:426
  40.3 4.3 %tables.1 = (bf16[8,512,256]{2,1,0:T(8,128)(2,1)S(1)}, bf16[8,288,144]{2,1,0:T(8,128)(2,1)S(1)}, bf16[8,256,48]{2,1,0:T(8,128)(2,1)S(1)}, bf16[8,144,48]{2,1,0:T...) custom-call(s32[3]{0:T(128)S(1)} %get-tuple-element.36.scal, f32[8,16]{1,0:T(8,128)S(1)} %copy-done.2, ...), custom_call_target="tpu_custom_call" | custom-call | flops 100000000 | bytes 65536 | tf_op jit(solution)/shard_map/tables/pallas_call | solution.py:440
  44.6 1.3 %near.1.z_ref = f32[256,4096]{1,0:T(8,128)S(1)} custom-call(bf16[256,4096]{1,0:T(8,128)(2,1)S(1)} %get-tuple-element.38.u_ref, bf16[8,512,256]{2,1,0:T(8,128)(2,1)S(1)} %get-tuple-element.39.t_ref), custom_call_target="tpu_custom_call" | custom-call | flops 100000000 | bytes 65536 | tf_op jit(solution)/shard_map/near/pallas_call | solution.py:451
  45.8 4.4 %collective-permute-done.2.tail_ref.part_ref = bf16[147,4096]{1,0:T(8,128)(2,1)S(1)} collective-permute-done((bf16[147,4096]{1,0:T(8,128)(2,1)S(1)}, bf16[147,4096]{1,0:T(8,128)(2,1)S(1)}, u32[]{:S(2)}, u32[]{:S(2)}) %collective-permute-start.2) | collective-permute-done | bytes 1204256 | tf_op jit(solution)/shard_map/ppermute | solution.py:349
  50.2 3.4 %tail.1 = (f32[144,4096]{1,0:T(8,128)S(1)}, f32[144,4096]{1,0:T(8,128)S(1)}) custom-call(s32[3]{0:T(128)S(1)} %get-tuple-element.36.scal, bf16[147,4096]{1,0:T(8,128)(2,1)S(1)} %collective-permute-done.2.tail_ref.part_ref, f32[3,3,4096]{2,1,0:T(4,128)S(1)} %get-tuple-element.34.w_ref, bf16[8,288,144]{2,1,0:T(8,128)(2,1)S(1)} %get-tuple-element.46.t_ref), custom_call_target="tpu_custom_call" | custom-call | flops 100000000 | bytes 65536 | tf_op jit(solution)/shard_map/tail/pallas_call | solution.py:460
  53.6 0.8 %place.1 = (bf16[48,4096]{1,0:T(8,128)(2,1)S(1)}, bf16[48,4096]{1,0:T(8,128)(2,1)S(1)}) custom-call(s32[3]{0:T(128)S(1)} %get-tuple-element.36.scal, bf16[16,4224]{1,0:T(8,128)(2,1)S(1)} %collective-permute-done.1.other_ref, bf16[147,4096]{1,0:T(8,128)(2,1)S(1)} %collective-permute-done.2.tail_ref.part_ref, ...), custom_call_target="tpu_custom_call" | custom-call | tf_op jit(solution)/shard_map/place/pallas_call | solution.py:427
  54.4 9.0 %final.1 = bf16[256,4096]{1,0:T(8,128)(2,1)} custom-call(s32[3]{0:T(128)S(1)} %get-tuple-element.36.scal, f32[256,4096]{1,0:T(8,128)S(1)} %get-tuple-element.37.q_ref, f32[256,4096]{1,0:T(8,128)S(1)} %near.1.z_ref, f32[144,4096]{1,0:T(8,128)S(1)} %get-tuple-element.47.qt_ref, f32[144,4096]{1,0:T(8,128)S(1)} %get-tuple-element.48.zt_ref, ...), custom_call_target="tpu_custom_call" | custom-call | flops 100000000 | bytes 65536 | tf_op jit(solution)/shard_map/final/pallas_call | solution.py:477
  (13 shorter events, 0.2 us)
Async XLA Ops:
  0.7 0.9 %copy-start.1 = (f32[3,3,4096]{2,1,0:T(4,128)S(1)}, f32[3,3,4096]{2,1,0:T(4,128)}, u32[]{:S(2)}) copy-start(f32[3,3,4096]{2,1,0:T(4,128)} %w_ref.2) | copy-start | bytes 442372
  1.6 0.7 %copy-start.2 = (f32[8,16]{1,0:T(8,128)S(1)}, f32[8,16]{1,0:T(8,128)}, u32[]{:S(2)}) copy-start(f32[8,16]{1,0:T(8,128)} %dec_ref.3) | copy-start | bytes 1540
  3.9 6.4 %collective-permute-start = (bf16[3,4096]{1,0:T(4,128)(2,1)S(1)}, bf16[3,4096]{1,0:T(4,128)(2,1)S(1)}, u32[]{:S(2)}, u32[]{:S(2)}) collective-permute-start(bf16[3,4096]{1,0:T(4,128)(2,1)S(1)} %get-tuple-element.33), channel_id=1, source_target_pairs={{0,2},{2,4},{4,6},{6,8},{8,10},{10,12},{12,14},{1,3},{3,5},{5,7},{... | collective-permute-start | bytes 73736 | tf_op jit(solution)/shard_map/ppermute | solution.py:349
  14.7 5.4 %collective-permute-start.1 = (bf16[16,4224]{1,0:T(8,128)(2,1)S(1)}, bf16[16,4224]{1,0:T(8,128)(2,1)S(1)}, u32[]{:S(2)}, u32[]{:S(2)}) collective-permute-start(bf16[16,4224]{1,0:T(8,128)(2,1)S(1)} %get-tuple-element.41.mine_ref), channel_id=1, source_target_pairs={{0,2},{2,0},{4,6},{6,4},{8,10},{10,8},{12,14},{14,12},{1,3},{3,1},... | collective-permute-start | bytes 405512 | tf_op jit(solution)/shard_map/ppermute | solution.py:399
  20.4 19.9 %copy-start.4 = (bf16[8,128]{1,0:T(8,128)(2,1)S(1)}, bf16[8,128]{1,0:T(8,128)(2,1)}, u32[]{:S(2)}) copy-start(bf16[8,128]{1,0:T(8,128)(2,1)} %param.13) | copy-start | bytes 6148
  20.4 19.9 %copy-start.3 = (f32[8,16]{1,0:T(8,128)S(1)}, f32[8,16]{1,0:T(8,128)}, u32[]{:S(2)}) copy-start(f32[8,16]{1,0:T(8,128)} %res_ref.1) | copy-start | bytes 1540
  20.5 29.6 %collective-permute-start.2 = (bf16[147,4096]{1,0:T(8,128)(2,1)S(1)}, bf16[147,4096]{1,0:T(8,128)(2,1)S(1)}, u32[]{:S(2)}, u32[]{:S(2)}) collective-permute-start(bf16[147,4096]{1,0:T(8,128)(2,1)S(1)} %pad_maximum_fusion), channel_id=1, source_target_pairs={{0,2},{2,4},{4,6},{6,8},{8,10},{10,12},{12,14},{1,3},{3,5},{5,7},{... | collective-permute-start | bytes 3612680 | tf_op jit(solution)/shard_map/ppermute | solution.py:349
  25.3 13.2 %collective-permute-start.3 = (bf16[32,4224]{1,0:T(8,128)(2,1)S(1)}, bf16[32,4224]{1,0:T(8,128)(2,1)S(1)}, u32[]{:S(2)}, u32[]{:S(2)}) collective-permute-start(bf16[32,4224]{1,0:T(8,128)(2,1)S(1)} %pair.1), channel_id=1, source_target_pairs={{0,4},{4,8},{8,12},{1,5},{5,9},{9,13},{16,20},{20,24},{24,28},{17,... | collective-permute-start | bytes 811016 | tf_op jit(solution)/shard_map/ppermute | solution.py:412
  28.7 8.3 %collective-permute-start.4 = (bf16[16,4224]{1,0:T(8,128)(2,1)S(1)}, bf16[16,4224]{1,0:T(8,128)(2,1)S(1)}, u32[]{:S(2)}, u32[]{:S(2)}) collective-permute-start(bf16[16,4224]{1,0:T(8,128)(2,1)S(1)} %slice.9), channel_id=1, source_target_pairs={{0,8},{4,12},{1,9},{5,13},{16,24},{20,28},{17,25},{21,29}} | collective-permute-start | bytes 405512 | tf_op jit(solution)/shard_map/ppermute | solution.py:414
  33.2 5.2 %collective-permute-start.5 = (bf16[16,4224]{1,0:T(8,128)(2,1)S(1)}, bf16[16,4224]{1,0:T(8,128)(2,1)S(1)}, u32[]{:S(2)}, u32[]{:S(2)}) collective-permute-start(bf16[16,4224]{1,0:T(8,128)(2,1)S(1)} %slice.9), channel_id=1, source_target_pairs={{0,12},{1,13},{16,28},{17,29}} | collective-permute-start | bytes 405512 | tf_op jit(solution)/shard_map/ppermute | solution.py:414
  38.7 14.8 %collective-permute-start.6 = (bf16[16,4096]{1,0:T(8,128)(2,1)S(1)}, bf16[16,4096]{1,0:T(8,128)(2,1)S(1)}, u32[]{:S(2)}, u32[]{:S(2)}) collective-permute-start(bf16[16,4096]{1,0:T(8,128)(2,1)S(1)} %get-tuple-element.52), channel_id=1, source_target_pairs={{0,2},{4,6},{8,10},{12,14},{1,3},{5,7},{9,11},{13,15},{16,18},{20,... | collective-permute-start | bytes 393224 | tf_op jit(solution)/shard_map/ppermute | solution.py:426
  50.2 4.2 %copy-start = (f32[3,3,4096]{2,1,0:T(4,128)S(1)}, f32[3,3,4096]{2,1,0:T(4,128)}, u32[]{:S(2)}) copy-start(f32[3,3,4096]{2,1,0:T(4,128)} %w_ref.3) | copy-start | bytes 442372

commit v5 on v4

--- a/solution.py
+++ b/solution.py
@@ -216,7 +216,7 @@
 
 
 def tables_kernel(cut, modes, length, scal, dec_ref, res_ref, mr_ref, *outs):
-    t_own, t_win, r_own, r_win, b_win, b_own = outs
+    t_own, t_win, r_own, r_win, b_all = outs
     g = pl.program_id(0)
     own, prior = scal[0], scal[1]
     wide = 2 * length
@@ -259,13 +259,14 @@
     o, n = iota((count, wide), 0), iota((count, wide), 1)
     back = dot(mr_ref[...], one(((n == 0) & (o == 0)) | ((n > 0) & (wide - n == o))))
     band = pltpu.roll(
-        jnp.broadcast_to(back, (WIN + length, wide)), 0, 1, stride=1, stride_axis=0
-    )
-    seen = (p <= t) & ((p >= own) == (t >= own))
-    b_own[...] = jnp.where(seen, band[:length, :length], 0.0).astype(BF)
-    tb, pb = iota((length, WIN), 0), iota((length, WIN), 1) + base
-    seen = (tb < own) & ((prior >= length) | (pb >= prior))
-    b_win[...] = jnp.where(seen, band[WIN : WIN + length, :WIN], 0.0).astype(BF)
+        jnp.broadcast_to(back, (2 * count, wide)), 0, 1, stride=1, stride_axis=0
+    )[count:, : 2 * count]
+    for first in range(0, length, count):
+        t = iota((count, 2 * count), 0) + first
+        p = iota((count, 2 * count), 1) + (first - count)
+        same = (p >= own) == (t >= own)
+        early = (p >= 0) | (prior >= length) | (p + length >= prior)
+        b_all[first : first + count, :] = jnp.where(same & early, band, 0.0).astype(BF)
 
 
 def tail_kernel(
@@ -301,7 +302,7 @@
 
 def final_kernel(
     lanes, scal, q_ref, z_ref, qt_ref, zt_ref, r_ref, rt_ref, st_ref, stt_ref,
-    w_ref, bt_ref, b_ref, out_ref, mask_ref, w_scr, q_scr, z_scr, o_scr, sems,
+    w_ref, b_ref, out_ref, mask_ref, w_scr, q_scr, z_scr, o_scr, sems,
 ):
     length = q_ref.shape[0]
 
@@ -328,8 +329,11 @@
                 ws[at, tile] = (combine(w[1], taps) * combine(w[2], taps)).astype(BF)
                 if at.start >= WIN:
                     qs[at.start - WIN : at.stop - WIN, tile] = combine(w[0], taps)
-        z = dot(bt_ref[i], ws[:WIN, :]) + dot(b_ref[i], ws[WIN:, :])
-        o_scr[i] = (qs[...] * z).astype(BF)
+        span = b_ref.shape[2] // 2
+        for first in range(0, length, span):
+            rows = slice(first, first + span)
+            z = dot(b_ref[i, rows, :], ws[WIN + first - span : WIN + first + span, :])
+            o_scr[i, rows, :] = (qs[rows, :] * z).astype(BF)
         copies.append(pltpu.make_async_copy(o_scr.at[i], out_ref.at[:, cols], sems.at[i]))
         copies[-1].start()
     for copy in copies:
@@ -435,9 +439,9 @@
 
     shapes = [
         (2 * length, length), (2 * WIN, WIN), (length, 3 * modes), (WIN, 3 * modes),
-        (length, WIN), (length, length),
+        (length, 2 * filter_len),
     ]
-    t_own, t_win, r_own, r_win, b_win, b_own = pl.pallas_call(
+    t_own, t_win, r_own, r_win, b_all = pl.pallas_call(
         functools.partial(tables_kernel, cut, modes, length),
         grid=(groups,),
         in_specs=[sm, fixed(groups, modes), fixed(groups, modes), single(1, filter_len)],
@@ -476,7 +480,7 @@
     full = WIN + length
     return pl.pallas_call(
         functools.partial(final_kernel, lanes),
-        in_specs=[sm] + [whole] * 11,
+        in_specs=[sm] + [whole] * 10,
         out_specs=pl.BlockSpec(memory_space=pl.ANY),
         out_shape=jax.ShapeDtypeStruct((length, channels), BF),
         scratch_shapes=[
@@ -490,7 +494,7 @@
         name="final",
     )(
         scal, q_own, z_own, q_win, z_win, r_own, r_win, own_state, win_state,
-        feat_second, b_win, b_own,
+        feat_second, b_all,
     )
 
 

time: 63.9 us -> 63.1 us (0.987)
  Pallas kernels: 25.7 us -> 24.8 us
    pallas_call x1, Pallas kernels: 9.03 us -> 8.23 us  [per_device(): pl.pallas_call(functools.partial(final_kernel, lanes), in_specs=[sm] + [w...]
where the time goes in v5:
time: 63.1 us; the launch traced here: 62.8 us
  Pallas kernels  24.8 us (39%)
  starting transfers between devices  21.9 us (35%)
  waiting for transfers between devices  13 us (21%)
  local copies, waits for them, and re-layouts  1.91 us (3%)
  between operations  1.01 us (2%)
    ppermute x2, starting transfers between devices, behind(): return lax.ppermute(array, 'seq', [(i, i + by) for i in range(size - by)])  8.85 us
    pallas_call x1, Pallas kernels, per_device(): pl.pallas_call(functools.partial(final_kernel, lanes), in_specs=[sm] + [w...  8.23 us
    ppermute x2, waiting for transfers between devices, behind(): return lax.ppermute(array, 'seq', [(i, i + by) for i in range(size - by)])  6.06 us
    ppermute x2, starting transfers between devices, per_device(): lax.ppermute(pair[:modes], 'seq', [(i, i + by) for i in range(0, size - b...  5.79 us
    pallas_call x1, Pallas kernels, per_device(): pl.pallas_call(functools.partial(states_kernel, cut, modes, lanes), in_sp...  4.35 us
    pallas_call x1, Pallas kernels, per_device(): pl.pallas_call(functools.partial(tables_kernel, cut, modes, length), grid...  4.18 us
    ppermute x2, waiting for transfers between devices, per_device(): lax.ppermute(pair[:modes], 'seq', [(i, i + by) for i in range(0, size - b...  3.91 us
    ppermute x1, starting transfers between devices, per_device(): lax.ppermute(pair, 'seq', [(i, i + 2) for i in range(0, size - 2, 2)])  3.42 us
  transfers between devices with their start and end apart: 7, of which 5 were waited for; matrix products, arithmetic and copies ran while one was open for 0% of the time, Pallas kernels for 16%

profile of v5, /device:TPU:0, one launch (start us, length us, event | category | flops | bytes accessed | tf_op | source)
XLA Modules:
  0.0 62.8 jit_solution(616733465574763710)
XLA Ops:
  0.7 0.9 %copy-done = f32[3,3,4096]{2,1,0:T(4,128)S(1)} copy-done((f32[3,3,4096]{2,1,0:T(4,128)S(1)}, f32[3,3,4096]{2,1,0:T(4,128)}, u32[]{:S(2)}) %copy-start) | copy-done | bytes 147480
  1.6 0.7 %copy-done.2 = f32[8,16]{1,0:T(8,128)S(1)} copy-done((f32[8,16]{1,0:T(8,128)S(1)}, f32[8,16]{1,0:T(8,128)}, u32[]{:S(2)}) %copy-start.2) | copy-done | bytes 536
  2.3 1.6 %load.1 = (bf16[256,4096]{1,0:T(8,128)(2,1)S(1)}, f32[3,3,4096]{2,1,0:T(4,128)S(1)}, f32[8,16]{1,0:T(8,128)S(1)}, bf16[3,4096]{1,0:T(4,128)(2,1)S(1)}) custom-call(s32[1]{0:T(128)S(6)} %copy.9.bounds, bf16[256,4096]{1,0:T(8,128)(2,1)} %x_ref.1, f32[3,3,4096]{2,1,0:T(4,128)S(1)} %copy-done, f32[8,16]{1,0:T(8,128)S(1)} %copy-done.2), custom_call_target="tpu_custom_call" | custom-call | tf_op jit(solution)/shard_map/load/pallas_call | solution.py:362
  3.9 4.8 %collective-permute-start = (bf16[3,4096]{1,0:T(4,128)(2,1)S(1)}, bf16[3,4096]{1,0:T(4,128)(2,1)S(1)}, u32[]{:S(2)}, u32[]{:S(2)}) collective-permute-start(bf16[3,4096]{1,0:T(4,128)(2,1)S(1)} %get-tuple-element.32), channel_id=1, source_target_pairs={{0,2},{2,4},{4,6},{6,8},{8,10},{10,12},{12,14},{1,3},{3,5},{5,7},{... | collective-permute-start | bytes 73736 | tf_op jit(solution)/shard_map/ppermute | solution.py:353
  8.8 1.6 %collective-permute-done.edge_ref = bf16[3,4096]{1,0:T(4,128)(2,1)S(1)} collective-permute-done((bf16[3,4096]{1,0:T(4,128)(2,1)S(1)}, bf16[3,4096]{1,0:T(4,128)(2,1)S(1)}, u32[]{:S(2)}, u32[]{:S(2)}) %collective-permute-start) | collective-permute-done | bytes 24608 | tf_op jit(solution)/shard_map/ppermute | solution.py:353
  10.4 4.3 %states.1 = (bf16[16,4224]{1,0:T(8,128)(2,1)S(1)}, bf16[16,4096]{1,0:T(8,128)(2,1)S(1)}, f32[256,4096]{1,0:T(8,128)S(1)}, bf16[256,4096]{1,0:T(8,128)(2,1)S(1)}, s32[3]{0:T(128)S(1)}) custom-call(s32[1]{0:T(128)S(6)} %copy.9.bounds, bf16[256,4096]{1,0:T(8,128)(2,1)S(1)} %get-tuple-element.42.x_ref, bf16[3,4096]{1,0:T(4,128)(2,1)S(1)} %collective-permute-done.edge_ref, ...), custom_call_target="tpu_custom_call" | custom-call | flops 100000000 | bytes 65536 | tf_op jit(solution)/shard_map/states/pallas_call | solution.py:385
  14.7 2.4 %collective-permute-start.1 = (bf16[16,4224]{1,0:T(8,128)(2,1)S(1)}, bf16[16,4224]{1,0:T(8,128)(2,1)S(1)}, u32[]{:S(2)}, u32[]{:S(2)}) collective-permute-start(bf16[16,4224]{1,0:T(8,128)(2,1)S(1)} %get-tuple-element.40.mine_ref), channel_id=1, source_target_pairs={{0,2},{2,0},{4,6},{6,4},{8,10},{10,8},{12,14},{14,12},{1,3},{3,1},... | collective-permute-start | bytes 405512 | tf_op jit(solution)/shard_map/ppermute | solution.py:403
  17.1 3.0 %collective-permute-done.1.other_ref = bf16[16,4224]{1,0:T(8,128)(2,1)S(1)} collective-permute-done((bf16[16,4224]{1,0:T(8,128)(2,1)S(1)}, bf16[16,4224]{1,0:T(8,128)(2,1)S(1)}, u32[]{:S(2)}, u32[]{:S(2)}) %collective-permute-start.1) | collective-permute-done | bytes 135200 | tf_op jit(solution)/shard_map/ppermute | solution.py:403
  20.1 0.3 slice.7
  20.5 4.0 %collective-permute-start.2 = (bf16[147,4096]{1,0:T(8,128)(2,1)S(1)}, bf16[147,4096]{1,0:T(8,128)(2,1)S(1)}, u32[]{:S(2)}, u32[]{:S(2)}) collective-permute-start(bf16[147,4096]{1,0:T(8,128)(2,1)S(1)} %pad_maximum_fusion), channel_id=1, source_target_pairs={{0,2},{2,4},{4,6},{6,8},{8,10},{10,12},{12,14},{1,3},{3,5},{5,7},{... | collective-permute-start | bytes 3612680 | tf_op jit(solution)/shard_map/ppermute | solution.py:353
  24.5 0.7 %pair.1 = bf16[32,4224]{1,0:T(8,128)(2,1)S(1)} custom-call(s32[3]{0:T(128)S(1)} %get-tuple-element.35.scal, bf16[16,4224]{1,0:T(8,128)(2,1)S(1)} %get-tuple-element.40.mine_ref, bf16[16,4224]{1,0:T(8,128)(2,1)S(1)} %collective-permute-done.1.other_ref, f32[8,16]{1,0:T(8,128)S(1)} %get-tuple-element.34.dec_ref), custom_call_target="tpu_custom_call" | custom-call | tf_op jit(solution)/shard_map/pair/pallas_call | solution.py:408
  25.3 3.4 %collective-permute-start.3 = (bf16[32,4224]{1,0:T(8,128)(2,1)S(1)}, bf16[32,4224]{1,0:T(8,128)(2,1)S(1)}, u32[]{:S(2)}, u32[]{:S(2)}) collective-permute-start(bf16[32,4224]{1,0:T(8,128)(2,1)S(1)} %pair.1), channel_id=1, source_target_pairs={{0,4},{4,8},{8,12},{1,5},{5,9},{9,13},{16,20},{20,24},{24,28},{17,... | collective-permute-start | bytes 811016 | tf_op jit(solution)/shard_map/ppermute | solution.py:416
  28.7 4.5 %collective-permute-start.4 = (bf16[16,4224]{1,0:T(8,128)(2,1)S(1)}, bf16[16,4224]{1,0:T(8,128)(2,1)S(1)}, u32[]{:S(2)}, u32[]{:S(2)}) collective-permute-start(bf16[16,4224]{1,0:T(8,128)(2,1)S(1)} %slice.9), channel_id=1, source_target_pairs={{0,8},{4,12},{1,9},{5,13},{16,24},{20,28},{17,25},{21,29}} | collective-permute-start | bytes 405512 | tf_op jit(solution)/shard_map/ppermute | solution.py:418
  33.2 1.3 %collective-permute-start.5 = (bf16[16,4224]{1,0:T(8,128)(2,1)S(1)}, bf16[16,4224]{1,0:T(8,128)(2,1)S(1)}, u32[]{:S(2)}, u32[]{:S(2)}) collective-permute-start(bf16[16,4224]{1,0:T(8,128)(2,1)S(1)} %slice.9), channel_id=1, source_target_pairs={{0,12},{1,13},{16,28},{17,29}} | collective-permute-start | bytes 405512 | tf_op jit(solution)/shard_map/ppermute | solution.py:418
  34.5 2.5 %collective-permute-done.4.refs_0_ = bf16[16,4224]{1,0:T(8,128)(2,1)S(1)} collective-permute-done((bf16[16,4224]{1,0:T(8,128)(2,1)S(1)}, bf16[16,4224]{1,0:T(8,128)(2,1)S(1)}, u32[]{:S(2)}, u32[]{:S(2)}) %collective-permute-start.4) | collective-permute-done | bytes 135200 | tf_op jit(solution)/shard_map/ppermute | solution.py:418
  37.0 1.4 %collective-permute-done.5.refs_1_ = bf16[16,4224]{1,0:T(8,128)(2,1)S(1)} collective-permute-done((bf16[16,4224]{1,0:T(8,128)(2,1)S(1)}, bf16[16,4224]{1,0:T(8,128)(2,1)S(1)}, u32[]{:S(2)}, u32[]{:S(2)}) %collective-permute-start.5) | collective-permute-done | bytes 135200 | tf_op jit(solution)/shard_map/ppermute | solution.py:418
  38.4 0.3 carry.1
  38.7 1.5 %collective-permute-start.6 = (bf16[16,4096]{1,0:T(8,128)(2,1)S(1)}, bf16[16,4096]{1,0:T(8,128)(2,1)S(1)}, u32[]{:S(2)}, u32[]{:S(2)}) collective-permute-start(bf16[16,4096]{1,0:T(8,128)(2,1)S(1)} %get-tuple-element.51), channel_id=1, source_target_pairs={{0,2},{4,6},{8,10},{12,14},{1,3},{5,7},{9,11},{13,15},{16,18},{20,... | collective-permute-start | bytes 393224 | tf_op jit(solution)/shard_map/ppermute | solution.py:430
  40.2 4.2 %tables.1 = (bf16[8,512,256]{2,1,0:T(8,128)(2,1)S(1)}, bf16[8,288,144]{2,1,0:T(8,128)(2,1)S(1)}, bf16[8,256,48]{2,1,0:T(8,128)(2,1)S(1)}, bf16[8,144,48]{2,1,0:T(8,128)(2,1)S(1)}, bf16[8,256,256]{2,1,0:T(8,128)(2,1)S(1)}) custom-call(s32[3]{0:T(128)S(1)} %get-tuple-element.35.scal, f32[8,16]{1,0:T(8,128)S(1)} %copy-done.2, f32[8,16]{1,0:T(8,128)S(1)} %copy-done.3, ...), custom_call_target="tpu_custom_call" | custom-call | flops 100000000 | bytes 65536 | tf_op jit(solution)/shard_map/tables/pallas_call | solution.py:444
  44.4 1.2 %near.1.z_ref = f32[256,4096]{1,0:T(8,128)S(1)} custom-call(bf16[256,4096]{1,0:T(8,128)(2,1)S(1)} %get-tuple-element.37.u_ref, bf16[8,512,256]{2,1,0:T(8,128)(2,1)S(1)} %get-tuple-element.38.t_ref), custom_call_target="tpu_custom_call" | custom-call | flops 100000000 | bytes 65536 | tf_op jit(solution)/shard_map/near/pallas_call | solution.py:455
  45.7 4.5 %collective-permute-done.2.tail_ref.part_ref = bf16[147,4096]{1,0:T(8,128)(2,1)S(1)} collective-permute-done((bf16[147,4096]{1,0:T(8,128)(2,1)S(1)}, bf16[147,4096]{1,0:T(8,128)(2,1)S(1)}, u32[]{:S(2)}, u32[]{:S(2)}) %collective-permute-start.2) | collective-permute-done | bytes 1204256 | tf_op jit(solution)/shard_map/ppermute | solution.py:353
  50.2 3.4 %tail.1 = (f32[144,4096]{1,0:T(8,128)S(1)}, f32[144,4096]{1,0:T(8,128)S(1)}) custom-call(s32[3]{0:T(128)S(1)} %get-tuple-element.35.scal, bf16[147,4096]{1,0:T(8,128)(2,1)S(1)} %collective-permute-done.2.tail_ref.part_ref, f32[3,3,4096]{2,1,0:T(4,128)S(1)} %get-tuple-element.33.w_ref, bf16[8,288,144]{2,1,0:T(8,128)(2,1)S(1)} %get-tuple-element.45.t_ref), custom_call_target="tpu_custom_call" | custom-call | flops 100000000 | bytes 65536 | tf_op jit(solution)/shard_map/tail/pallas_call | solution.py:464
  53.6 0.8 %place.1 = (bf16[48,4096]{1,0:T(8,128)(2,1)S(1)}, bf16[48,4096]{1,0:T(8,128)(2,1)S(1)}) custom-call(s32[3]{0:T(128)S(1)} %get-tuple-element.35.scal, bf16[16,4224]{1,0:T(8,128)(2,1)S(1)} %collective-permute-done.1.other_ref, bf16[147,4096]{1,0:T(8,128)(2,1)S(1)} %collective-permute-done.2.tail_ref.part_ref, ...), custom_call_target="tpu_custom_call" | custom-call | tf_op jit(solution)/shard_map/place/pallas_call | solution.py:431
  54.4 8.2 %final.1 = bf16[256,4096]{1,0:T(8,128)(2,1)} custom-call(s32[3]{0:T(128)S(1)} %get-tuple-element.35.scal, f32[256,4096]{1,0:T(8,128)S(1)} %get-tuple-element.36.q_ref, f32[256,4096]{1,0:T(8,128)S(1)} %near.1.z_ref, f32[144,4096]{1,0:T(8,128)S(1)} %get-tuple-element.46.qt_ref, f32[144,4096]{1,0:T(8,128)S(1)} %get-tuple-element.47.zt_ref, ...), custom_call_target="tpu_custom_call" | custom-call | flops 100000000 | bytes 65536 | tf_op jit(solution)/shard_map/final/pallas_call | solution.py:481
  (13 shorter events, 0.2 us)
Async XLA Ops:
  0.7 0.9 %copy-start = (f32[3,3,4096]{2,1,0:T(4,128)S(1)}, f32[3,3,4096]{2,1,0:T(4,128)}, u32[]{:S(2)}) copy-start(f32[3,3,4096]{2,1,0:T(4,128)} %w_ref.2) | copy-start | bytes 442372
  1.6 0.7 %copy-start.2 = (f32[8,16]{1,0:T(8,128)S(1)}, f32[8,16]{1,0:T(8,128)}, u32[]{:S(2)}) copy-start(f32[8,16]{1,0:T(8,128)} %dec_ref.3) | copy-start | bytes 1540
  3.9 6.4 %collective-permute-start = (bf16[3,4096]{1,0:T(4,128)(2,1)S(1)}, bf16[3,4096]{1,0:T(4,128)(2,1)S(1)}, u32[]{:S(2)}, u32[]{:S(2)}) collective-permute-start(bf16[3,4096]{1,0:T(4,128)(2,1)S(1)} %get-tuple-element.32), channel_id=1, source_target_pairs={{0,2},{2,4},{4,6},{6,8},{8,10},{10,12},{12,14},{1,3},{3,5},{5,7},{... | collective-permute-start | bytes 73736 | tf_op jit(solution)/shard_map/ppermute | solution.py:353
  14.7 5.4 %collective-permute-start.1 = (bf16[16,4224]{1,0:T(8,128)(2,1)S(1)}, bf16[16,4224]{1,0:T(8,128)(2,1)S(1)}, u32[]{:S(2)}, u32[]{:S(2)}) collective-permute-start(bf16[16,4224]{1,0:T(8,128)(2,1)S(1)} %get-tuple-element.40.mine_ref), channel_id=1, source_target_pairs={{0,2},{2,0},{4,6},{6,4},{8,10},{10,8},{12,14},{14,12},{1,3},{3,1},... | collective-permute-start | bytes 405512 | tf_op jit(solution)/shard_map/ppermute | solution.py:403
  20.4 19.9 %copy-start.4 = (bf16[8,128]{1,0:T(8,128)(2,1)S(1)}, bf16[8,128]{1,0:T(8,128)(2,1)}, u32[]{:S(2)}) copy-start(bf16[8,128]{1,0:T(8,128)(2,1)} %param.13) | copy-start | bytes 6148
  20.4 19.9 %copy-start.3 = (f32[8,16]{1,0:T(8,128)S(1)}, f32[8,16]{1,0:T(8,128)}, u32[]{:S(2)}) copy-start(f32[8,16]{1,0:T(8,128)} %res_ref.1) | copy-start | bytes 1540
  20.5 29.7 %collective-permute-start.2 = (bf16[147,4096]{1,0:T(8,128)(2,1)S(1)}, bf16[147,4096]{1,0:T(8,128)(2,1)S(1)}, u32[]{:S(2)}, u32[]{:S(2)}) collective-permute-start(bf16[147,4096]{1,0:T(8,128)(2,1)S(1)} %pad_maximum_fusion), channel_id=1, source_target_pairs={{0,2},{2,4},{4,6},{6,8},{8,10},{10,12},{12,14},{1,3},{3,5},{5,7},{... | collective-permute-start | bytes 3612680 | tf_op jit(solution)/shard_map/ppermute | solution.py:353
  25.3 13.2 %collective-permute-start.3 = (bf16[32,4224]{1,0:T(8,128)(2,1)S(1)}, bf16[32,4224]{1,0:T(8,128)(2,1)S(1)}, u32[]{:S(2)}, u32[]{:S(2)}) collective-permute-start(bf16[32,4224]{1,0:T(8,128)(2,1)S(1)} %pair.1), channel_id=1, source_target_pairs={{0,4},{4,8},{8,12},{1,5},{5,9},{9,13},{16,20},{20,24},{24,28},{17,... | collective-permute-start | bytes 811016 | tf_op jit(solution)/shard_map/ppermute | solution.py:416
  28.7 8.3 %collective-permute-start.4 = (bf16[16,4224]{1,0:T(8,128)(2,1)S(1)}, bf16[16,4224]{1,0:T(8,128)(2,1)S(1)}, u32[]{:S(2)}, u32[]{:S(2)}) collective-permute-start(bf16[16,4224]{1,0:T(8,128)(2,1)S(1)} %slice.9), channel_id=1, source_target_pairs={{0,8},{4,12},{1,9},{5,13},{16,24},{20,28},{17,25},{21,29}} | collective-permute-start | bytes 405512 | tf_op jit(solution)/shard_map/ppermute | solution.py:418
  33.2 5.2 %collective-permute-start.5 = (bf16[16,4224]{1,0:T(8,128)(2,1)S(1)}, bf16[16,4224]{1,0:T(8,128)(2,1)S(1)}, u32[]{:S(2)}, u32[]{:S(2)}) collective-permute-start(bf16[16,4224]{1,0:T(8,128)(2,1)S(1)} %slice.9), channel_id=1, source_target_pairs={{0,12},{1,13},{16,28},{17,29}} | collective-permute-start | bytes 405512 | tf_op jit(solution)/shard_map/ppermute | solution.py:418
  38.7 14.8 %collective-permute-start.6 = (bf16[16,4096]{1,0:T(8,128)(2,1)S(1)}, bf16[16,4096]{1,0:T(8,128)(2,1)S(1)}, u32[]{:S(2)}, u32[]{:S(2)}) collective-permute-start(bf16[16,4096]{1,0:T(8,128)(2,1)S(1)} %get-tuple-element.51), channel_id=1, source_target_pairs={{0,2},{4,6},{8,10},{12,14},{1,3},{5,7},{9,11},{13,15},{16,18},{20,... | collective-permute-start | bytes 393224 | tf_op jit(solution)/shard_map/ppermute | solution.py:430
  50.2 4.2 %copy-start.1 = (f32[3,3,4096]{2,1,0:T(4,128)S(1)}, f32[3,3,4096]{2,1,0:T(4,128)}, u32[]{:S(2)}) copy-start(f32[3,3,4096]{2,1,0:T(4,128)} %w_ref.3) | copy-start | bytes 442372

commit v6 on v5

--- a/solution.py
+++ b/solution.py
@@ -88,13 +88,10 @@
     return hi, (v - hi.astype(F32)).astype(BF)
 
 
-def load_kernel(bounds, x_ref, w_ref, dec_ref, x_out, w_out, dec_out, edge_out, sems):
-    pairs = ((x_ref, x_out), (w_ref, w_out), (dec_ref, dec_out))
-    copies = [pltpu.make_async_copy(a, b, sems.at[i]) for i, (a, b) in enumerate(pairs)]
-    for copy in copies:
-        copy.start()
-    for copy in copies:
-        copy.wait()
+def load_kernel(bounds, x_ref, x_out, edge_out, sem):
+    copy = pltpu.make_async_copy(x_ref, x_out, sem)
+    copy.start()
+    copy.wait()
     length, width = x_out.shape
     last = x_out[length - 16 :, :].astype(F32)[14:]
     own = jnp.full((1, width), bounds[0], jnp.int32).astype(F32)
@@ -359,16 +356,17 @@
     steps, wide = groups // count, lanes * count
 
     hbm = pl.BlockSpec(memory_space=pl.ANY)
-    held, held_first, held_decay, edge = pl.pallas_call(
+    held, edge = pl.pallas_call(
         load_kernel,
-        in_specs=[sm] + [hbm] * 3,
-        out_specs=[whole] * 4,
-        out_shape=[jax.ShapeDtypeStruct(a.shape, a.dtype) for a in (inputs, feat_first, li_decay)]
-        + [jax.ShapeDtypeStruct((3, channels), BF)],
-        scratch_shapes=[pltpu.SemaphoreType.DMA((3,))],
+        in_specs=[sm, hbm],
+        out_specs=[whole] * 2,
+        out_shape=[
+            jax.ShapeDtypeStruct(inputs.shape, BF), jax.ShapeDtypeStruct((3, channels), BF),
+        ],
+        scratch_shapes=[pltpu.SemaphoreType.DMA],
         compiler_params=pltpu.CompilerParams(vmem_limit_bytes=50 * 1024 * 1024),
         name="load",
-    )(bounds, inputs, feat_first, li_decay)
+    )(bounds, inputs)
     edge = behind(edge, 1)
     def block(*shape):
         return pl.BlockSpec(shape, lambda g: (0,) * (len(shape) - 1) + (g,))
@@ -399,7 +397,7 @@
         compiler_params=params,
         cost_estimate=pl.CostEstimate(flops=10**8, bytes_accessed=2**16, transcendentals=0),
         name="states",
-    )(bounds, held, edge, held_first, held_decay)
+    )(bounds, held, edge, feat_first, li_decay)
     other = lax.ppermute(mine, "seq", [(i, i ^ 1) for i in range(size)])
     inputs_late, part, other = lax.optimization_barrier((held, part, other))
     message = jnp.concatenate([part, inputs_late[length - rows :]], 0)
@@ -412,7 +410,7 @@
         out_shape=jax.ShapeDtypeStruct((2 * modes, channels + LANE), BF),
         compiler_params=params,
         name="pair",
-    )(scal, mine, other, held_decay)
+    )(scal, mine, other, li_decay)
     near = lax.ppermute(pair, "seq", [(i, i + 2) for i in range(0, size - 2, 2)])
     far = [
         lax.ppermute(pair[:modes], "seq", [(i, i + by) for i in range(0, size - by, 2)])
@@ -426,7 +424,7 @@
         out_shape=[jax.ShapeDtypeStruct((modes, channels), BF), state_shape, state_shape],
         compiler_params=params,
         name="carry",
-    )(near, held_decay, *far)
+    )(near, li_decay, *far)
     sent = lax.ppermute(send, "seq", [(i, i + 1) for i in range(0, size, 2)])
     own_state, win_state = pl.pallas_call(
         functools.partial(place_kernel, cut, modes, length),
@@ -435,7 +433,7 @@
         out_shape=[jax.ShapeDtypeStruct((3 * modes, channels), BF)] * 2,
         compiler_params=params,
         name="place",
-    )(scal, other, tail, sent, even_own, even_late, held_decay)
+    )(scal, other, tail, sent, even_own, even_late, li_decay)
 
     shapes = [
         (2 * length, length), (2 * WIN, WIN), (length, 3 * modes), (WIN, 3 * modes),
@@ -476,7 +474,7 @@
         compiler_params=params,
         cost_estimate=pl.CostEstimate(flops=10**8, bytes_accessed=2**16, transcendentals=0),
         name="tail",
-    )(scal, tail, held_first, t_win)
+    )(scal, tail, feat_first, t_win)
     full = WIN + length
     return pl.pallas_call(
         functools.partial(final_kernel, lanes),

time: 63.1 us -> 61.4 us (0.973)
  local copies, waits for them, and re-layouts: 1.91 us -> 0.33 us
    unnamed x10, local copies, waits for them, and re-layouts: 1.62 us -> 0.02 us
where the time goes in v6:
time: 61.4 us; the launch traced here: 61.1 us
  Pallas kernels  24.7 us (40%)
  starting transfers between devices  21.9 us (36%)
  waiting for transfers between devices  13 us (21%)
  between operations  1.04 us (2%)
    ppermute x2, starting transfers between devices, behind(): return lax.ppermute(array, 'seq', [(i, i + by) for i in range(size - by)])  8.85 us
    pallas_call x1, Pallas kernels, per_device(): pl.pallas_call(functools.partial(final_kernel, lanes), in_specs=[sm] + [w...  8.23 us
    ppermute x2, waiting for transfers between devices, behind(): return lax.ppermute(array, 'seq', [(i, i + by) for i in range(size - by)])  6.06 us
    ppermute x2, starting transfers between devices, per_device(): lax.ppermute(pair[:modes], 'seq', [(i, i + by) for i in range(0, size - b...  5.78 us
    pallas_call x1, Pallas kernels, per_device(): pl.pallas_call(functools.partial(states_kernel, cut, modes, lanes), in_sp...  4.28 us
    pallas_call x1, Pallas kernels, per_device(): pl.pallas_call(functools.partial(tables_kernel, cut, modes, length), grid...  4.18 us
    ppermute x2, waiting for transfers between devices, per_device(): lax.ppermute(pair[:modes], 'seq', [(i, i + by) for i in range(0, size - b...  3.92 us
    ppermute x1, starting transfers between devices, per_device(): lax.ppermute(pair, 'seq', [(i, i + 2) for i in range(0, size - 2, 2)])  3.42 us
  transfers between devices with their start and end apart: 7, of which 5 were waited for; matrix products, arithmetic and copies ran while one was open for 0% of the time, Pallas kernels for 16%

profile of v6, /device:TPU:0, one launch (start us, length us, event | category | flops | bytes accessed | tf_op | source)
XLA Modules:
  0.0 61.1 jit_solution(895011442312697104)
XLA Ops:
  0.7 1.6 %load.1 = (bf16[256,4096]{1,0:T(8,128)(2,1)S(1)}, bf16[3,4096]{1,0:T(4,128)(2,1)S(1)}) custom-call(s32[1]{0:T(128)S(6)} %copy.9.bounds, bf16[256,4096]{1,0:T(8,128)(2,1)} %x_ref.1), custom_call_target="tpu_custom_call" | custom-call | tf_op jit(solution)/shard_map/load/pallas_call | solution.py:359
  2.3 4.8 %collective-permute-start = (bf16[3,4096]{1,0:T(4,128)(2,1)S(1)}, bf16[3,4096]{1,0:T(4,128)(2,1)S(1)}, u32[]{:S(2)}, u32[]{:S(2)}) collective-permute-start(bf16[3,4096]{1,0:T(4,128)(2,1)S(1)} %get-tuple-element.30), channel_id=1, source_target_pairs={{0,2},{2,4},{4,6},{6,8},{8,10},{10,12},{12,14},{1,3},{3,5},{5,7},{... | collective-permute-start | bytes 73736 | tf_op jit(solution)/shard_map/ppermute | solution.py:350
  7.2 1.6 %collective-permute-done.edge_ref = bf16[3,4096]{1,0:T(4,128)(2,1)S(1)} collective-permute-done((bf16[3,4096]{1,0:T(4,128)(2,1)S(1)}, bf16[3,4096]{1,0:T(4,128)(2,1)S(1)}, u32[]{:S(2)}, u32[]{:S(2)}) %collective-permute-start) | collective-permute-done | bytes 24608 | tf_op jit(solution)/shard_map/ppermute | solution.py:350
  8.8 4.3 %states.1 = (bf16[16,4224]{1,0:T(8,128)(2,1)S(1)}, bf16[16,4096]{1,0:T(8,128)(2,1)S(1)}, f32[256,4096]{1,0:T(8,128)S(1)}, bf16[256,4096]{1,0:T(8,128)(2,1)S(1)}, s32[3]{0:T(128)S(1)}) custom-call(s32[1]{0:T(128)S(6)} %copy.9.bounds, bf16[256,4096]{1,0:T(8,128)(2,1)S(1)} %get-tuple-element.38.x_ref, bf16[3,4096]{1,0:T(4,128)(2,1)S(1)} %collective-permute-done.edge_ref, ...), custom_call_target="tpu_custom_call" | custom-call | flops 100000000 | bytes 65536 | tf_op jit(solution)/shard_map/states/pallas_call | solution.py:383
  13.1 2.4 %collective-permute-start.1 = (bf16[16,4224]{1,0:T(8,128)(2,1)S(1)}, bf16[16,4224]{1,0:T(8,128)(2,1)S(1)}, u32[]{:S(2)}, u32[]{:S(2)}) collective-permute-start(bf16[16,4224]{1,0:T(8,128)(2,1)S(1)} %get-tuple-element.36.mine_ref), channel_id=1, source_target_pairs={{0,2},{2,0},{4,6},{6,4},{8,10},{10,8},{12,14},{14,12},{1,3},{3,1},... | collective-permute-start | bytes 405512 | tf_op jit(solution)/shard_map/ppermute | solution.py:401
  15.4 3.0 %collective-permute-done.1.other_ref = bf16[16,4224]{1,0:T(8,128)(2,1)S(1)} collective-permute-done((bf16[16,4224]{1,0:T(8,128)(2,1)S(1)}, bf16[16,4224]{1,0:T(8,128)(2,1)S(1)}, u32[]{:S(2)}, u32[]{:S(2)}) %collective-permute-start.1) | collective-permute-done | bytes 135200 | tf_op jit(solution)/shard_map/ppermute | solution.py:401
  18.4 0.3 slice.7
  18.7 0.0 copy-start.4
  18.8 0.1 pad_maximum_fusion
  18.9 4.0 %collective-permute-start.2 = (bf16[147,4096]{1,0:T(8,128)(2,1)S(1)}, bf16[147,4096]{1,0:T(8,128)(2,1)S(1)}, u32[]{:S(2)}, u32[]{:S(2)}) collective-permute-start(bf16[147,4096]{1,0:T(8,128)(2,1)S(1)} %pad_maximum_fusion), channel_id=1, source_target_pairs={{0,2},{2,4},{4,6},{6,8},{8,10},{10,12},{12,14},{1,3},{3,5},{5,7},{... | collective-permute-start | bytes 3612680 | tf_op jit(solution)/shard_map/ppermute | solution.py:350
  22.9 0.7 %pair.1 = bf16[32,4224]{1,0:T(8,128)(2,1)S(1)} custom-call(s32[3]{0:T(128)S(1)} %get-tuple-element.31.scal, bf16[16,4224]{1,0:T(8,128)(2,1)S(1)} %get-tuple-element.36.mine_ref, bf16[16,4224]{1,0:T(8,128)(2,1)S(1)} %collective-permute-done.1.other_ref, f32[8,16]{1,0:T(8,128)S(1)} %copy-done.2), custom_call_target="tpu_custom_call" | custom-call | tf_op jit(solution)/shard_map/pair/pallas_call | solution.py:406
  23.6 3.4 %collective-permute-start.3 = (bf16[32,4224]{1,0:T(8,128)(2,1)S(1)}, bf16[32,4224]{1,0:T(8,128)(2,1)S(1)}, u32[]{:S(2)}, u32[]{:S(2)}) collective-permute-start(bf16[32,4224]{1,0:T(8,128)(2,1)S(1)} %pair.1), channel_id=1, source_target_pairs={{0,4},{4,8},{8,12},{1,5},{5,9},{9,13},{16,20},{20,24},{24,28},{17,... | collective-permute-start | bytes 811016 | tf_op jit(solution)/shard_map/ppermute | solution.py:414
  27.1 4.5 %collective-permute-start.4 = (bf16[16,4224]{1,0:T(8,128)(2,1)S(1)}, bf16[16,4224]{1,0:T(8,128)(2,1)S(1)}, u32[]{:S(2)}, u32[]{:S(2)}) collective-permute-start(bf16[16,4224]{1,0:T(8,128)(2,1)S(1)} %slice.9), channel_id=1, source_target_pairs={{0,8},{4,12},{1,9},{5,13},{16,24},{20,28},{17,25},{21,29}} | collective-permute-start | bytes 405512 | tf_op jit(solution)/shard_map/ppermute | solution.py:416
  31.6 1.3 %collective-permute-start.5 = (bf16[16,4224]{1,0:T(8,128)(2,1)S(1)}, bf16[16,4224]{1,0:T(8,128)(2,1)S(1)}, u32[]{:S(2)}, u32[]{:S(2)}) collective-permute-start(bf16[16,4224]{1,0:T(8,128)(2,1)S(1)} %slice.9), channel_id=1, source_target_pairs={{0,12},{1,13},{16,28},{17,29}} | collective-permute-start | bytes 405512 | tf_op jit(solution)/shard_map/ppermute | solution.py:416
  32.9 2.5 %collective-permute-done.4.refs_0_ = bf16[16,4224]{1,0:T(8,128)(2,1)S(1)} collective-permute-done((bf16[16,4224]{1,0:T(8,128)(2,1)S(1)}, bf16[16,4224]{1,0:T(8,128)(2,1)S(1)}, u32[]{:S(2)}, u32[]{:S(2)}) %collective-permute-start.4) | collective-permute-done | bytes 135200 | tf_op jit(solution)/shard_map/ppermute | solution.py:416
  35.4 1.4 %collective-permute-done.5.refs_1_ = bf16[16,4224]{1,0:T(8,128)(2,1)S(1)} collective-permute-done((bf16[16,4224]{1,0:T(8,128)(2,1)S(1)}, bf16[16,4224]{1,0:T(8,128)(2,1)S(1)}, u32[]{:S(2)}, u32[]{:S(2)}) %collective-permute-start.5) | collective-permute-done | bytes 135200 | tf_op jit(solution)/shard_map/ppermute | solution.py:416
  36.8 0.3 carry.1
  37.1 1.5 %collective-permute-start.6 = (bf16[16,4096]{1,0:T(8,128)(2,1)S(1)}, bf16[16,4096]{1,0:T(8,128)(2,1)S(1)}, u32[]{:S(2)}, u32[]{:S(2)}) collective-permute-start(bf16[16,4096]{1,0:T(8,128)(2,1)S(1)} %get-tuple-element.47), channel_id=1, source_target_pairs={{0,2},{4,6},{8,10},{12,14},{1,3},{5,7},{9,11},{13,15},{16,18},{20,... | collective-permute-start | bytes 393224 | tf_op jit(solution)/shard_map/ppermute | solution.py:428
  38.6 4.2 %tables.1 = (bf16[8,512,256]{2,1,0:T(8,128)(2,1)S(1)}, bf16[8,288,144]{2,1,0:T(8,128)(2,1)S(1)}, bf16[8,256,48]{2,1,0:T(8,128)(2,1)S(1)}, bf16[8,144,48]{2,1,0:T(8,128)(2,1)S(1)}, bf16[8,256,256]{2,1,0:T(8,128)(2,1)S(1)}) custom-call(s32[3]{0:T(128)S(1)} %get-tuple-element.31.scal, f32[8,16]{1,0:T(8,128)S(1)} %copy-done.2, f32[8,16]{1,0:T(8,128)S(1)} %copy-done.3, ...), custom_call_target="tpu_custom_call" | custom-call | flops 100000000 | bytes 65536 | tf_op jit(solution)/shard_map/tables/pallas_call | solution.py:442
  42.8 1.3 %near.1.z_ref = f32[256,4096]{1,0:T(8,128)S(1)} custom-call(bf16[256,4096]{1,0:T(8,128)(2,1)S(1)} %get-tuple-element.33.u_ref, bf16[8,512,256]{2,1,0:T(8,128)(2,1)S(1)} %get-tuple-element.34.t_ref), custom_call_target="tpu_custom_call" | custom-call | flops 100000000 | bytes 65536 | tf_op jit(solution)/shard_map/near/pallas_call | solution.py:453
  44.1 4.5 %collective-permute-done.2.tail_ref.part_ref = bf16[147,4096]{1,0:T(8,128)(2,1)S(1)} collective-permute-done((bf16[147,4096]{1,0:T(8,128)(2,1)S(1)}, bf16[147,4096]{1,0:T(8,128)(2,1)S(1)}, u32[]{:S(2)}, u32[]{:S(2)}) %collective-permute-start.2) | collective-permute-done | bytes 1204256 | tf_op jit(solution)/shard_map/ppermute | solution.py:350
  48.5 3.4 %tail.1 = (f32[144,4096]{1,0:T(8,128)S(1)}, f32[144,4096]{1,0:T(8,128)S(1)}) custom-call(s32[3]{0:T(128)S(1)} %get-tuple-element.31.scal, bf16[147,4096]{1,0:T(8,128)(2,1)S(1)} %collective-permute-done.2.tail_ref.part_ref, f32[3,3,4096]{2,1,0:T(4,128)S(1)} %copy-done, bf16[8,288,144]{2,1,0:T(8,128)(2,1)S(1)} %get-tuple-element.41.t_ref), custom_call_target="tpu_custom_call" | custom-call | flops 100000000 | bytes 65536 | tf_op jit(solution)/shard_map/tail/pallas_call | solution.py:462
  51.9 0.8 %place.1 = (bf16[48,4096]{1,0:T(8,128)(2,1)S(1)}, bf16[48,4096]{1,0:T(8,128)(2,1)S(1)}) custom-call(s32[3]{0:T(128)S(1)} %get-tuple-element.31.scal, bf16[16,4224]{1,0:T(8,128)(2,1)S(1)} %collective-permute-done.1.other_ref, bf16[147,4096]{1,0:T(8,128)(2,1)S(1)} %collective-permute-done.2.tail_ref.part_ref, ...), custom_call_target="tpu_custom_call" | custom-call | tf_op jit(solution)/shard_map/place/pallas_call | solution.py:429
  52.7 8.2 %final.1 = bf16[256,4096]{1,0:T(8,128)(2,1)} custom-call(s32[3]{0:T(128)S(1)} %get-tuple-element.31.scal, f32[256,4096]{1,0:T(8,128)S(1)} %get-tuple-element.32.q_ref, f32[256,4096]{1,0:T(8,128)S(1)} %near.1.z_ref, f32[144,4096]{1,0:T(8,128)S(1)} %get-tuple-element.42.qt_ref, f32[144,4096]{1,0:T(8,128)S(1)} %get-tuple-element.43.zt_ref, ...), custom_call_target="tpu_custom_call" | custom-call | flops 100000000 | bytes 65536 | tf_op jit(solution)/shard_map/final/pallas_call | solution.py:479
  (13 shorter events, 0.0 us)
Async XLA Ops:
  0.0 8.8 %copy-start = (f32[3,3,4096]{2,1,0:T(4,128)S(1)}, f32[3,3,4096]{2,1,0:T(4,128)}, u32[]{:S(2)}) copy-start(f32[3,3,4096]{2,1,0:T(4,128)} %w_ref.4) | copy-start | bytes 442372
  0.0 8.8 %copy-start.2 = (f32[8,16]{1,0:T(8,128)S(1)}, f32[8,16]{1,0:T(8,128)}, u32[]{:S(2)}) copy-start(f32[8,16]{1,0:T(8,128)} %dec_ref.9) | copy-start | bytes 1540
  2.3 6.4 %collective-permute-start = (bf16[3,4096]{1,0:T(4,128)(2,1)S(1)}, bf16[3,4096]{1,0:T(4,128)(2,1)S(1)}, u32[]{:S(2)}, u32[]{:S(2)}) collective-permute-start(bf16[3,4096]{1,0:T(4,128)(2,1)S(1)} %get-tuple-element.30), channel_id=1, source_target_pairs={{0,2},{2,4},{4,6},{6,8},{8,10},{10,12},{12,14},{1,3},{3,5},{5,7},{... | collective-permute-start | bytes 73736 | tf_op jit(solution)/shard_map/ppermute | solution.py:350
  13.1 5.4 %collective-permute-start.1 = (bf16[16,4224]{1,0:T(8,128)(2,1)S(1)}, bf16[16,4224]{1,0:T(8,128)(2,1)S(1)}, u32[]{:S(2)}, u32[]{:S(2)}) collective-permute-start(bf16[16,4224]{1,0:T(8,128)(2,1)S(1)} %get-tuple-element.36.mine_ref), channel_id=1, source_target_pairs={{0,2},{2,0},{4,6},{6,4},{8,10},{10,8},{12,14},{14,12},{1,3},{3,1},... | collective-permute-start | bytes 405512 | tf_op jit(solution)/shard_map/ppermute | solution.py:401
  18.7 19.9 %copy-start.4 = (bf16[8,128]{1,0:T(8,128)(2,1)S(1)}, bf16[8,128]{1,0:T(8,128)(2,1)}, u32[]{:S(2)}) copy-start(bf16[8,128]{1,0:T(8,128)(2,1)} %param.13) | copy-start | bytes 6148
  18.7 19.9 %copy-start.3 = (f32[8,16]{1,0:T(8,128)S(1)}, f32[8,16]{1,0:T(8,128)}, u32[]{:S(2)}) copy-start(f32[8,16]{1,0:T(8,128)} %res_ref.1) | copy-start | bytes 1540
  18.9 29.7 %collective-permute-start.2 = (bf16[147,4096]{1,0:T(8,128)(2,1)S(1)}, bf16[147,4096]{1,0:T(8,128)(2,1)S(1)}, u32[]{:S(2)}, u32[]{:S(2)}) collective-permute-start(bf16[147,4096]{1,0:T(8,128)(2,1)S(1)} %pad_maximum_fusion), channel_id=1, source_target_pairs={{0,2},{2,4},{4,6},{6,8},{8,10},{10,12},{12,14},{1,3},{3,5},{5,7},{... | collective-permute-start | bytes 3612680 | tf_op jit(solution)/shard_map/ppermute | solution.py:350
  23.6 13.2 %collective-permute-start.3 = (bf16[32,4224]{1,0:T(8,128)(2,1)S(1)}, bf16[32,4224]{1,0:T(8,128)(2,1)S(1)}, u32[]{:S(2)}, u32[]{:S(2)}) collective-permute-start(bf16[32,4224]{1,0:T(8,128)(2,1)S(1)} %pair.1), channel_id=1, source_target_pairs={{0,4},{4,8},{8,12},{1,5},{5,9},{9,13},{16,20},{20,24},{24,28},{17,... | collective-permute-start | bytes 811016 | tf_op jit(solution)/shard_map/ppermute | solution.py:414
  27.1 8.3 %collective-permute-start.4 = (bf16[16,4224]{1,0:T(8,128)(2,1)S(1)}, bf16[16,4224]{1,0:T(8,128)(2,1)S(1)}, u32[]{:S(2)}, u32[]{:S(2)}) collective-permute-start(bf16[16,4224]{1,0:T(8,128)(2,1)S(1)} %slice.9), channel_id=1, source_target_pairs={{0,8},{4,12},{1,9},{5,13},{16,24},{20,28},{17,25},{21,29}} | collective-permute-start | bytes 405512 | tf_op jit(solution)/shard_map/ppermute | solution.py:416
  31.6 5.2 %collective-permute-start.5 = (bf16[16,4224]{1,0:T(8,128)(2,1)S(1)}, bf16[16,4224]{1,0:T(8,128)(2,1)S(1)}, u32[]{:S(2)}, u32[]{:S(2)}) collective-permute-start(bf16[16,4224]{1,0:T(8,128)(2,1)S(1)} %slice.9), channel_id=1, source_target_pairs={{0,12},{1,13},{16,28},{17,29}} | collective-permute-start | bytes 405512 | tf_op jit(solution)/shard_map/ppermute | solution.py:416
  37.1 14.8 %collective-permute-start.6 = (bf16[16,4096]{1,0:T(8,128)(2,1)S(1)}, bf16[16,4096]{1,0:T(8,128)(2,1)S(1)}, u32[]{:S(2)}, u32[]{:S(2)}) collective-permute-start(bf16[16,4096]{1,0:T(8,128)(2,1)S(1)} %get-tuple-element.47), channel_id=1, source_target_pairs={{0,2},{4,6},{8,10},{12,14},{1,3},{5,7},{9,11},{13,15},{16,18},{20,... | collective-permute-start | bytes 393224 | tf_op jit(solution)/shard_map/ppermute | solution.py:428
  48.5 4.2 %copy-start.1 = (f32[3,3,4096]{2,1,0:T(4,128)S(1)}, f32[3,3,4096]{2,1,0:T(4,128)}, u32[]{:S(2)}) copy-start(f32[3,3,4096]{2,1,0:T(4,128)} %w_ref.5) | copy-start | bytes 442372

commit v7 on v6

--- a/solution.py
+++ b/solution.py
@@ -267,11 +267,10 @@
 
 
 def tail_kernel(
-    modes, length, lanes, scal, tail_ref, w_ref, t_ref, q_ref, z_ref, mask_ref, x_scr, u_scr
+    modes, lanes, tail_ref, w_ref, t_ref, mask_ref, q_ref, z_ref, x_scr, u_scr
 ):
     rows = tail_ref.shape[0] - modes
 
-    write_masks(mask_ref, WIN, scal[0], scal[1], length)
     x_scr[:, : 8 + WIN - rows, :] = jnp.zeros(
         (x_scr.shape[0], 8 + WIN - rows, x_scr.shape[2]), F32
     )
@@ -290,20 +289,20 @@
         z_ref[:, cols] = near[:WIN] + near[WIN:]
 
 
-def near_kernel(lanes, u_ref, t_ref, z_ref):
+def near_kernel(lanes, scal, u_ref, t_ref, z_ref, mask_ref):
     length = u_ref.shape[0]
+    write_masks(mask_ref, WIN, scal[0], scal[1], length)
     for i, cols in spans(u_ref.shape[1] // lanes, lanes):
         near = dot(t_ref[i], u_ref[:, cols])
         z_ref[:, cols] = near[:length] + near[length:]
 
 
 def final_kernel(
-    lanes, scal, q_ref, z_ref, qt_ref, zt_ref, r_ref, rt_ref, st_ref, stt_ref,
-    w_ref, b_ref, out_ref, mask_ref, w_scr, q_scr, z_scr, o_scr, sems,
+    lanes, q_ref, z_ref, qt_ref, zt_ref, r_ref, rt_ref, st_ref, stt_ref,
+    w_ref, b_ref, mask_ref, out_ref, w_scr, q_scr, z_scr, o_scr, sems,
 ):
     length = q_ref.shape[0]
 
-    write_masks(mask_ref, WIN, scal[0], scal[1], length)
     copies = []
     for i, cols in spans(q_ref.shape[1] // lanes, lanes):
         k = i % w_scr.shape[0]
@@ -450,39 +449,41 @@
         name="tables",
     )(scal, li_decay, li_residue, mr_filter.reshape(groups, 1, filter_len))
 
-    z_own = pl.pallas_call(
+    full = WIN + length
+    z_own, masks = pl.pallas_call(
         functools.partial(near_kernel, lanes),
-        in_specs=[whole] * 2,
-        out_specs=whole,
-        out_shape=jax.ShapeDtypeStruct((length, channels), F32),
+        in_specs=[sm] + [whole] * 2,
+        out_specs=[whole] * 2,
+        out_shape=[
+            jax.ShapeDtypeStruct((length, channels), F32),
+            jax.ShapeDtypeStruct((2, full, LANE), F32),
+        ],
         compiler_params=params,
         cost_estimate=pl.CostEstimate(flops=10**8, bytes_accessed=2**16, transcendentals=0),
         name="near",
-    )(u_own, t_own)
+    )(scal, u_own, t_own)
     q_win, z_win = pl.pallas_call(
-        functools.partial(tail_kernel, modes, length, lanes),
-        in_specs=[sm] + [whole] * 3,
+        functools.partial(tail_kernel, modes, lanes),
+        in_specs=[whole] * 4,
         out_specs=[whole] * 2,
         out_shape=[
             jax.ShapeDtypeStruct((WIN, channels), F32),
             jax.ShapeDtypeStruct((WIN, channels), F32),
         ],
         scratch_shapes=[
-            pltpu.VMEM((2, WIN, LANE), F32), pltpu.VMEM((groups, 8 + WIN, lanes), F32),
+            pltpu.VMEM((groups, 8 + WIN, lanes), F32),
             pltpu.VMEM((groups, WIN, lanes), BF),
         ],
         compiler_params=params,
         cost_estimate=pl.CostEstimate(flops=10**8, bytes_accessed=2**16, transcendentals=0),
         name="tail",
-    )(scal, tail, feat_first, t_win)
-    full = WIN + length
+    )(tail, feat_first, t_win, masks)
     return pl.pallas_call(
         functools.partial(final_kernel, lanes),
-        in_specs=[sm] + [whole] * 10,
+        in_specs=[whole] * 11,
         out_specs=pl.BlockSpec(memory_space=pl.ANY),
         out_shape=jax.ShapeDtypeStruct((length, channels), BF),
         scratch_shapes=[
-            pltpu.VMEM((2, full, LANE), F32),
             pltpu.VMEM((count, full, lanes), BF), pltpu.VMEM((count, length, lanes), F32),
             pltpu.VMEM((count, full, lanes), F32), pltpu.VMEM((groups, length, lanes), BF),
             pltpu.SemaphoreType.DMA((groups,)),
@@ -491,8 +492,8 @@
         cost_estimate=pl.CostEstimate(flops=10**8, bytes_accessed=2**16, transcendentals=0),
         name="final",
     )(
-        scal, q_own, z_own, q_win, z_win, r_own, r_win, own_state, win_state,
-        feat_second, b_all,
+        q_own, z_own, q_win, z_win, r_own, r_win, own_state, win_state,
+        feat_second, b_all, masks,
     )
 
 

time: 61.4 us -> 60.1 us (0.979)
  waiting for transfers between devices: 13 us -> 12.3 us
    ppermute x2, waiting for transfers between devices: 6.06 us -> 5.37 us  [behind(): return lax.ppermute(array, 'seq', [(i, i + by) for i in range(size - by)])]
  transfers between devices with their start and end apart: 7 -> 7, of which waited for: 5 -> 5; matrix products, arithmetic and copies ran while one was open for 0% -> 0% of each run, Pallas kernels for 16% -> 17%
where the time goes in v7:
time: 60.1 us; the launch traced here: 59.8 us
  Pallas kernels  24.1 us (40%)
  starting transfers between devices  21.9 us (36%)
  waiting for transfers between devices  12.3 us (20%)
  between operations  1.04 us (2%)
    ppermute x2, starting transfers between devices, behind(): return lax.ppermute(array, 'seq', [(i, i + by) for i in range(size - by)])  8.85 us
    pallas_call x1, Pallas kernels, per_device(): pl.pallas_call(functools.partial(final_kernel, lanes), in_specs=[whole] *...  7.53 us
    ppermute x2, starting transfers between devices, per_device(): lax.ppermute(pair[:modes], 'seq', [(i, i + by) for i in range(0, size - b...  5.78 us
    ppermute x2, waiting for transfers between devices, behind(): return lax.ppermute(array, 'seq', [(i, i + by) for i in range(size - by)])  5.37 us
    pallas_call x1, Pallas kernels, per_device(): pl.pallas_call(functools.partial(states_kernel, cut, modes, lanes), in_sp...  4.28 us
    pallas_call x1, Pallas kernels, per_device(): pl.pallas_call(functools.partial(tables_kernel, cut, modes, length), grid...  4.18 us
    ppermute x2, waiting for transfers between devices, per_device(): lax.ppermute(pair[:modes], 'seq', [(i, i + by) for i in range(0, size - b...  3.92 us
    ppermute x1, starting transfers between devices, per_device(): lax.ppermute(pair, 'seq', [(i, i + 2) for i in range(0, size - 2, 2)])  3.42 us
  transfers between devices with their start and end apart: 7, of which 5 were waited for; matrix products, arithmetic and copies ran while one was open for 0% of the time, Pallas kernels for 17%

profile of v7, /device:TPU:0, one launch (start us, length us, event | category | flops | bytes accessed | tf_op | source)
XLA Modules:
  0.0 59.8 jit_solution(11465305142881532945)
XLA Ops:
  0.7 1.6 %load.1 = (bf16[256,4096]{1,0:T(8,128)(2,1)S(1)}, bf16[3,4096]{1,0:T(4,128)(2,1)S(1)}) custom-call(s32[1]{0:T(128)S(6)} %copy.9.bounds, bf16[256,4096]{1,0:T(8,128)(2,1)} %x_ref.1), custom_call_target="tpu_custom_call" | custom-call | tf_op jit(solution)/shard_map/load/pallas_call | solution.py:358
  2.3 4.8 %collective-permute-start = (bf16[3,4096]{1,0:T(4,128)(2,1)S(1)}, bf16[3,4096]{1,0:T(4,128)(2,1)S(1)}, u32[]{:S(2)}, u32[]{:S(2)}) collective-permute-start(bf16[3,4096]{1,0:T(4,128)(2,1)S(1)} %get-tuple-element.32), channel_id=1, source_target_pairs={{0,2},{2,4},{4,6},{6,8},{8,10},{10,12},{12,14},{1,3},{3,5},{5,7},{... | collective-permute-start | bytes 73736 | tf_op jit(solution)/shard_map/ppermute | solution.py:349
  7.2 1.6 %collective-permute-done.edge_ref = bf16[3,4096]{1,0:T(4,128)(2,1)S(1)} collective-permute-done((bf16[3,4096]{1,0:T(4,128)(2,1)S(1)}, bf16[3,4096]{1,0:T(4,128)(2,1)S(1)}, u32[]{:S(2)}, u32[]{:S(2)}) %collective-permute-start) | collective-permute-done | bytes 24608 | tf_op jit(solution)/shard_map/ppermute | solution.py:349
  8.8 4.3 %states.1 = (bf16[16,4224]{1,0:T(8,128)(2,1)S(1)}, bf16[16,4096]{1,0:T(8,128)(2,1)S(1)}, f32[256,4096]{1,0:T(8,128)S(1)}, bf16[256,4096]{1,0:T(8,128)(2,1)S(1)}, s32[3]{0:T(128)S(1)}) custom-call(s32[1]{0:T(128)S(6)} %copy.9.bounds, bf16[256,4096]{1,0:T(8,128)(2,1)S(1)} %get-tuple-element.41.x_ref, bf16[3,4096]{1,0:T(4,128)(2,1)S(1)} %collective-permute-done.edge_ref, ...), custom_call_target="tpu_custom_call" | custom-call | flops 100000000 | bytes 65536 | tf_op jit(solution)/shard_map/states/pallas_call | solution.py:382
  13.1 2.4 %collective-permute-start.1 = (bf16[16,4224]{1,0:T(8,128)(2,1)S(1)}, bf16[16,4224]{1,0:T(8,128)(2,1)S(1)}, u32[]{:S(2)}, u32[]{:S(2)}) collective-permute-start(bf16[16,4224]{1,0:T(8,128)(2,1)S(1)} %get-tuple-element.39.mine_ref), channel_id=1, source_target_pairs={{0,2},{2,0},{4,6},{6,4},{8,10},{10,8},{12,14},{14,12},{1,3},{3,1},... | collective-permute-start | bytes 405512 | tf_op jit(solution)/shard_map/ppermute | solution.py:400
  15.4 3.0 %collective-permute-done.1.other_ref = bf16[16,4224]{1,0:T(8,128)(2,1)S(1)} collective-permute-done((bf16[16,4224]{1,0:T(8,128)(2,1)S(1)}, bf16[16,4224]{1,0:T(8,128)(2,1)S(1)}, u32[]{:S(2)}, u32[]{:S(2)}) %collective-permute-start.1) | collective-permute-done | bytes 135200 | tf_op jit(solution)/shard_map/ppermute | solution.py:400
  18.4 0.3 slice.7
  18.7 0.0 copy-start.4
  18.8 0.1 pad_maximum_fusion
  18.9 4.0 %collective-permute-start.2 = (bf16[147,4096]{1,0:T(8,128)(2,1)S(1)}, bf16[147,4096]{1,0:T(8,128)(2,1)S(1)}, u32[]{:S(2)}, u32[]{:S(2)}) collective-permute-start(bf16[147,4096]{1,0:T(8,128)(2,1)S(1)} %pad_maximum_fusion), channel_id=1, source_target_pairs={{0,2},{2,4},{4,6},{6,8},{8,10},{10,12},{12,14},{1,3},{3,5},{5,7},{... | collective-permute-start | bytes 3612680 | tf_op jit(solution)/shard_map/ppermute | solution.py:349
  22.9 0.7 %pair.1 = bf16[32,4224]{1,0:T(8,128)(2,1)S(1)} custom-call(s32[3]{0:T(128)S(1)} %get-tuple-element.34.scal, bf16[16,4224]{1,0:T(8,128)(2,1)S(1)} %get-tuple-element.39.mine_ref, bf16[16,4224]{1,0:T(8,128)(2,1)S(1)} %collective-permute-done.1.other_ref, f32[8,16]{1,0:T(8,128)S(1)} %copy-done.2), custom_call_target="tpu_custom_call" | custom-call | tf_op jit(solution)/shard_map/pair/pallas_call | solution.py:405
  23.6 3.4 %collective-permute-start.3 = (bf16[32,4224]{1,0:T(8,128)(2,1)S(1)}, bf16[32,4224]{1,0:T(8,128)(2,1)S(1)}, u32[]{:S(2)}, u32[]{:S(2)}) collective-permute-start(bf16[32,4224]{1,0:T(8,128)(2,1)S(1)} %pair.1), channel_id=1, source_target_pairs={{0,4},{4,8},{8,12},{1,5},{5,9},{9,13},{16,20},{20,24},{24,28},{17,... | collective-permute-start | bytes 811016 | tf_op jit(solution)/shard_map/ppermute | solution.py:413
  27.1 4.5 %collective-permute-start.4 = (bf16[16,4224]{1,0:T(8,128)(2,1)S(1)}, bf16[16,4224]{1,0:T(8,128)(2,1)S(1)}, u32[]{:S(2)}, u32[]{:S(2)}) collective-permute-start(bf16[16,4224]{1,0:T(8,128)(2,1)S(1)} %slice.9), channel_id=1, source_target_pairs={{0,8},{4,12},{1,9},{5,13},{16,24},{20,28},{17,25},{21,29}} | collective-permute-start | bytes 405512 | tf_op jit(solution)/shard_map/ppermute | solution.py:415
  31.6 1.3 %collective-permute-start.5 = (bf16[16,4224]{1,0:T(8,128)(2,1)S(1)}, bf16[16,4224]{1,0:T(8,128)(2,1)S(1)}, u32[]{:S(2)}, u32[]{:S(2)}) collective-permute-start(bf16[16,4224]{1,0:T(8,128)(2,1)S(1)} %slice.9), channel_id=1, source_target_pairs={{0,12},{1,13},{16,28},{17,29}} | collective-permute-start | bytes 405512 | tf_op jit(solution)/shard_map/ppermute | solution.py:415
  32.9 2.5 %collective-permute-done.4.refs_0_ = bf16[16,4224]{1,0:T(8,128)(2,1)S(1)} collective-permute-done((bf16[16,4224]{1,0:T(8,128)(2,1)S(1)}, bf16[16,4224]{1,0:T(8,128)(2,1)S(1)}, u32[]{:S(2)}, u32[]{:S(2)}) %collective-permute-start.4) | collective-permute-done | bytes 135200 | tf_op jit(solution)/shard_map/ppermute | solution.py:415
  35.3 1.4 %collective-permute-done.5.refs_1_ = bf16[16,4224]{1,0:T(8,128)(2,1)S(1)} collective-permute-done((bf16[16,4224]{1,0:T(8,128)(2,1)S(1)}, bf16[16,4224]{1,0:T(8,128)(2,1)S(1)}, u32[]{:S(2)}, u32[]{:S(2)}) %collective-permute-start.5) | collective-permute-done | bytes 135200 | tf_op jit(solution)/shard_map/ppermute | solution.py:415
  36.8 0.3 carry.1
  37.1 1.5 %collective-permute-start.6 = (bf16[16,4096]{1,0:T(8,128)(2,1)S(1)}, bf16[16,4096]{1,0:T(8,128)(2,1)S(1)}, u32[]{:S(2)}, u32[]{:S(2)}) collective-permute-start(bf16[16,4096]{1,0:T(8,128)(2,1)S(1)} %get-tuple-element.51), channel_id=1, source_target_pairs={{0,2},{4,6},{8,10},{12,14},{1,3},{5,7},{9,11},{13,15},{16,18},{20,... | collective-permute-start | bytes 393224 | tf_op jit(solution)/shard_map/ppermute | solution.py:427
  38.6 4.2 %tables.1 = (bf16[8,512,256]{2,1,0:T(8,128)(2,1)S(1)}, bf16[8,288,144]{2,1,0:T(8,128)(2,1)S(1)}, bf16[8,256,48]{2,1,0:T(8,128)(2,1)S(1)}, bf16[8,144,48]{2,1,0:T(8,128)(2,1)S(1)}, bf16[8,256,256]{2,1,0:T(8,128)(2,1)S(1)}) custom-call(s32[3]{0:T(128)S(1)} %get-tuple-element.34.scal, f32[8,16]{1,0:T(8,128)S(1)} %copy-done.2, f32[8,16]{1,0:T(8,128)S(1)} %copy-done.3, ...), custom_call_target="tpu_custom_call" | custom-call | flops 100000000 | bytes 65536 | tf_op jit(solution)/shard_map/tables/pallas_call | solution.py:441
  42.8 1.9 %near.1 = (f32[256,4096]{1,0:T(8,128)S(1)}, f32[2,400,128]{2,1,0:T(8,128)S(1)}) custom-call(s32[3]{0:T(128)S(1)} %get-tuple-element.34.scal, bf16[256,4096]{1,0:T(8,128)(2,1)S(1)} %get-tuple-element.35.u_ref, bf16[8,512,256]{2,1,0:T(8,128)(2,1)S(1)} %get-tuple-element.36.t_ref), custom_call_target="tpu_custom_call" | custom-call | flops 100000000 | bytes 65536 | tf_op jit(solution)/shard_map/near/pallas_call | solution.py:453
  44.7 3.8 %collective-permute-done.2.tail_ref.part_ref = bf16[147,4096]{1,0:T(8,128)(2,1)S(1)} collective-permute-done((bf16[147,4096]{1,0:T(8,128)(2,1)S(1)}, bf16[147,4096]{1,0:T(8,128)(2,1)S(1)}, u32[]{:S(2)}, u32[]{:S(2)}) %collective-permute-start.2) | collective-permute-done | bytes 1204256 | tf_op jit(solution)/shard_map/ppermute | solution.py:349
  48.5 2.8 %tail.1 = (f32[144,4096]{1,0:T(8,128)S(1)}, f32[144,4096]{1,0:T(8,128)S(1)}) custom-call(bf16[147,4096]{1,0:T(8,128)(2,1)S(1)} %collective-permute-done.2.tail_ref.part_ref, f32[3,3,4096]{2,1,0:T(4,128)S(1)} %copy-done, bf16[8,288,144]{2,1,0:T(8,128)(2,1)S(1)} %get-tuple-element.44.t_ref, f32[2,400,128]{2,1,0:T(8,128)S(1)} %get-tuple-element.45.mask_ref), custom_call_target="tpu_custom_call" | custom-call | flops 100000000 | bytes 65536 | tf_op jit(solution)/shard_map/tail/pallas_call | solution.py:465
  51.3 0.8 %place.1 = (bf16[48,4096]{1,0:T(8,128)(2,1)S(1)}, bf16[48,4096]{1,0:T(8,128)(2,1)S(1)}) custom-call(s32[3]{0:T(128)S(1)} %get-tuple-element.34.scal, bf16[16,4224]{1,0:T(8,128)(2,1)S(1)} %collective-permute-done.1.other_ref, bf16[147,4096]{1,0:T(8,128)(2,1)S(1)} %collective-permute-done.2.tail_ref.part_ref, ...), custom_call_target="tpu_custom_call" | custom-call | tf_op jit(solution)/shard_map/place/pallas_call | solution.py:428
  52.1 7.5 %final.1 = bf16[256,4096]{1,0:T(8,128)(2,1)} custom-call(f32[256,4096]{1,0:T(8,128)S(1)} %get-tuple-element.33.q_ref, f32[256,4096]{1,0:T(8,128)S(1)} %get-tuple-element.37.z_ref, f32[144,4096]{1,0:T(8,128)S(1)} %get-tuple-element.46.qt_ref, f32[144,4096]{1,0:T(8,128)S(1)} %get-tuple-element.47.zt_ref, bf16[8,256,48]{2,1,0:T(8,128)(2,1)S(1)} %get-tuple-element.48.r_ref, ...), custom_call_target="tpu_custom_call" | custom-call | flops 100000000 | bytes 65536 | tf_op jit(solution)/shard_map/final/pallas_call | solution.py:481
  (13 shorter events, 0.0 us)
Async XLA Ops:
  0.0 8.8 %copy-start = (f32[3,3,4096]{2,1,0:T(4,128)S(1)}, f32[3,3,4096]{2,1,0:T(4,128)}, u32[]{:S(2)}) copy-start(f32[3,3,4096]{2,1,0:T(4,128)} %w_ref.4) | copy-start | bytes 442372
  0.0 8.8 %copy-start.2 = (f32[8,16]{1,0:T(8,128)S(1)}, f32[8,16]{1,0:T(8,128)}, u32[]{:S(2)}) copy-start(f32[8,16]{1,0:T(8,128)} %dec_ref.9) | copy-start | bytes 1540
  2.3 6.4 %collective-permute-start = (bf16[3,4096]{1,0:T(4,128)(2,1)S(1)}, bf16[3,4096]{1,0:T(4,128)(2,1)S(1)}, u32[]{:S(2)}, u32[]{:S(2)}) collective-permute-start(bf16[3,4096]{1,0:T(4,128)(2,1)S(1)} %get-tuple-element.32), channel_id=1, source_target_pairs={{0,2},{2,4},{4,6},{6,8},{8,10},{10,12},{12,14},{1,3},{3,5},{5,7},{... | collective-permute-start | bytes 73736 | tf_op jit(solution)/shard_map/ppermute | solution.py:349
  13.1 5.4 %collective-permute-start.1 = (bf16[16,4224]{1,0:T(8,128)(2,1)S(1)}, bf16[16,4224]{1,0:T(8,128)(2,1)S(1)}, u32[]{:S(2)}, u32[]{:S(2)}) collective-permute-start(bf16[16,4224]{1,0:T(8,128)(2,1)S(1)} %get-tuple-element.39.mine_ref), channel_id=1, source_target_pairs={{0,2},{2,0},{4,6},{6,4},{8,10},{10,8},{12,14},{14,12},{1,3},{3,1},... | collective-permute-start | bytes 405512 | tf_op jit(solution)/shard_map/ppermute | solution.py:400
  18.7 19.8 %copy-start.4 = (bf16[8,128]{1,0:T(8,128)(2,1)S(1)}, bf16[8,128]{1,0:T(8,128)(2,1)}, u32[]{:S(2)}) copy-start(bf16[8,128]{1,0:T(8,128)(2,1)} %param.13) | copy-start | bytes 6148
  18.7 19.8 %copy-start.3 = (f32[8,16]{1,0:T(8,128)S(1)}, f32[8,16]{1,0:T(8,128)}, u32[]{:S(2)}) copy-start(f32[8,16]{1,0:T(8,128)} %res_ref.1) | copy-start | bytes 1540
  18.9 29.6 %collective-permute-start.2 = (bf16[147,4096]{1,0:T(8,128)(2,1)S(1)}, bf16[147,4096]{1,0:T(8,128)(2,1)S(1)}, u32[]{:S(2)}, u32[]{:S(2)}) collective-permute-start(bf16[147,4096]{1,0:T(8,128)(2,1)S(1)} %pad_maximum_fusion), channel_id=1, source_target_pairs={{0,2},{2,4},{4,6},{6,8},{8,10},{10,12},{12,14},{1,3},{3,5},{5,7},{... | collective-permute-start | bytes 3612680 | tf_op jit(solution)/shard_map/ppermute | solution.py:349
  23.6 13.2 %collective-permute-start.3 = (bf16[32,4224]{1,0:T(8,128)(2,1)S(1)}, bf16[32,4224]{1,0:T(8,128)(2,1)S(1)}, u32[]{:S(2)}, u32[]{:S(2)}) collective-permute-start(bf16[32,4224]{1,0:T(8,128)(2,1)S(1)} %pair.1), channel_id=1, source_target_pairs={{0,4},{4,8},{8,12},{1,5},{5,9},{9,13},{16,20},{20,24},{24,28},{17,... | collective-permute-start | bytes 811016 | tf_op jit(solution)/shard_map/ppermute | solution.py:413
  27.1 8.3 %collective-permute-start.4 = (bf16[16,4224]{1,0:T(8,128)(2,1)S(1)}, bf16[16,4224]{1,0:T(8,128)(2,1)S(1)}, u32[]{:S(2)}, u32[]{:S(2)}) collective-permute-start(bf16[16,4224]{1,0:T(8,128)(2,1)S(1)} %slice.9), channel_id=1, source_target_pairs={{0,8},{4,12},{1,9},{5,13},{16,24},{20,28},{17,25},{21,29}} | collective-permute-start | bytes 405512 | tf_op jit(solution)/shard_map/ppermute | solution.py:415
  31.6 5.2 %collective-permute-start.5 = (bf16[16,4224]{1,0:T(8,128)(2,1)S(1)}, bf16[16,4224]{1,0:T(8,128)(2,1)S(1)}, u32[]{:S(2)}, u32[]{:S(2)}) collective-permute-start(bf16[16,4224]{1,0:T(8,128)(2,1)S(1)} %slice.9), channel_id=1, source_target_pairs={{0,12},{1,13},{16,28},{17,29}} | collective-permute-start | bytes 405512 | tf_op jit(solution)/shard_map/ppermute | solution.py:415
  37.1 14.2 %collective-permute-start.6 = (bf16[16,4096]{1,0:T(8,128)(2,1)S(1)}, bf16[16,4096]{1,0:T(8,128)(2,1)S(1)}, u32[]{:S(2)}, u32[]{:S(2)}) collective-permute-start(bf16[16,4096]{1,0:T(8,128)(2,1)S(1)} %get-tuple-element.51), channel_id=1, source_target_pairs={{0,2},{4,6},{8,10},{12,14},{1,3},{5,7},{9,11},{13,15},{16,18},{20,... | collective-permute-start | bytes 393224 | tf_op jit(solution)/shard_map/ppermute | solution.py:427
  48.5 3.6 %copy-start.1 = (f32[3,3,4096]{2,1,0:T(4,128)S(1)}, f32[3,3,4096]{2,1,0:T(4,128)}, u32[]{:S(2)}) copy-start(f32[3,3,4096]{2,1,0:T(4,128)} %w_ref.5) | copy-start | bytes 442372
